TPU v7x, 32 devices: a whole 2x2x4 slice. The times are simulated.
32 devices in a mesh: grp: 2 (over y), tm: 4 (over z), mod: 4 (over x, core).
Axes of the slice: x: 2, y: 2, z: 4, core: 2. Of those that a mesh axis runs over, the one named last changes fastest.
Arguments:
- phase: float32 [16, 512, 128], P(('grp', 'tm'), 'mod'), parts along dimension 0, may hold values from -4 to 4
- direction: float32 [16, 512, 128], P(('grp', 'tm'), 'mod'), parts along dimension 0, may hold values from -16 to 16
- pupil_mask: int32 [512, 128], replicated, may hold values 0 or 1
- mod_tilts: int32 [4], P('mod'), may hold values from -8 to 8
- wind_codes: int32 [1024, 128], P('grp'), parts along dimension 0, may hold values from 0 to 15
- noise_weight: float32 [16, 1024, 128], P(('grp', 'tm')), parts along dimension 0, may hold values from 0.075 to 0.75
Outputs:
- hess_vec: float32 [16, 512, 128], P(('grp', 'tm'), 'mod'), parts along dimension 0
- curvature: float32 [2], P('grp'), parts along dimension 0
There are 2 independent parts, one for each index of `grp`. A program takes and returns all parts, laid end to end along the dimension named above; an argument that names none is the same for every part. Nothing has to cross between parts.
All inputs are finite; a program needn't handle non-finite values.
Results may differ from a plain program's by a relative error of at most 0.0003.
Values sent between devices are 32-bit elements; how exact they have to be, the bound alone decides.
No kernel may reach another device: no remote copies, remote signals or barrier semaphores. Data moves between devices by JAX's collectives and lax.ppermute only.
A program may use at most 64 MiB of HBM per device.

v0:
```python
import jax
import jax.numpy as jnp
from jax import lax
from jax.sharding import PartitionSpec as P

HIGHEST = lax.Precision.HIGHEST


def with_halo(cells, sides, width):
    for axis, dim in sides:
        count = lax.axis_size(axis)
        ends = count - 1
        head = lax.slice_in_dim(cells, 0, width, axis=dim)
        tail = lax.slice_in_dim(cells, cells.shape[dim] - width, cells.shape[dim], axis=dim)
        cells = jnp.concatenate(
            [
                lax.ppermute(tail, axis, [(i, (i + 1) % count) for i in range(ends)]),
                cells,
                lax.ppermute(head, axis, [((i + 1) % count, i) for i in range(ends)]),
            ],
            axis=dim,
        )
    return cells


def square_table(count, orient):
    index_range = jnp.arange(count, dtype=jnp.int32)
    turn_counts = index_range[:, None] * index_range[None, :] % count
    angles = orient * 2.0 * jnp.pi / count * turn_counts.astype(jnp.float32)
    return (jnp.cos(angles), jnp.sin(angles))


def complex_mix(form, table_real, table_imag, field_real, field_imag):
    real_real = jnp.einsum(form, table_real, field_real, precision=HIGHEST)
    imag_imag = jnp.einsum(form, table_imag, field_imag, precision=HIGHEST)
    real_imag = jnp.einsum(form, table_real, field_imag, precision=HIGHEST)
    imag_real = jnp.einsum(form, table_imag, field_real, precision=HIGHEST)
    return (real_real - imag_imag, real_imag + imag_real)


def transform(field_real, field_imag, orient):
    batch_size, length, row_count = field_real.shape
    outer_size = 32
    inner_size = length // outer_size
    first_real, first_imag = square_table(outer_size, orient)
    second_real, second_imag = square_table(inner_size, orient)
    turn_counts = (
        jnp.arange(outer_size, dtype=jnp.int32)[:, None]
        * jnp.arange(inner_size, dtype=jnp.int32)[None, :]
        % length
    )
    angles = orient * 2.0 * jnp.pi / length * turn_counts.astype(jnp.float32)
    twist_real = jnp.cos(angles)[None, :, :, None]
    twist_imag = jnp.sin(angles)[None, :, :, None]
    shaped_real = field_real.reshape(batch_size, outer_size, inner_size, row_count)
    shaped_imag = field_imag.reshape(batch_size, outer_size, inner_size, row_count)
    section_real, section_imag = complex_mix(
        "kn,bnmr->bkmr", first_real, first_imag, shaped_real, shaped_imag
    )
    turned_real = section_real * twist_real - section_imag * twist_imag
    turned_imag = section_real * twist_imag + section_imag * twist_real
    final_real, final_imag = complex_mix(
        "dm,bkmr->bdkr", second_real, second_imag, turned_real, turned_imag
    )
    return (
        final_real.reshape(batch_size, length, row_count),
        final_imag.reshape(batch_size, length, row_count),
    )


def roof_mask(length, shift_bins):
    freq_index = jnp.arange(length, dtype=jnp.int32)
    signed_freq = jnp.where(freq_index < length // 2, freq_index, freq_index - length)
    turn_counts = shift_bins * jnp.abs(signed_freq) % length
    angles = -2.0 * jnp.pi / length * turn_counts.astype(jnp.float32)
    return (jnp.cos(angles), jnp.sin(angles))


def pyramid(field_real, field_imag, gain_real, gain_imag):
    spectrum_real, spectrum_imag = transform(field_real, field_imag, -1.0)
    column_real = gain_real[None, :, None]
    column_imag = gain_imag[None, :, None]
    masked_real = spectrum_real * column_real - spectrum_imag * column_imag
    masked_imag = spectrum_real * column_imag + spectrum_imag * column_real
    back_real, back_imag = transform(masked_real, masked_imag, 1.0)
    inverse_length = 1.0 / field_real.shape[1]
    return (back_real * inverse_length, back_imag * inverse_length)


def row_ahead(field):
    return jnp.pad(field[:, :, 1:], ((0, 0), (0, 0), (0, 1)))


def row_behind(field):
    return jnp.pad(field[:, :, :-1], ((0, 0), (0, 0), (1, 0)))


def flow_terms(extended, frac_x, frac_r, first_frame, total_frames, first_pixel):
    frames_ext, width_ext, row_count = extended.shape
    frames_dev = frames_ext - 2
    near_x = jnp.pad(frac_x, ((1, 0), (0, 0)))
    near_r = jnp.pad(frac_r, ((1, 0), (0, 0)))
    stay_stay = (1.0 - near_x) * (1.0 - near_r)
    ahead_stay = near_x * (1.0 - near_r)
    stay_ahead = (1.0 - near_x) * near_r
    ahead_ahead = near_x * near_r
    base_cells = extended[:, :-1, :]
    ahead_cells = extended[:, 1:, :]
    moved = (
        stay_stay * base_cells
        + ahead_stay * ahead_cells
        + stay_ahead * row_ahead(base_cells)
        + ahead_ahead * row_ahead(ahead_cells)
    )
    flow = extended[1:, :-1, :] - moved[:-1]
    frame_ids = first_frame - 1 + lax.broadcasted_iota(jnp.int32, flow.shape, 0)
    pixel_ids = first_pixel - 1 + lax.broadcasted_iota(jnp.int32, flow.shape, 1)
    valid = (frame_ids >= 0) & (frame_ids <= total_frames - 2) & (pixel_ids >= 0)
    flow = jnp.where(valid, flow, 0.0)
    spread = (
        (stay_stay * flow)[:, 1:]
        + (ahead_stay * flow)[:, :-1]
        + row_behind((stay_ahead * flow)[:, 1:] + (ahead_ahead * flow)[:, :-1])
    )
    prior = flow[:frames_dev, 1:] - spread[1:]
    return (prior, flow[1:, 1:])


def forward_pass(full_phase, full_direction, tilts, amplitude, gain_real, gain_imag):
    frames_dev, pupil_width, row_count = full_phase.shape
    line_length = 2 * pupil_width
    quarter = pupil_width // 2
    local_points = tilts.shape[0]
    positions = quarter + jnp.arange(pupil_width, dtype=jnp.int32)
    tilt_turns = tilts[:, None] * positions[None, :] % line_length
    tilt_angles = 2.0 * jnp.pi / line_length * tilt_turns.astype(jnp.float32)
    angles = full_phase[None] + tilt_angles[:, None, :, None]
    field_real = amplitude * jnp.cos(angles)
    field_imag = amplitude * jnp.sin(angles)
    margins = ((0, 0), (quarter, quarter), (0, 0))
    line_batch = local_points * frames_dev

    def padded_lines(field):
        return jnp.pad(field.reshape(line_batch, pupil_width, row_count), margins)

    image_real, image_imag = pyramid(
        padded_lines(field_real), padded_lines(field_imag), gain_real, gain_imag
    )
    push_real, push_imag = pyramid(
        padded_lines(-field_imag * full_direction),
        padded_lines(field_real * full_direction),
        gain_real,
        gain_imag,
    )
    signal_terms = (2.0 * (image_real * push_real + image_imag * push_imag)).reshape(
        local_points, frames_dev, line_length, row_count
    )
    return (field_real, field_imag, image_real, image_imag, jnp.sum(signal_terms, axis=0))


def backward_pass(
    field_real, field_imag, image_real, image_imag, weighted_full, gain_real, gain_imag
):
    local_points, frames_dev, pupil_width, row_count = field_real.shape
    line_length = 2 * pupil_width
    quarter = pupil_width // 2
    line_batch = local_points * frames_dev
    image_shaped_real = image_real.reshape(local_points, frames_dev, line_length, row_count)
    image_shaped_imag = image_imag.reshape(local_points, frames_dev, line_length, row_count)
    source_real = (weighted_full[None] * image_shaped_real).reshape(
        line_batch, line_length, row_count
    )
    source_imag = (weighted_full[None] * image_shaped_imag).reshape(
        line_batch, line_length, row_count
    )
    back_real, back_imag = pyramid(source_real, source_imag, gain_real, -gain_imag)
    back_real = back_real[:, quarter : quarter + pupil_width].reshape(
        local_points, frames_dev, pupil_width, row_count
    )
    back_imag = back_imag[:, quarter : quarter + pupil_width].reshape(
        local_points, frames_dev, pupil_width, row_count
    )
    return -2.0 * jnp.sum(field_imag * back_real - field_real * back_imag, axis=0)


def per_device(phase, direction, pupil_mask, mod_tilts, wind_codes, noise_weight):
    frames_dev, shard_width, row_count = phase.shape
    mod_count = lax.axis_size("mod")
    pupil_width = shard_width * mod_count
    line_length = 2 * pupil_width
    quarter = pupil_width // 2
    mod_index = lax.axis_index("mod")
    first_frame = lax.axis_index("tm") * frames_dev
    total_frames = frames_dev * lax.axis_size("tm")
    first_pixel = mod_index * shard_width
    frac_x = ((wind_codes % 4).astype(jnp.float32) + 0.5) / 4.0
    frac_r = ((wind_codes // 4).astype(jnp.float32) + 0.5) / 4.0
    gain_real, gain_imag = roof_mask(line_length, quarter)
    rimmed = with_halo(direction, (("tm", 0),), 1)
    full_phase, full_rim = (
        lax.all_gather(phase, "mod", axis=1, tiled=True),
        lax.all_gather(rimmed, "mod", axis=1, tiled=True),
    )
    full_direction = full_rim[1:-1]
    extended = jnp.pad(full_rim, ((0, 0), (1, 1), (0, 0)))
    prior_lines, flow_lines = flow_terms(extended, frac_x, frac_r, first_frame, total_frames, 0)
    prior = lax.dynamic_slice_in_dim(prior_lines, first_pixel, shard_width, 1)
    amplitude = pupil_mask.astype(jnp.float32)
    field_real, field_imag, image_real, image_imag, signal_local = forward_pass(
        full_phase, full_direction, mod_tilts, amplitude, gain_real, gain_imag
    )
    signal_full = lax.psum(signal_local, "mod")
    weighted_used = noise_weight * signal_full
    grad_lines = backward_pass(
        field_real, field_imag, image_real, image_imag, weighted_used, gain_real, gain_imag
    )
    grad_own = lax.psum_scatter(grad_lines, "mod", scatter_dimension=1, tiled=True)
    hess_vec = grad_own + prior
    curvature_total = lax.psum(jnp.sum(direction * hess_vec), ("tm", "mod"))
    entry_count = float(total_frames * pupil_width * row_count)
    curvature = (curvature_total / entry_count).reshape(1)
    return (hess_vec, curvature)


def solution(mesh):
    return jax.shard_map(
        per_device,
        mesh=mesh,
        in_specs=(
            P(("grp", "tm"), "mod", None),
            P(("grp", "tm"), "mod", None),
            P(),
            P("mod"),
            P("grp", None),
            P(("grp", "tm"), None, None),
        ),
        out_specs=(P(("grp", "tm"), "mod", None), P("grp")),
        check_vma=False,
    )
```

profile of v0, /device:TPU:0, one launch (start us, length us, event | category | flops | bytes accessed | tf_op | source)
XLA Modules:
  0.0 234.9 jit_solution(14579527725214481166)
XLA Ops:
  8.1 4.9 %collective-permute-start = (f32[1,128,128]{2,1,0:T(8,128)S(1)}, f32[1,128,128]{2,1,0:T(8,128)S(1)}, u32[]{:S(2)}, u32[]{:S(2)}) collective-permute-start(f32[1,128,128]{2,1,0:T(8,128)S(1)} %get-tuple-element.39), channel_id=1, source_target_pairs={{0,4},{4,8},{8,12},{1,5},{5,9},{9,13},{2,6},{6,10},{10,14},{3,7},{... | collective-permute-start | bytes 196616 | tf_op jit(solution)/shard_map/ppermute | solution.py:17
  13.1 1.3 collective-permute-start.1
  16.0 3.2 %collective-permute-done.1 = f32[1,128,128]{2,1,0:T(8,128)S(1)} collective-permute-done((f32[1,128,128]{2,1,0:T(8,128)S(1)}, f32[1,128,128]{2,1,0:T(8,128)S(1)}, u32[]{:S(2)}, u32[]{:S(2)}) %collective-permute-start.1) | collective-permute-done | bytes 65568 | tf_op jit(solution)/shard_map/ppermute | solution.py:19
  19.2 1.6 pad_maximum_fusion
  26.2 9.4 %all_gather.6 = f32[2,512,128]{2,1,0:T(8,128)S(1)} all-gather(f32[2,128,128]{2,1,0:T(8,128)S(1)} %copy-done.19), channel_id=1, replica_groups=mesh['grp'=2,'tm'=4,'mod'=4] {'mod'}, dimensions={1}, use_global_device_ids=true | all-gather | bytes 655360 | tf_op jit(solution)/shard_map/all_gather | solution.py:201
  35.6 4.0 %all-gather.2.cloned.1.call-done = f32[4,512,128]{2,1,0:T(8,128)} async-done(((f32[4,128,128]{2,1,0:T(8,128)}), f32[4,512,128]{2,1,0:T(8,128)}) %all-gather.2.cloned.1.call-update) | async-done | bytes 1048592 | tf_op jit(solution)/shard_map/all_gather | solution.py:202
  39.6 4.1 %negate_multiply_fusion = (f32[2,512,128]{2,1,0:T(8,128)S(1)}, f32[2,512,128]{2,1,0:T(8,128)S(1)}, f32[2,512,128]{2,1,0:T(8,128)S(1)}, f32[2,512,128]{2,1,0:T(8,128)S(1)}) fusion(f32[4,512,128]{2,1,0:T(8,128)} %all-gather.2.cloned.1.call-done, f32[2,512,128]{2,1,0:T(8,128)S(1)} %all_gather.6, f32[512]{0:T(512)S(1)} %fusion.179, ...), kind=kLoop, calls=%fused_computation.154 | loop fusion | flops 786432 | bytes 3409920 | tf_op jit(solution)/shard_map/mul | solution.py:150
  43.8 1.7 fusion.80
  45.6 1.7 fusion.84
  47.3 1.8 fusion.28
  49.1 1.8 fusion.29
  50.9 1.7 fusion.66
  52.7 1.7 fusion.62
  54.4 2.0 fusion.21
  56.4 2.2 multiply_subtract_fusion.5
  58.7 1.7 fusion.78
  60.4 1.7 fusion.74
  62.1 1.7 fusion.27
  63.8 1.8 fusion.26
  65.6 1.3 fusion.94
  66.9 1.3 fusion.95
  68.2 1.9 fusion.60
  70.1 1.7 fusion.56
  71.8 1.7 fusion.19
  73.5 1.7 fusion.18
  75.3 1.3 fusion.97
  76.6 1.3 fusion.96
  77.9 1.3 fusion.25
  79.2 1.3 fusion.24
  80.5 1.7 fusion.17
  82.2 1.8 multiply_subtract_fusion.3
  84.0 1.7 fusion.54
  85.7 1.7 fusion.50
  87.4 1.8 fusion.15
  89.8 1.7 fusion.68
  91.5 1.7 fusion.72
  93.2 1.9 fusion.13
  95.8 1.8 fusion.11
  98.2 1.8 fusion.23
  100.5 1.3 fusion.31
  102.2 1.5 constant_dynamic-slice_fusion
  103.8 1.5 pad_slice_fusion.3
  105.2 2.0 pad_slice_fusion.1
  107.2 30.2 %all-reduce.12.cloned.1.call-done = f32[2,1024,128]{2,1,0:T(8,128)} async-done(((f32[2,1024,128]{2,1,0:T(8,128)}), f32[2,1024,128]{2,1,0:T(8,128)}) %all-reduce.12.cloned.1.call-update) | async-done | bytes 1048592 | tf_op jit(solution)/shard_map/psum | solution.py:212
  137.4 1.8 bitcast_multiply_fusion.3
  139.2 1.7 fusion.48
  140.9 1.7 fusion.44
  142.7 1.8 fusion.9
  144.5 2.1 multiply_subtract_fusion.2
  146.5 1.7 fusion.42
  148.2 1.7 fusion.38
  150.0 2.1 fusion.7
  152.1 1.8 fusion.6
  153.8 1.3 fusion.99
  156.4 1.3 fusion.5
  157.7 1.5 multiply_subtract_fusion
  159.3 1.7 fusion.36
  161.0 1.9 fusion.32
  162.9 1.7 fusion.3
  165.2 1.7 fusion.1
  169.9 2.1 fusion.87
  173.2 18.0 %reduce-scatter.2.cloned.1.call-done = f32[2,128,128]{2,1,0:T(8,128)} async-done(((f32[2,512,128]{2,1,0:T(8,128)}), f32[2,128,128]{2,1,0:T(8,128)}) %reduce-scatter.2.cloned.1.call-update) | async-done | bytes 131088 | tf_op jit(solution)/shard_map/reduce_scatter | solution.py:217
  191.3 2.3 multiply_reduce_fusion
  193.6 32.8 %psum.15 = f32[]{:T(128)} all-reduce(f32[]{:T(128)} %get-tuple-element.2), channel_id=1, replica_groups=mesh['grp'=2,'tm'=4,'mod'=4] {'tm','mod'}, use_global_device_ids=true, to_apply=%region_3.4 | all-reduce | flops 1 | bytes 8 | tf_op jit(solution)/shard_map/psum | solution.py:219
  (87 shorter events, 16.3 us)
Async XLA Ops:
  7.2 15.0 %copy-start.13 = (s32[512,128]{1,0:T(8,128)S(1)}, s32[512,128]{1,0:T(8,128)}, u32[]{:S(2)}) copy-start(s32[512,128]{1,0:T(8,128)} %param.10) | copy-start | bytes 786436
  7.2 32.4 %all-gather.2.cloned.1.call-start = ((), (), s32[]{:S(2)}) async-start(), calls=%async_computation.1 | async-start | bytes 1310720 | tf_op jit(solution)/shard_map/all_gather | solution.py:202
  8.1 7.9 %collective-permute-start = (f32[1,128,128]{2,1,0:T(8,128)S(1)}, f32[1,128,128]{2,1,0:T(8,128)S(1)}, u32[]{:S(2)}, u32[]{:S(2)}) collective-permute-start(f32[1,128,128]{2,1,0:T(8,128)S(1)} %get-tuple-element.39), channel_id=1, source_target_pairs={{0,4},{4,8},{8,12},{1,5},{5,9},{9,13},{2,6},{6,10},{10,14},{3,7},{... | collective-permute-start | bytes 196616 | tf_op jit(solution)/shard_map/ppermute | solution.py:17
  13.1 6.2 %collective-permute-start.1 = (f32[1,128,128]{2,1,0:T(8,128)S(1)}, f32[1,128,128]{2,1,0:T(8,128)S(1)}, u32[]{:S(2)}, u32[]{:S(2)}) collective-permute-start(f32[1,128,128]{2,1,0:T(8,128)S(1)} %get-tuple-element.40), channel_id=1, source_target_pairs={{4,0},{8,4},{12,8},{5,1},{9,5},{13,9},{6,2},{10,6},{14,10},{7,3},{... | collective-permute-start | bytes 196616 | tf_op jit(solution)/shard_map/ppermute | solution.py:19
  20.9 116.5 %all-reduce.12.cloned.1.call-start = ((), (), s32[]{:S(2)}) async-start(), calls=%async_computation.2 | async-start | bytes 2097152 | tf_op jit(solution)/shard_map/psum | solution.py:212
  21.1 35.3 %copy-start.15 = (f32[32,32]{0,1:T(8,128)}, f32[32,32]{0,1:T(8,128)S(1)}, u32[]{:S(2)}) copy-start(f32[32,32]{0,1:T(8,128)S(1)} %copy.45) | copy-start | bytes 12292
  21.3 35.2 %copy-start.17 = (f32[32,32]{0,1:T(8,128)}, f32[32,32]{0,1:T(8,128)S(1)}, u32[]{:S(2)}) copy-start(f32[32,32]{0,1:T(8,128)S(1)} %copy.48) | copy-start | bytes 12292
  22.5 0.7 copy-start.7
  22.5 1.5 copy-start.8
  22.5 13.1 %copy-start.9 = (f32[513,128]{1,0:T(8,128)}, f32[513,128]{1,0:T(8,128)S(1)}, u32[]{:S(2)}) copy-start(f32[513,128]{1,0:T(8,128)S(1)} %get-tuple-element.36) | copy-start | bytes 787972
  22.5 3.7 %copy-start.19 = (f32[2,128,128]{2,1,0:T(8,128)S(1)}, f32[2,128,128]{2,1,0:T(8,128)}, u32[]{:S(2)}) copy-start(f32[2,128,128]{2,1,0:T(8,128)} %param.6) | copy-start | bytes 393220
  43.7 1.8 copy-start.1
  43.7 1.8 copy-start.3
  101.9 1.9 copy-start
  101.9 89.4 %reduce-scatter.2.cloned.1.call-start = ((), (), s32[]{:S(2)}) async-start(), calls=%async_computation.3 | async-start | bytes 655360 | tf_op jit(solution)/shard_map/reduce_scatter | solution.py:217
  142.6 1.8 copy-start.16
  142.6 1.8 copy-start.18
  167.0 1.0 copy-start.2
  167.0 1.2 copy-start.4
  168.2 1.4 copy-start.5
  168.2 1.7 copy-start.6
  172.1 1.0 copy-start.11
  172.1 1.0 copy-start.12
  173.1 18.1 %copy-start.10 = (f32[2,128,128]{2,1,0:T(8,128)S(1)}, f32[2,128,128]{2,1,0:T(8,128)}, u32[]{:S(2)}) copy-start(f32[2,128,128]{2,1,0:T(8,128)} %param.7) | copy-start | bytes 393220
  173.1 18.1 %copy-start.14 = (f32[128,128]{1,0:T(8,128)S(1)}, f32[128,128]{1,0:T(8,128)}, u32[]{:S(2)}) copy-start(f32[128,128]{1,0:T(8,128)} %get-tuple-element.46) | copy-start | bytes 196612
Sparse Core Ops, SparseCore 0:
  21.0 18.5 all-gather.1
  102.0 35.3 all-reduce.11
  169.2 22.0 reduce-scatter.1
where the time goes:
time: 238 us; the launch traced here: 235 us
  matrix products  80.7 us (34%)
  waiting for transfers between devices  55.5 us (23%)
  blocking collectives  42.3 us (18%)
  between operations  17.1 us (7%)
  local copies, waits for them, and re-layouts  16.5 us (7%)
  other arithmetic  16.2 us (7%)
  starting transfers between devices  6.63 us (3%)
    psum x1, blocking collectives, per_device(): curvature_total = lax.psum(jnp.sum(direction * hess_vec), ('tm', 'mod'))  32.8 us
    psum x1, waiting for transfers between devices, per_device(): signal_full = lax.psum(signal_local, 'mod')  30.2 us
    dot_general x12, matrix products, complex_mix(): imag_real = jnp.einsum(form, table_imag, field_real, precision=HIGHEST)  21.3 us
    dot_general x12, matrix products, complex_mix(): imag_imag = jnp.einsum(form, table_imag, field_imag, precision=HIGHEST)  20.6 us
    dot_general x12, matrix products, complex_mix(): real_real = jnp.einsum(form, table_real, field_real, precision=HIGHEST)  19.4 us
    dot_general x12, matrix products, complex_mix(): real_imag = jnp.einsum(form, table_real, field_imag, precision=HIGHEST)  19.4 us
    reduce_scatter x1, waiting for transfers between devices, per_device(): lax.psum_scatter(grad_lines, 'mod', scatter_dimension=1, tiled=True)  18 us
    all_gather x1, blocking collectives, per_device(): lax.all_gather(phase, 'mod', axis=1, tiled=True)  9.44 us
  transfers between devices with their start and end apart: 5, of which 4 were waited for; matrix products, arithmetic and copies ran while one was open for 5% of the time, Pallas kernels for 0%

commit v1 on v0

v1 whole, which is shorter than its diff:
```python
import functools

import jax
import jax.numpy as jnp
import ml_dtypes
import numpy as np
from jax import lax
from jax.experimental import pallas as pl
from jax.experimental.pallas import tpu as pltpu
from jax.sharding import PartitionSpec as P

LANES = 128
SUB = 8
CHUNK = 32
VMEM = pl.BlockSpec(memory_space=pltpu.VMEM)
SMEM = pl.BlockSpec(memory_space=pltpu.SMEM)


def params():
    return pltpu.CompilerParams(vmem_limit_bytes=48 * 1024 * 1024)


class Plan:
    def __init__(self, frames, shard, rows, points, mods):
        self.frames, self.shard, self.rows, self.mods = frames, shard, rows, mods
        self.points = points
        self.pupil = shard * mods
        self.length = 2 * self.pupil
        assert rows == LANES and mods % frames == 0
        self.groups = mods // frames
        self.width = rows // self.groups
        assert 2 * self.width <= LANES
        self.copies = LANES // self.width
        self.total_points = points * mods
        assert self.total_points % self.copies == 0
        self.tiles = self.total_points // self.copies
        self.half = shard // 2
        self.cells = self.pupil // 2
        self.extra = -(-(points + 2 * frames) // SUB) * SUB


def roof_tables(plan):
    cells, length = plan.cells, plan.length
    index = np.arange(cells)
    turned = (index + cells // 2) % cells

    def kernel(gap):
        return 2.0 / length / np.cos(2.0 * np.pi * gap / length)

    even = kernel(2 * turned[:, None] - (2 * index[None, :] + 1))
    odd = kernel(2 * turned[:, None] + 1 - 2 * index[None, :])

    def split(table):
        high = table.astype(ml_dtypes.bfloat16)
        low = (table - high.astype(np.float64)).astype(ml_dtypes.bfloat16)
        return np.concatenate([high, high, low], axis=1)

    return split(even), split(odd), split(even.T), split(odd.T)


def spread(cells, plan, first):
    lane = lax.broadcasted_iota(jnp.int32, cells.shape, 1)
    width = plan.width
    if 2 * width == LANES:
        other = pltpu.roll(cells, width, 1)
        keep = (lane < width) if first == 0 else (lane >= width)
        return jnp.where(keep, cells, other)
    if first:
        cells = pltpu.roll(cells, LANES - first, 1)
    cells = jnp.where(lane < width, cells, 0.0)
    step = width
    while step < LANES:
        cells = cells + pltpu.roll(cells, step, 1)
        step *= 2
    return cells


def lane_sum(cells, plan):
    step = plan.width
    while step < LANES:
        cells = cells + pltpu.roll(cells, step, 1)
        step *= 2
    return cells


def pack_kernel(plan, me_ref, tilt_ref, phase_ref, direction_ref, *outs):
    me = me_ref[0]
    width, half, shard = plan.width, plan.half, plan.shard
    lane = lax.broadcasted_iota(jnp.int32, (half, LANES), 1)
    for k, out in enumerate(outs):
        dest = me ^ k
        frame, group = dest // plan.groups, dest % plan.groups
        back = (LANES - group * width) % LANES
        ahead = (LANES + width - group * width) % LANES
        for parity in range(2):
            own = pl.ds(parity, half, stride=2)
            one = pltpu.roll(phase_ref[frame, own, :], back, 1)
            two = pltpu.roll(direction_ref[frame, own, :], ahead, 1)
            out[parity * half : (parity + 1) * half, :] = jnp.where(lane < width, one, two)
        rows = [jnp.full((1, LANES), tilt_ref[p], jnp.int32).astype(jnp.float32) for p in range(plan.points)]
        for f in range(plan.frames):
            rows += [direction_ref[f, 0:1, :], direction_ref[f, shard - 1 : shard, :]]
        rows += [jnp.zeros((1, LANES), jnp.float32)] * (plan.extra - len(rows))
        out[shard : shard + plan.extra, :] = jnp.concatenate(rows, axis=0)


def wave(turns):
    quarters = jnp.round(turns * 4.0)
    angle = (turns - quarters * 0.25) * (2.0 * np.pi)
    square = angle * angle
    sin_part = ((-1.9515295891e-4 * square + 8.3321608736e-3) * square - 1.6666654611e-1) * square * angle + angle
    cos_part = (
        (2.443315711809948e-5 * square - 1.388731625493765e-3) * square + 4.166664568298827e-2
    ) * (square * square) + (1.0 - 0.5 * square)
    count = quarters.astype(jnp.int32)
    odd = (count & 1) != 0
    cosine = jnp.where(odd, sin_part, cos_part)
    sine = jnp.where(odd, cos_part, sin_part)
    cosine = jnp.where(((count + 1) & 2) != 0, -cosine, cosine)
    sine = jnp.where((count & 2) != 0, -sine, sine)
    return cosine, sine


def put_split(ref, parity, row, rows, cells, column, value):
    high = value.astype(jnp.bfloat16)
    low = (value - high.astype(jnp.float32)).astype(jnp.bfloat16)
    where = slice(column, column + LANES)
    ref[parity, row : row + rows, where] = high
    ref[parity, cells + row : cells + row + rows, where] = low
    ref[parity, 2 * cells + row : 2 * cells + row + rows, where] = high


def main_kernel(plan, me_ref, *refs):
    mods, half, cells, width = plan.mods, plan.half, plan.cells, plan.width
    tiles, wide = plan.tiles, plan.tiles * LANES
    pieces = refs[:mods]
    mask_ref, noise_ref, even_ref, odd_ref, even_back_ref, odd_back_ref, prev_ref, next_ref, flow_ref = refs[mods : mods + 9]
    outs = refs[mods + 9 : 2 * mods + 9]
    turn_ref, dir_ref, cos_ref, sin_ref, in_ref, image_ref, fold_ref, grad_ref = refs[2 * mods + 9 :]
    me = me_ref[0]
    frame, group = me // plan.groups, me % plan.groups
    group_back = (LANES - group * width) % LANES
    lane_row = lax.broadcasted_iota(jnp.int32, (1, LANES), 1)

    for k, piece in enumerate(pieces):
        place = pl.ds(pl.multiple_of((me ^ k) * half, SUB), half)
        for parity in range(2):
            cells_in = piece[parity * half : (parity + 1) * half, :]
            turn_ref[parity, place, :] = spread(cells_in, plan, 0) * (0.5 / np.pi)
            dir_ref[parity, place, :] = spread(cells_in, plan, width)

    tilt_rows = [jnp.zeros((1, LANES), jnp.float32)] * tiles
    for k, piece in enumerate(pieces):
        for p in range(plan.points):
            tile, slot = divmod(k * plan.points + p, plan.copies)
            row = piece[plan.shard + p : plan.shard + p + 1, :]
            tilt_rows[tile] = jnp.where(lane_row // width == slot, row, tilt_rows[tile])

    for parity in range(2):
        for row in range(0, cells, CHUNK):
            here = slice(row, row + CHUNK)
            turns = turn_ref[parity, here, :]
            push = dir_ref[parity, here, :]
            picked = mask_ref[pl.ds(2 * row + parity, CHUNK, stride=2), :].astype(jnp.float32)
            mask = spread(pltpu.roll(picked, group_back, 1), plan, 0)
            spots = lax.broadcasted_iota(jnp.int32, (CHUNK, LANES), 0)
            spots = (2 * (spots + row) + (parity + plan.pupil // 2)).astype(jnp.float32) / plan.length
            for tile in range(tiles):
                tilt = spots * tilt_rows[tile]
                cosine, sine = wave(turns + (tilt - jnp.round(tilt)))
                cosine, sine = cosine * mask, sine * mask
                at = tile * LANES
                cos_ref[parity, here, at : at + LANES] = cosine
                sin_ref[parity, here, at : at + LANES] = sine
                put_split(in_ref, parity, row, CHUNK, cells, at, cosine)
                put_split(in_ref, parity, row, CHUNK, cells, wide + at, sine)
                put_split(in_ref, parity, row, CHUNK, cells, 2 * wide + at, -sine * push)
                put_split(in_ref, parity, row, CHUNK, cells, 3 * wide + at, cosine * push)

    for parity, table in enumerate((even_ref, odd_ref)):
        image_ref[parity] = jnp.dot(table[...], in_ref[1 - parity], preferred_element_type=jnp.float32)

    total = jnp.zeros((SUB, LANES), jnp.float32)
    quarter = cells // 2
    for parity in range(2):
        for row in range(0, cells, CHUNK):
            here = slice(row, row + CHUNK)
            push = dir_ref[parity, here, :]
            even_sum = odd_sum = shift = 0.0
            for tile in range(tiles):
                at = tile * LANES
                cosine = cos_ref[parity, here, at : at + LANES]
                sine = sin_ref[parity, here, at : at + LANES]
                image_cos, image_sin, push_real, push_imag = [
                    image_ref[parity, here, q * wide + at : q * wide + at + LANES] for q in range(4)
                ]
                even_sum += image_sin * push_imag + image_cos * push_real
                odd_sum += cosine * (push_imag - push * image_cos) - sine * (push_real + push * image_sin)
                shift += cosine * image_cos + sine * image_sin
            even_sum = lane_sum(even_sum, plan) * 2.0
            odd_sum = lane_sum(odd_sum, plan)
            signal_after, signal_before = even_sum + odd_sum, even_sum - odd_sum
            inner = row % quarter
            low_half = row < quarter
            after_at = (2 if low_half else 1) * (plan.pupil // 2) + 2 * inner + parity
            before_at = (0 if low_half else 3) * (plan.pupil // 2) + 2 * inner + parity
            noise_after, noise_before = [
                spread(pltpu.roll(noise_ref[frame, pl.ds(first, CHUNK, stride=2), :], group_back, 1), plan, 0)
                for first in (after_at, before_at)
            ]
            weighted_after, weighted_before = noise_after * signal_after, noise_before * signal_before
            squares = weighted_after * signal_after + weighted_before * signal_before
            for r in range(0, CHUNK, SUB):
                total += squares[r : r + SUB]
            both = weighted_after + weighted_before
            gap = (weighted_after - weighted_before) * 0.5
            grad_ref[parity, here, :] = -gap * shift
            for tile in range(tiles):
                at = tile * LANES
                cosine = cos_ref[parity, here, at : at + LANES]
                sine = sin_ref[parity, here, at : at + LANES]
                image_cos = image_ref[parity, here, at : at + LANES]
                image_sin = image_ref[parity, here, wide + at : wide + at + LANES]
                put_split(fold_ref, parity, row, CHUNK, cells, at, gap * cosine + both * image_sin)
                put_split(fold_ref, parity, row, CHUNK, cells, wide + at, gap * sine - both * image_cos)

    for parity, table in enumerate((odd_back_ref, even_back_ref)):
        image_ref[parity, :, : 2 * wide] = jnp.dot(table[...], fold_ref[1 - parity], preferred_element_type=jnp.float32)

    for row in range(0, cells, CHUNK):
        here = slice(row, row + CHUNK)
        grads = []
        for parity in range(2):
            grad = grad_ref[parity, here, :]
            for tile in range(tiles):
                at = tile * LANES
                grad += cos_ref[parity, here, at : at + LANES] * image_ref[parity, here, at : at + LANES]
                grad += sin_ref[parity, here, at : at + LANES] * image_ref[parity, here, wide + at : wide + at + LANES]
            grads.append(lane_sum(grad, plan) * 2.0)
        lane = lax.broadcasted_iota(jnp.int32, (CHUNK, LANES), 1)
        grad_ref[0, here, :] = jnp.where(lane < width, grads[0], grads[1])

    total = jnp.sum(total, axis=0, keepdims=True) / plan.copies + jnp.sum(flow_ref[...], axis=0, keepdims=True)
    rows = [total, prev_ref[0:1, :], next_ref[plan.shard - 1 : plan.shard, :]]
    rows += [jnp.zeros((1, LANES), jnp.float32)] * (SUB - len(rows))
    tail = jnp.concatenate(rows, axis=0)
    for k, out in enumerate(outs):
        place = pl.ds(pl.multiple_of((me ^ k) * half, SUB), half)
        out[0:half, :] = grad_ref[0, place, :]
        out[half : half + SUB, :] = tail


def row_ahead(cells):
    lane = lax.broadcasted_iota(jnp.int32, cells.shape, 1)
    return jnp.where(lane == LANES - 1, 0.0, pltpu.roll(cells, LANES - 1, 1))


def row_behind(cells):
    lane = lax.broadcasted_iota(jnp.int32, cells.shape, 1)
    return jnp.where(lane == 0, 0.0, pltpu.roll(cells, 1, 1))


def shares(codes):
    ahead_x = ((codes % 4).astype(jnp.float32) + 0.5) / 4.0
    ahead_r = ((codes // 4).astype(jnp.float32) + 0.5) / 4.0
    return (1.0 - ahead_x) * (1.0 - ahead_r), ahead_x * (1.0 - ahead_r), (1.0 - ahead_x) * ahead_r, ahead_x * ahead_r


def prior_kernel(plan, total_frames, place_ref, *refs):
    mods, shard, frames = plan.mods, plan.shard, plan.frames
    pieces = refs[: mods - 1]
    direction_ref, prev_ref, next_ref, codes_ref, prior_ref, flow_ref, coef_ref = refs[mods - 1 :]
    me, first_frame = place_ref[0], place_ref[1]
    zero_row = jnp.zeros((1, LANES), jnp.float32)

    below = [zero_row] * (frames + 2)
    above = [zero_row] * (frames + 2)
    for k in range(1, mods):
        source = me ^ k
        for f in range(frames):
            at = shard + plan.points + 2 * f
            above[f + 1] = jnp.where(source == me + 1, pieces[k - 1][at : at + 1, :], above[f + 1])
            below[f + 1] = jnp.where(source == me - 1, pieces[k - 1][at + 1 : at + 2, :], below[f + 1])

    cells = [prev_ref[...]] + [direction_ref[f] for f in range(frames)] + [next_ref[...]]
    row_id = lax.broadcasted_iota(jnp.int32, (shard, LANES), 0)

    def from_next(body, last):
        return jnp.where(row_id == shard - 1, last, pltpu.roll(body, shard - 1, 0))

    def from_last(body, first):
        return jnp.where(row_id == 0, first, pltpu.roll(body, 1, 0))

    begin = pl.multiple_of(me * shard, SUB)
    coef = shares(codes_ref[pl.ds(begin, shard), :])
    before = pl.multiple_of(jnp.maximum(begin - SUB, 0), SUB)
    edge = [jnp.where(me > 0, c[SUB - 1 : SUB], 0.0) for c in shares(codes_ref[pl.ds(before, SUB), :])]

    def moved(share, base, ahead):
        return share[0] * base + share[1] * ahead + share[2] * row_ahead(base) + share[3] * row_ahead(ahead)

    flow, flow_edge = [], []
    for t in range(frames + 1):
        frame = first_frame + t - 1
        valid = (frame >= 0) & (frame <= total_frames - 2)
        ahead = from_next(cells[t], above[t])
        flow.append(jnp.where(valid, cells[t + 1] - moved(coef, cells[t], ahead), 0.0))
        if t > 0:
            value = below[t + 1] - moved(edge, below[t], cells[t][0:1])
            flow_edge.append(jnp.where(valid & (me > 0), value, 0.0))
    total = jnp.zeros((SUB, LANES), jnp.float32)
    for t in range(frames):
        square = flow[t + 1] * flow[t + 1]
        for r in range(0, shard, SUB):
            total += square[r : r + SUB]
        base, side = flow[t + 1], flow_edge[t]
        spread_to = (
            coef[0] * base
            + from_last(coef[1] * base, edge[1] * side)
            + row_behind(coef[2] * base + from_last(coef[3] * base, edge[3] * side))
        )
        prior_ref[t] = flow[t] - spread_to
    flow_ref[...] = total
    rows = [coef[1][shard - 1 : shard], coef[3][shard - 1 : shard], edge[1], edge[3]]
    rows += [zero_row] * (SUB - len(rows))
    coef_ref[...] = jnp.concatenate(rows, axis=0)


def final_kernel(plan, me_ref, *refs):
    mods, half, width, shard = plan.mods, plan.half, plan.width, plan.shard
    pieces = refs[:mods]
    prior_ref, coef_ref, hess_ref, sum_ref = refs[mods : mods + 4]
    me = me_ref[0]
    lane = lax.broadcasted_iota(jnp.int32, (half, LANES), 1)
    for parity in range(2):
        own = pl.ds(parity, half, stride=2)
        for f in range(plan.frames):
            hess_ref[f, own, :] = prior_ref[f, own, :]
        for k, piece in enumerate(pieces):
            source = me ^ k
            frame, group = source // plan.groups, source % plan.groups
            turn = (group * width - parity * width + LANES) % LANES
            moved = pltpu.roll(piece[0:half, :], turn, 1)
            hess_ref[frame, own, :] += jnp.where(lane // width == group, moved, 0.0)
    zero_row = jnp.zeros((1, LANES), jnp.float32)
    total, above, below = zero_row, zero_row, zero_row
    for k, piece in enumerate(pieces):
        source = me ^ k
        total += piece[half : half + 1, :]
        above = jnp.where(source == me + 1, piece[half + 1 : half + 2, :], above)
        below = jnp.where(source == me - 1, piece[half + 2 : half + 3, :], below)
    hess_ref[0, shard - 1 : shard, :] -= coef_ref[0:1, :] * above + coef_ref[1:2, :] * row_ahead(above)
    hess_ref[plan.frames - 1, 0:1, :] -= coef_ref[2:3, :] * below + row_behind(coef_ref[3:4, :] * below)
    sum_ref[...] = jnp.broadcast_to(total, (SUB, LANES))


def exchange(arrays, axis):
    count = lax.axis_size(axis)
    return [arrays[0]] + [
        lax.ppermute(arrays[k], axis, [(i, i ^ k) for i in range(count)]) for k in range(1, count)
    ]


def per_device(phase, direction, pupil_mask, mod_tilts, wind_codes, noise_weight):
    frames, shard, rows = phase.shape
    mods, steps = lax.axis_size("mod"), lax.axis_size("tm")
    plan = Plan(frames, shard, rows, mod_tilts.shape[0], mods)
    f32 = jnp.float32
    me = lax.axis_index("mod").astype(jnp.int32).reshape(1)
    place = jnp.stack([lax.axis_index("mod"), lax.axis_index("tm") * frames]).astype(jnp.int32)
    total_frames = frames * steps

    packed = pl.pallas_call(
        functools.partial(pack_kernel, plan),
        out_shape=[jax.ShapeDtypeStruct((shard + plan.extra, LANES), f32)] * mods,
        in_specs=[SMEM, SMEM, VMEM, VMEM],
        out_specs=[VMEM] * mods,
        compiler_params=params(),
        name="pack",
    )(me, mod_tilts, phase, direction)
    pieces = exchange(packed, "mod")
    prev_frame = lax.ppermute(direction[-1], "tm", [(i, i + 1) for i in range(steps - 1)])
    next_frame = lax.ppermute(direction[0], "tm", [(i + 1, i) for i in range(steps - 1)])

    prior, flow_total, coef = pl.pallas_call(
        functools.partial(prior_kernel, plan, total_frames),
        out_shape=[
            jax.ShapeDtypeStruct(phase.shape, f32),
            jax.ShapeDtypeStruct((SUB, LANES), f32),
            jax.ShapeDtypeStruct((SUB, LANES), f32),
        ],
        in_specs=[SMEM] + [VMEM] * (mods + 3),
        out_specs=[VMEM] * 3,
        compiler_params=params(),
        name="prior",
    )(place, *pieces[1:], direction, prev_frame, next_frame, wind_codes)

    tables = [jnp.asarray(t) for t in roof_tables(plan)]
    cells, wide = plan.cells, plan.tiles * LANES
    grads = pl.pallas_call(
        functools.partial(main_kernel, plan),
        out_shape=[jax.ShapeDtypeStruct((plan.half + SUB, LANES), f32)] * mods,
        in_specs=[SMEM] + [VMEM] * (mods + 9),
        out_specs=[VMEM] * mods,
        scratch_shapes=[
            pltpu.VMEM((2, cells, LANES), f32),
            pltpu.VMEM((2, cells, LANES), f32),
            pltpu.VMEM((2, cells, wide), f32),
            pltpu.VMEM((2, cells, wide), f32),
            pltpu.VMEM((2, 3 * cells, 4 * wide), jnp.bfloat16),
            pltpu.VMEM((2, cells, 4 * wide), f32),
            pltpu.VMEM((2, 3 * cells, 2 * wide), jnp.bfloat16),
            pltpu.VMEM((2, cells, LANES), f32),
        ],
        compiler_params=params(),
        name="data_term",
    )(me, *pieces, pupil_mask, noise_weight, *tables, prev_frame, next_frame, flow_total)
    returned = exchange(grads, "mod")

    hess_vec, mod_total = pl.pallas_call(
        functools.partial(final_kernel, plan),
        out_shape=[jax.ShapeDtypeStruct(phase.shape, f32), jax.ShapeDtypeStruct((SUB, LANES), f32)],
        in_specs=[SMEM] + [VMEM] * (mods + 2),
        out_specs=[VMEM] * 2,
        compiler_params=params(),
        name="join",
    )(me, *returned, prior, coef)
    group_total = sum(exchange([mod_total] * steps, "tm"))
    curvature = (jnp.sum(group_total[0]) / float(total_frames * plan.pupil * rows)).reshape(1)
    return hess_vec, curvature


def solution(mesh):
    return jax.shard_map(
        per_device,
        mesh=mesh,
        in_specs=(
            P(("grp", "tm"), "mod", None),
            P(("grp", "tm"), "mod", None),
            P(),
            P("mod"),
            P("grp", None),
            P(("grp", "tm"), None, None),
        ),
        out_specs=(P(("grp", "tm"), "mod", None), P("grp")),
        check_vma=False,
    )
```

time: 238 us -> 42.2 us (0.18); the launches traced: 235 us -> 41.7 us
  matrix products: 80.7 us -> 0 us
  waiting for transfers between devices: 55.5 us -> 9.74 us
  blocking collectives: 42.3 us -> 0 us
  other arithmetic: 16.2 us -> 0.68 us
  between operations: 17.1 us -> 3.17 us
  local copies, waits for them, and re-layouts: 16.5 us -> 7.76 us
  starting transfers between devices: 6.63 us -> 15.3 us
  Pallas kernels: 0 us -> 5.09 us
    dot_general x48 -> x0, matrix products: 80.7 us -> none  [the longest x12 21.3 us: complex_mix(): imag_real = jnp.einsum(form, table_imag, field_real, precision=HIGHEST)]
    psum x1 -> x0, blocking collectives: 32.8 us -> none  [per_device(): curvature_total = lax.psum(jnp.sum(direction * hess_vec), ('tm', 'mod'))]
    psum x1 -> x0, waiting for transfers between devices: 30.2 us -> none  [per_device(): signal_full = lax.psum(signal_local, 'mod')]
    reduce_scatter x1 -> x0, waiting for transfers between devices: 18 us -> none  [per_device(): lax.psum_scatter(grad_lines, 'mod', scatter_dimension=1, tiled=True)]
    all_gather x1 -> x0, blocking collectives: 9.44 us -> none  [per_device(): lax.all_gather(phase, 'mod', axis=1, tiled=True)]
    ppermute x2 -> x11, starting transfers between devices: 6.22 us -> 15.3 us  [the longest x9 8.45 us: exchange(): lax.ppermute(arrays[k], axis, [(i, i ^ k) for i in range(count)])]
    mul x6 -> x0, other arithmetic: 8.21 us -> none  [the longest x1 4.07 us: forward_pass(): -field_imag * full_direction]
    slice x9 -> x0, local copies, waits for them, and re-layouts: 7.5 us -> none  [the longest x1 1.96 us: row_ahead(): return jnp.pad(field[:, :, 1:], ((0, 0), (0, 0), (0, 1)))]
  transfers between devices with their start and end apart: 5 -> 11, of which waited for: 4 -> 7; matrix products, arithmetic and copies ran while one was open for 5% -> 0% of each run, Pallas kernels for 0% -> 0%
where the time goes in v1:
time: 42.2 us; the launch traced here: 41.7 us
  starting transfers between devices  15.3 us (36%)
  waiting for transfers between devices  9.74 us (23%)
  local copies, waits for them, and re-layouts  7.76 us (18%)
  Pallas kernels  5.09 us (12%)
  between operations  3.17 us (8%)
  other arithmetic  0.68 us (2%)
    ppermute x9, waiting for transfers between devices, exchange(): lax.ppermute(arrays[k], axis, [(i, i ^ k) for i in range(count)])  9.73 us
    ppermute x9, starting transfers between devices, exchange(): lax.ppermute(arrays[k], axis, [(i, i ^ k) for i in range(count)])  8.45 us
    unnamed x18, local copies, waits for them, and re-layouts  6.78 us
    ppermute x1, starting transfers between devices, per_device(): lax.ppermute(direction[-1], 'tm', [(i, i + 1) for i in range(steps - 1)])  5.56 us
    pallas_call x1, Pallas kernels, per_device(): pl.pallas_call(functools.partial(main_kernel, plan), out_shape=[jax.Shape...  3.26 us
    ppermute x1, starting transfers between devices, per_device(): lax.ppermute(direction[0], 'tm', [(i + 1, i) for i in range(steps - 1)])  1.29 us
    squeeze x1, local copies, waits for them, and re-layouts, per_device(): direction[0]  0.98 us
  transfers between devices with their start and end apart: 11, of which 7 were waited for; matrix products, arithmetic and copies ran while one was open for 0% of the time, Pallas kernels for 0%

profile of v1, /device:TPU:0, one launch (start us, length us, event | category | flops | bytes accessed | tf_op | source)
XLA Modules:
  0.0 41.7 jit_solution(14375689400114932710)
XLA Ops:
  0.6 0.0 copy-start
  0.6 0.0 copy-start.1
  0.6 1.0 %slice_bitcast_fusion = (f32[128,128]{1,0:T(8,128)S(1)}, f32[128,128]{1,0:T(8,128)S(1)}) fusion(f32[2,128,128]{2,1,0:T(8,128)} %refs_3_.1), kind=kLoop, calls=%fused_computation | loop fusion | bytes 262144 | tf_op jit(solution)/shard_map/squeeze | solution.py:383
  1.6 1.3 %collective-permute-start.4 = (f32[128,128]{1,0:T(8,128)S(1)}, f32[128,128]{1,0:T(8,128)S(1)}, u32[]{:S(2)}, u32[]{:S(2)}) collective-permute-start(f32[128,128]{1,0:T(8,128)S(1)} %get-tuple-element.28), channel_id=1, source_target_pairs={{4,0},{8,4},{12,8},{5,1},{9,5},{13,9},{6,2},{10,6},{14,10},{7,3},{... | collective-permute-start | bytes 196616 | tf_op jit(solution)/shard_map/ppermute | solution.py:383
  2.9 5.6 %collective-permute-start.3 = (f32[128,128]{1,0:T(8,128)S(1)}, f32[128,128]{1,0:T(8,128)S(1)}, u32[]{:S(2)}, u32[]{:S(2)}) collective-permute-start(f32[128,128]{1,0:T(8,128)S(1)} %get-tuple-element.29), channel_id=1, source_target_pairs={{0,4},{4,8},{8,12},{1,5},{5,9},{9,13},{2,6},{6,10},{10,14},{3,7},{... | collective-permute-start | bytes 196616 | tf_op jit(solution)/shard_map/ppermute | solution.py:382
  9.1 0.0 copy-done
  9.2 0.0 copy-start.8
  9.2 0.9 %copy-done.8 = f32[2,128,128]{2,1,0:T(8,128)S(1)} copy-done((f32[2,128,128]{2,1,0:T(8,128)S(1)}, f32[2,128,128]{2,1,0:T(8,128)}, u32[]{:S(2)}) %copy-start.8) | copy-done | bytes 131096
  10.1 0.2 pack.1
  10.3 0.1 collective-permute-start
  10.4 2.0 %collective-permute-start.1 = (f32[136,128]{1,0:T(8,128)S(1)}, f32[136,128]{1,0:T(8,128)S(1)}, u32[]{:S(2)}, u32[]{:S(2)}) collective-permute-start(f32[136,128]{1,0:T(8,128)S(1)} %get-tuple-element.17), channel_id=1, source_target_pairs={{0,2},{1,3},{2,0},{3,1},{4,6},{5,7},{6,4},{7,5},{8,10},{9,11},{10,... | collective-permute-start | bytes 208904 | tf_op jit(solution)/shard_map/ppermute | solution.py:360
  12.3 0.1 collective-permute-start.2
  12.4 0.1 pad_add_fusion.place_ref
  12.5 0.0 collective-permute-done.4.refs_5_.refs_11_
  12.5 0.0 collective-permute-done.3.refs_4_.refs_10_
  12.5 0.0 collective-permute-done.refs_0_.refs_1_
  12.5 2.6 %collective-permute-done.1.refs_1_.refs_2_ = f32[136,128]{1,0:T(8,128)S(1)} collective-permute-done((f32[136,128]{1,0:T(8,128)S(1)}, f32[136,128]{1,0:T(8,128)S(1)}, u32[]{:S(2)}, u32[]{:S(2)}) %collective-permute-start.1) | collective-permute-done | bytes 69664 | tf_op jit(solution)/shard_map/ppermute | solution.py:360
  15.1 1.4 %collective-permute-done.2.refs_2_.refs_3_ = f32[136,128]{1,0:T(8,128)S(1)} collective-permute-done((f32[136,128]{1,0:T(8,128)S(1)}, f32[136,128]{1,0:T(8,128)S(1)}, u32[]{:S(2)}, u32[]{:S(2)}) %collective-permute-start.2) | collective-permute-done | bytes 69664 | tf_op jit(solution)/shard_map/ppermute | solution.py:360
  16.5 0.0 copy-start.6
  16.5 0.9 %copy-done.6 = s32[512,128]{1,0:T(8,128)S(1)} copy-done((s32[512,128]{1,0:T(8,128)S(1)}, s32[512,128]{1,0:T(8,128)}, u32[]{:S(2)}) %copy-start.6) | copy-done | bytes 262168
  17.4 0.8 %prior.1 = (f32[2,128,128]{2,1,0:T(8,128)S(1)}, f32[8,128]{1,0:T(8,128)S(1)}, f32[8,128]{1,0:T(8,128)S(1)}) custom-call(s32[2]{0:T(128)S(1)} %pad_add_fusion.place_ref, f32[136,128]{1,0:T(8,128)S(1)} %collective-permute-done.refs_0_.refs_1_, f32[136,128]{1,0:T(8,128)S(1)} %collective-permute-done.1.refs_1_.refs_2_, ...), custom_call_target="tpu_custom_call" | custom-call | tf_op jit(solution)/shard_map/prior/pallas_call | solution.py:385
  18.3 0.0 copy-done.1
  18.3 0.0 copy-start.2
  18.3 1.0 %copy-done.2 = bf16[256,768]{1,0:T(8,128)(2,1)S(1)} copy-done((bf16[256,768]{1,0:T(8,128)(2,1)S(1)}, bf16[256,768]{1,0:T(8,128)(2,1)}, u32[]{:S(2)}) %copy-start.2) | copy-done | bytes 393240
  19.3 0.0 copy-start.3
  19.3 1.0 %copy-done.3 = bf16[256,768]{1,0:T(8,128)(2,1)S(1)} copy-done((bf16[256,768]{1,0:T(8,128)(2,1)S(1)}, bf16[256,768]{1,0:T(8,128)(2,1)}, u32[]{:S(2)}) %copy-start.3) | copy-done | bytes 393240
  20.3 0.0 copy-start.4
  20.3 1.0 %copy-done.4 = bf16[256,768]{1,0:T(8,128)(2,1)S(1)} copy-done((bf16[256,768]{1,0:T(8,128)(2,1)S(1)}, bf16[256,768]{1,0:T(8,128)(2,1)}, u32[]{:S(2)}) %copy-start.4) | copy-done | bytes 393240
  21.3 0.0 copy-start.5
  21.3 1.0 %copy-done.5 = bf16[256,768]{1,0:T(8,128)(2,1)S(1)} copy-done((bf16[256,768]{1,0:T(8,128)(2,1)S(1)}, bf16[256,768]{1,0:T(8,128)(2,1)}, u32[]{:S(2)}) %copy-start.5) | copy-done | bytes 393240
  22.3 0.0 copy-start.7
  22.3 0.9 %copy-done.7 = s32[512,128]{1,0:T(8,128)S(1)} copy-done((s32[512,128]{1,0:T(8,128)S(1)}, s32[512,128]{1,0:T(8,128)}, u32[]{:S(2)}) %copy-start.7) | copy-done | bytes 262168
  23.2 3.3 %data_term.1 = (f32[72,128]{1,0:T(8,128)S(1)}, f32[72,128]{1,0:T(8,128)S(1)}, f32[72,128]{1,0:T(8,128)S(1)}, f32[72,128]{1,0:T(8,128)S(1)}) custom-call(s32[1]{0:T(128)} %bitcast.me_ref, f32[136,128]{1,0:T(8,128)S(1)} %get-tuple-element.15.refs_0_, f32[136,128]{1,0:T(8,128)S(1)} %collective-permute-done.refs_0_.refs_1_, ...), custom_call_target="tpu_custom_call" | custom-call | tf_op jit(solution)/shard_map/data_term/pallas_call | solution.py:400
  26.5 0.2 collective-permute-start.5
  26.7 1.5 %collective-permute-start.6 = (f32[72,128]{1,0:T(8,128)S(1)}, f32[72,128]{1,0:T(8,128)S(1)}, u32[]{:S(2)}, u32[]{:S(2)}) collective-permute-start(f32[72,128]{1,0:T(8,128)S(1)} %get-tuple-element.22), channel_id=1, source_target_pairs={{0,2},{1,3},{2,0},{3,1},{4,6},{5,7},{6,4},{7,5},{8,10},{9,11},{10,... | collective-permute-start | bytes 110600 | tf_op jit(solution)/shard_map/ppermute | solution.py:360
  28.3 0.2 collective-permute-start.7
  28.4 0.0 collective-permute-done.5.refs_1_
  28.4 2.3 %collective-permute-done.6.refs_2_ = f32[72,128]{1,0:T(8,128)S(1)} collective-permute-done((f32[72,128]{1,0:T(8,128)S(1)}, f32[72,128]{1,0:T(8,128)S(1)}, u32[]{:S(2)}, u32[]{:S(2)}) %collective-permute-start.6) | collective-permute-done | bytes 36896 | tf_op jit(solution)/shard_map/ppermute | solution.py:360
  30.7 1.2 %collective-permute-done.7.refs_3_ = f32[72,128]{1,0:T(8,128)S(1)} collective-permute-done((f32[72,128]{1,0:T(8,128)S(1)}, f32[72,128]{1,0:T(8,128)S(1)}, u32[]{:S(2)}, u32[]{:S(2)}) %collective-permute-start.7) | collective-permute-done | bytes 36896 | tf_op jit(solution)/shard_map/ppermute | solution.py:360
  31.9 0.8 %join.1 = (f32[2,128,128]{2,1,0:T(8,128)}, f32[8,128]{1,0:T(8,128)S(1)}) custom-call(s32[1]{0:T(128)} %bitcast.me_ref, f32[72,128]{1,0:T(8,128)S(1)} %get-tuple-element.20.refs_0_, f32[72,128]{1,0:T(8,128)S(1)} %collective-permute-done.5.refs_1_, f32[72,128]{1,0:T(8,128)S(1)} %collective-permute-done.6.refs_2_, ...), custom_call_target="tpu_custom_call" | custom-call | tf_op jit(solution)/shard_map/join/pallas_call | solution.py:420
  32.7 1.4 %collective-permute-start.10 = (f32[8,128]{1,0:T(8,128)S(1)}, f32[8,128]{1,0:T(8,128)S(1)}, u32[]{:S(2)}, u32[]{:S(2)}) collective-permute-start(f32[8,128]{1,0:T(8,128)S(1)} %get-tuple-element.27), channel_id=1, source_target_pairs={{0,12},{4,8},{8,4},{12,0},{1,13},{5,9},{9,5},{13,1},{2,14},{6,10},... | collective-permute-start | bytes 12296 | tf_op jit(solution)/shard_map/ppermute | solution.py:360
  34.1 1.6 %collective-permute-start.9 = (f32[8,128]{1,0:T(8,128)S(1)}, f32[8,128]{1,0:T(8,128)S(1)}, u32[]{:S(2)}, u32[]{:S(2)}) collective-permute-start(f32[8,128]{1,0:T(8,128)S(1)} %get-tuple-element.27), channel_id=1, source_target_pairs={{0,8},{4,12},{8,0},{12,4},{1,9},{5,13},{9,1},{13,5},{2,10},{6,14},... | collective-permute-start | bytes 12296 | tf_op jit(solution)/shard_map/ppermute | solution.py:360
  35.8 1.3 %collective-permute-start.8 = (f32[8,128]{1,0:T(8,128)S(1)}, f32[8,128]{1,0:T(8,128)S(1)}, u32[]{:S(2)}, u32[]{:S(2)}) collective-permute-start(f32[8,128]{1,0:T(8,128)S(1)} %get-tuple-element.27), channel_id=1, source_target_pairs={{0,4},{4,0},{8,12},{12,8},{1,5},{5,1},{9,13},{13,9},{2,6},{6,2},{1... | collective-permute-start | bytes 12296 | tf_op jit(solution)/shard_map/ppermute | solution.py:360
  37.1 1.0 %collective-permute-done.10 = f32[8,128]{1,0:T(8,128)S(1)} collective-permute-done((f32[8,128]{1,0:T(8,128)S(1)}, f32[8,128]{1,0:T(8,128)S(1)}, u32[]{:S(2)}, u32[]{:S(2)}) %collective-permute-start.10) | collective-permute-done | bytes 4128 | tf_op jit(solution)/shard_map/ppermute | solution.py:360
  38.1 0.5 %collective-permute-done.9 = f32[8,128]{1,0:T(8,128)S(1)} collective-permute-done((f32[8,128]{1,0:T(8,128)S(1)}, f32[8,128]{1,0:T(8,128)S(1)}, u32[]{:S(2)}, u32[]{:S(2)}) %collective-permute-start.9) | collective-permute-done | bytes 4128 | tf_op jit(solution)/shard_map/ppermute | solution.py:360
  38.6 0.7 %collective-permute-done.8 = f32[8,128]{1,0:T(8,128)S(1)} collective-permute-done((f32[8,128]{1,0:T(8,128)S(1)}, f32[8,128]{1,0:T(8,128)S(1)}, u32[]{:S(2)}, u32[]{:S(2)}) %collective-permute-start.8) | collective-permute-done | bytes 4128 | tf_op jit(solution)/shard_map/ppermute | solution.py:360
  39.4 0.6 %slice_reduce_fusion = f32[]{:T(128)} fusion(f32[8,128]{1,0:T(8,128)S(1)} %add_add_fusion), kind=kLoop, calls=%fused_computation.4 | loop fusion | flops 127 | bytes 516 | tf_op jit(solution)/shard_map/reduce_sum | solution.py:429
  (1 shorter events, 0.0 us)
Async XLA Ops:
  0.6 8.5 %copy-start = (f32[2,128,128]{2,1,0:T(8,128)S(1)}, f32[2,128,128]{2,1,0:T(8,128)}, u32[]{:S(2)}) copy-start(f32[2,128,128]{2,1,0:T(8,128)} %refs_3_.1) | copy-start | bytes 393220
  0.6 17.6 %copy-start.1 = (f32[2,1024,128]{2,1,0:T(8,128)S(1)}, f32[2,1024,128]{2,1,0:T(8,128)}, u32[]{:S(2)}) copy-start(f32[2,1024,128]{2,1,0:T(8,128)} %refs_5_.1) | copy-start | bytes 3145732
  1.6 10.9 %collective-permute-start.4 = (f32[128,128]{1,0:T(8,128)S(1)}, f32[128,128]{1,0:T(8,128)S(1)}, u32[]{:S(2)}, u32[]{:S(2)}) collective-permute-start(f32[128,128]{1,0:T(8,128)S(1)} %get-tuple-element.28), channel_id=1, source_target_pairs={{4,0},{8,4},{12,8},{5,1},{9,5},{13,9},{6,2},{10,6},{14,10},{7,3},{... | collective-permute-start | bytes 196616 | tf_op jit(solution)/shard_map/ppermute | solution.py:383
  2.9 9.6 %collective-permute-start.3 = (f32[128,128]{1,0:T(8,128)S(1)}, f32[128,128]{1,0:T(8,128)S(1)}, u32[]{:S(2)}, u32[]{:S(2)}) collective-permute-start(f32[128,128]{1,0:T(8,128)S(1)} %get-tuple-element.29), channel_id=1, source_target_pairs={{0,4},{4,8},{8,12},{1,5},{5,9},{9,13},{2,6},{6,10},{10,14},{3,7},{... | collective-permute-start | bytes 196616 | tf_op jit(solution)/shard_map/ppermute | solution.py:382
  9.2 0.9 %copy-start.8 = (f32[2,128,128]{2,1,0:T(8,128)S(1)}, f32[2,128,128]{2,1,0:T(8,128)}, u32[]{:S(2)}) copy-start(f32[2,128,128]{2,1,0:T(8,128)} %phase_ref.1) | copy-start | bytes 393220
  10.3 2.2 %collective-permute-start = (f32[136,128]{1,0:T(8,128)S(1)}, f32[136,128]{1,0:T(8,128)S(1)}, u32[]{:S(2)}, u32[]{:S(2)}) collective-permute-start(f32[136,128]{1,0:T(8,128)S(1)} %get-tuple-element.16), channel_id=1, source_target_pairs={{0,1},{1,0},{2,3},{3,2},{4,5},{5,4},{6,7},{7,6},{8,9},{9,8},{10,11... | collective-permute-start | bytes 208904 | tf_op jit(solution)/shard_map/ppermute | solution.py:360
  10.4 4.8 %collective-permute-start.1 = (f32[136,128]{1,0:T(8,128)S(1)}, f32[136,128]{1,0:T(8,128)S(1)}, u32[]{:S(2)}, u32[]{:S(2)}) collective-permute-start(f32[136,128]{1,0:T(8,128)S(1)} %get-tuple-element.17), channel_id=1, source_target_pairs={{0,2},{1,3},{2,0},{3,1},{4,6},{5,7},{6,4},{7,5},{8,10},{9,11},{10,... | collective-permute-start | bytes 208904 | tf_op jit(solution)/shard_map/ppermute | solution.py:360
  12.3 4.1 %collective-permute-start.2 = (f32[136,128]{1,0:T(8,128)S(1)}, f32[136,128]{1,0:T(8,128)S(1)}, u32[]{:S(2)}, u32[]{:S(2)}) collective-permute-start(f32[136,128]{1,0:T(8,128)S(1)} %get-tuple-element.18), channel_id=1, source_target_pairs={{0,3},{1,2},{2,1},{3,0},{4,7},{5,6},{6,5},{7,4},{8,11},{9,10},{10,... | collective-permute-start | bytes 208904 | tf_op jit(solution)/shard_map/ppermute | solution.py:360
  16.5 1.0 %copy-start.6 = (s32[512,128]{1,0:T(8,128)S(1)}, s32[512,128]{1,0:T(8,128)}, u32[]{:S(2)}) copy-start(s32[512,128]{1,0:T(8,128)} %refs_6_.2) | copy-start | bytes 786436
  18.3 1.0 %copy-start.2 = (bf16[256,768]{1,0:T(8,128)(2,1)S(1)}, bf16[256,768]{1,0:T(8,128)(2,1)}, u32[]{:S(2)}) copy-start(bf16[256,768]{1,0:T(8,128)(2,1)} %constant.25.clone.refs_9_) | copy-start | bytes 1179652
  19.3 1.0 %copy-start.3 = (bf16[256,768]{1,0:T(8,128)(2,1)S(1)}, bf16[256,768]{1,0:T(8,128)(2,1)}, u32[]{:S(2)}) copy-start(bf16[256,768]{1,0:T(8,128)(2,1)} %constant.24.clone.refs_8_) | copy-start | bytes 1179652
  20.3 1.0 %copy-start.4 = (bf16[256,768]{1,0:T(8,128)(2,1)S(1)}, bf16[256,768]{1,0:T(8,128)(2,1)}, u32[]{:S(2)}) copy-start(bf16[256,768]{1,0:T(8,128)(2,1)} %constant.23.clone.refs_7_) | copy-start | bytes 1179652
  21.3 1.0 %copy-start.5 = (bf16[256,768]{1,0:T(8,128)(2,1)S(1)}, bf16[256,768]{1,0:T(8,128)(2,1)}, u32[]{:S(2)}) copy-start(bf16[256,768]{1,0:T(8,128)(2,1)} %constant.22.clone.refs_6_) | copy-start | bytes 1179652
  22.3 0.9 %copy-start.7 = (s32[512,128]{1,0:T(8,128)S(1)}, s32[512,128]{1,0:T(8,128)}, u32[]{:S(2)}) copy-start(s32[512,128]{1,0:T(8,128)} %refs_4_.1) | copy-start | bytes 786436
  26.5 1.9 %collective-permute-start.5 = (f32[72,128]{1,0:T(8,128)S(1)}, f32[72,128]{1,0:T(8,128)S(1)}, u32[]{:S(2)}, u32[]{:S(2)}) collective-permute-start(f32[72,128]{1,0:T(8,128)S(1)} %get-tuple-element.21), channel_id=1, source_target_pairs={{0,1},{1,0},{2,3},{3,2},{4,5},{5,4},{6,7},{7,6},{8,9},{9,8},{10,11... | collective-permute-start | bytes 110600 | tf_op jit(solution)/shard_map/ppermute | solution.py:360
  26.7 4.0 %collective-permute-start.6 = (f32[72,128]{1,0:T(8,128)S(1)}, f32[72,128]{1,0:T(8,128)S(1)}, u32[]{:S(2)}, u32[]{:S(2)}) collective-permute-start(f32[72,128]{1,0:T(8,128)S(1)} %get-tuple-element.22), channel_id=1, source_target_pairs={{0,2},{1,3},{2,0},{3,1},{4,6},{5,7},{6,4},{7,5},{8,10},{9,11},{10,... | collective-permute-start | bytes 110600 | tf_op jit(solution)/shard_map/ppermute | solution.py:360
  28.3 3.6 %collective-permute-start.7 = (f32[72,128]{1,0:T(8,128)S(1)}, f32[72,128]{1,0:T(8,128)S(1)}, u32[]{:S(2)}, u32[]{:S(2)}) collective-permute-start(f32[72,128]{1,0:T(8,128)S(1)} %get-tuple-element.23), channel_id=1, source_target_pairs={{0,3},{1,2},{2,1},{3,0},{4,7},{5,6},{6,5},{7,4},{8,11},{9,10},{10,... | collective-permute-start | bytes 110600 | tf_op jit(solution)/shard_map/ppermute | solution.py:360
  32.7 5.4 %collective-permute-start.10 = (f32[8,128]{1,0:T(8,128)S(1)}, f32[8,128]{1,0:T(8,128)S(1)}, u32[]{:S(2)}, u32[]{:S(2)}) collective-permute-start(f32[8,128]{1,0:T(8,128)S(1)} %get-tuple-element.27), channel_id=1, source_target_pairs={{0,12},{4,8},{8,4},{12,0},{1,13},{5,9},{9,5},{13,1},{2,14},{6,10},... | collective-permute-start | bytes 12296 | tf_op jit(solution)/shard_map/ppermute | solution.py:360
  34.1 4.5 %collective-permute-start.9 = (f32[8,128]{1,0:T(8,128)S(1)}, f32[8,128]{1,0:T(8,128)S(1)}, u32[]{:S(2)}, u32[]{:S(2)}) collective-permute-start(f32[8,128]{1,0:T(8,128)S(1)} %get-tuple-element.27), channel_id=1, source_target_pairs={{0,8},{4,12},{8,0},{12,4},{1,9},{5,13},{9,1},{13,5},{2,10},{6,14},... | collective-permute-start | bytes 12296 | tf_op jit(solution)/shard_map/ppermute | solution.py:360
  35.8 3.6 %collective-permute-start.8 = (f32[8,128]{1,0:T(8,128)S(1)}, f32[8,128]{1,0:T(8,128)S(1)}, u32[]{:S(2)}, u32[]{:S(2)}) collective-permute-start(f32[8,128]{1,0:T(8,128)S(1)} %get-tuple-element.27), channel_id=1, source_target_pairs={{0,4},{4,0},{8,12},{12,8},{1,5},{5,1},{9,13},{13,9},{2,6},{6,2},{1... | collective-permute-start | bytes 12296 | tf_op jit(solution)/shard_map/ppermute | solution.py:360

commit v2 on v1

--- a/solution.py
+++ b/solution.py
@@ -14,6 +14,7 @@
 CHUNK = 32
 VMEM = pl.BlockSpec(memory_space=pltpu.VMEM)
 SMEM = pl.BlockSpec(memory_space=pltpu.SMEM)
+HBM = pl.BlockSpec(memory_space=pltpu.HBM)
 
 
 def params():
@@ -83,10 +84,27 @@
     return cells
 
 
-def pack_kernel(plan, me_ref, tilt_ref, phase_ref, direction_ref, *outs):
-    me = me_ref[0]
-    width, half, shard = plan.width, plan.half, plan.shard
+def place_on(axis):
+    return lax.axis_index(axis)
+
+
+def pack_kernel(plan, tilt_hbm, phase_hbm, direction_hbm, *refs):
+    mods = plan.mods
+    outs = refs[:mods]
+    direction_ref, first_ref, second_ref, phase_ref, tilt_ref, sems = refs[mods:]
+    loads = [
+        pltpu.make_async_copy(source, target, sems.at[i])
+        for i, (source, target) in enumerate(
+            ((direction_hbm, direction_ref), (phase_hbm, phase_ref), (tilt_hbm, tilt_ref))
+        )
+    ]
+    for load in loads:
+        load.start()
+    me, step = place_on("mod"), place_on("tm")
+    width, half, shard, frames = plan.width, plan.half, plan.shard, plan.frames
     lane = lax.broadcasted_iota(jnp.int32, (half, LANES), 1)
+    for load in loads:
+        load.wait()
     for k, out in enumerate(outs):
         dest = me ^ k
         frame, group = dest // plan.groups, dest % plan.groups
@@ -98,10 +116,59 @@
             two = pltpu.roll(direction_ref[frame, own, :], ahead, 1)
             out[parity * half : (parity + 1) * half, :] = jnp.where(lane < width, one, two)
         rows = [jnp.full((1, LANES), tilt_ref[p], jnp.int32).astype(jnp.float32) for p in range(plan.points)]
-        for f in range(plan.frames):
+        for f in range(frames):
             rows += [direction_ref[f, 0:1, :], direction_ref[f, shard - 1 : shard, :]]
         rows += [jnp.zeros((1, LANES), jnp.float32)] * (plan.extra - len(rows))
         out[shard : shard + plan.extra, :] = jnp.concatenate(rows, axis=0)
+    even = step % 2 == 0
+    first_ref[...] = direction_ref[jnp.where(even, frames - 1, 0)]
+    second_ref[...] = direction_ref[jnp.where(even, 0, frames - 1)]
+
+
+def prep_kernel(plan, seed_ref, mask_hbm, noise_hbm, codes_hbm, *refs):
+    tables_hbm, refs = refs[:4], refs[4:]
+    tables, (mask_out, noise_out, coef_out, edge_out), refs = refs[:4], refs[4:8], refs[8:]
+    mask_ref, noise_ref, codes_ref, sems = refs
+    me = place_on("mod")
+    shard, cells, quarter_line = plan.shard, plan.cells, plan.pupil // 2
+    frame, group = me // plan.groups, me % plan.groups
+    group_back = (LANES - group * plan.width) % LANES
+    begin = pl.multiple_of(me * shard, SUB)
+    before = pl.multiple_of(jnp.maximum(begin - SUB, 0), SUB)
+    pairs = [
+        (mask_hbm, mask_ref),
+        (noise_hbm.at[frame], noise_ref),
+        (codes_hbm.at[pl.ds(before, SUB)], codes_ref.at[0:SUB]),
+        (codes_hbm.at[pl.ds(begin, shard)], codes_ref.at[SUB : SUB + shard]),
+    ] + list(zip(tables_hbm, tables))
+    loads = [pltpu.make_async_copy(source, target, sems.at[i]) for i, (source, target) in enumerate(pairs)]
+    for load in loads:
+        load.start()
+
+    def own_rows(cells_in):
+        return spread(pltpu.roll(cells_in, group_back, 1), plan, 0)
+
+    loads[0].wait()
+    for parity in range(2):
+        for row in range(0, cells, CHUNK):
+            picked = mask_ref[pl.ds(2 * row + parity, CHUNK, stride=2), :].astype(jnp.float32)
+            mask_out[parity, row : row + CHUNK, :] = own_rows(picked)
+    loads[1].wait()
+    for parity in range(2):
+        for row in range(0, cells, CHUNK):
+            low_half = row < cells // 2
+            inner = 2 * (row % (cells // 2)) + parity
+            for side, block in enumerate((2, 0) if low_half else (1, 3)):
+                picked = noise_ref[pl.ds(block * quarter_line + inner, CHUNK, stride=2), :]
+                noise_out[side, parity, row : row + CHUNK, :] = own_rows(picked)
+    loads[2].wait()
+    loads[3].wait()
+    for i, share in enumerate(shares(codes_ref[SUB : SUB + shard, :])):
+        coef_out[i] = share
+    for i, share in enumerate(shares(codes_ref[0:SUB, :])):
+        edge_out[i] = jnp.where(me > 0, share, 0.0)
+    for load in loads[4:]:
+        load.wait()
 
 
 def wave(turns):
@@ -130,16 +197,14 @@
     ref[parity, 2 * cells + row : 2 * cells + row + rows, where] = high
 
 
-def main_kernel(plan, me_ref, *refs):
-    mods, half, cells, width = plan.mods, plan.half, plan.cells, plan.width
+def forward_kernel(plan, *refs):
+    mods, half, cells = plan.mods, plan.half, plan.cells
     tiles, wide = plan.tiles, plan.tiles * LANES
     pieces = refs[:mods]
-    mask_ref, noise_ref, even_ref, odd_ref, even_back_ref, odd_back_ref, prev_ref, next_ref, flow_ref = refs[mods : mods + 9]
-    outs = refs[mods + 9 : 2 * mods + 9]
-    turn_ref, dir_ref, cos_ref, sin_ref, in_ref, image_ref, fold_ref, grad_ref = refs[2 * mods + 9 :]
-    me = me_ref[0]
-    frame, group = me // plan.groups, me % plan.groups
-    group_back = (LANES - group * width) % LANES
+    mask_ref, noise_ref, even_ref, odd_ref, flow_ref = refs[mods : mods + 5]
+    cos_ref, sin_ref, fold_ref, grad_ref, total_ref = refs[mods + 5 : mods + 10]
+    turn_ref, dir_ref, in_ref, image_ref = refs[mods + 10 :]
+    me = place_on("mod")
     lane_row = lax.broadcasted_iota(jnp.int32, (1, LANES), 1)
 
     for k, piece in enumerate(pieces):
@@ -147,22 +212,21 @@
         for parity in range(2):
             cells_in = piece[parity * half : (parity + 1) * half, :]
             turn_ref[parity, place, :] = spread(cells_in, plan, 0) * (0.5 / np.pi)
-            dir_ref[parity, place, :] = spread(cells_in, plan, width)
+            dir_ref[parity, place, :] = spread(cells_in, plan, plan.width)
 
     tilt_rows = [jnp.zeros((1, LANES), jnp.float32)] * tiles
     for k, piece in enumerate(pieces):
         for p in range(plan.points):
             tile, slot = divmod(k * plan.points + p, plan.copies)
             row = piece[plan.shard + p : plan.shard + p + 1, :]
-            tilt_rows[tile] = jnp.where(lane_row // width == slot, row, tilt_rows[tile])
+            tilt_rows[tile] = jnp.where(lane_row // plan.width == slot, row, tilt_rows[tile])
 
     for parity in range(2):
         for row in range(0, cells, CHUNK):
             here = slice(row, row + CHUNK)
             turns = turn_ref[parity, here, :]
             push = dir_ref[parity, here, :]
-            picked = mask_ref[pl.ds(2 * row + parity, CHUNK, stride=2), :].astype(jnp.float32)
-            mask = spread(pltpu.roll(picked, group_back, 1), plan, 0)
+            mask = mask_ref[parity, here, :]
             spots = lax.broadcasted_iota(jnp.int32, (CHUNK, LANES), 0)
             spots = (2 * (spots + row) + (parity + plan.pupil // 2)).astype(jnp.float32) / plan.length
             for tile in range(tiles):
@@ -181,7 +245,6 @@
         image_ref[parity] = jnp.dot(table[...], in_ref[1 - parity], preferred_element_type=jnp.float32)
 
     total = jnp.zeros((SUB, LANES), jnp.float32)
-    quarter = cells // 2
     for parity in range(2):
         for row in range(0, cells, CHUNK):
             here = slice(row, row + CHUNK)
@@ -200,15 +263,8 @@
             even_sum = lane_sum(even_sum, plan) * 2.0
             odd_sum = lane_sum(odd_sum, plan)
             signal_after, signal_before = even_sum + odd_sum, even_sum - odd_sum
-            inner = row % quarter
-            low_half = row < quarter
-            after_at = (2 if low_half else 1) * (plan.pupil // 2) + 2 * inner + parity
-            before_at = (0 if low_half else 3) * (plan.pupil // 2) + 2 * inner + parity
-            noise_after, noise_before = [
-                spread(pltpu.roll(noise_ref[frame, pl.ds(first, CHUNK, stride=2), :], group_back, 1), plan, 0)
-                for first in (after_at, before_at)
-            ]
-            weighted_after, weighted_before = noise_after * signal_after, noise_before * signal_before
+            weighted_after = noise_ref[0, parity, here, :] * signal_after
+            weighted_before = noise_ref[1, parity, here, :] * signal_before
             squares = weighted_after * signal_after + weighted_before * signal_before
             for r in range(0, CHUNK, SUB):
                 total += squares[r : r + SUB]
@@ -223,30 +279,40 @@
                 image_sin = image_ref[parity, here, wide + at : wide + at + LANES]
                 put_split(fold_ref, parity, row, CHUNK, cells, at, gap * cosine + both * image_sin)
                 put_split(fold_ref, parity, row, CHUNK, cells, wide + at, gap * sine - both * image_cos)
-
-    for parity, table in enumerate((odd_back_ref, even_back_ref)):
-        image_ref[parity, :, : 2 * wide] = jnp.dot(table[...], fold_ref[1 - parity], preferred_element_type=jnp.float32)
-
+    total_ref[...] = total / plan.copies + flow_ref[...]
+
+
+def backward_kernel(plan, cos_ref, sin_ref, fold_ref, start_ref, even_ref, odd_ref, grad_ref, image_ref):
+    cells, tiles, wide = plan.cells, plan.tiles, plan.tiles * LANES
+    for parity, table in enumerate((odd_ref, even_ref)):
+        image_ref[parity] = jnp.dot(table[...], fold_ref[1 - parity], preferred_element_type=jnp.float32)
+    lane = lax.broadcasted_iota(jnp.int32, (CHUNK, LANES), 1)
     for row in range(0, cells, CHUNK):
         here = slice(row, row + CHUNK)
         grads = []
         for parity in range(2):
-            grad = grad_ref[parity, here, :]
+            grad = start_ref[parity, here, :]
             for tile in range(tiles):
                 at = tile * LANES
                 grad += cos_ref[parity, here, at : at + LANES] * image_ref[parity, here, at : at + LANES]
                 grad += sin_ref[parity, here, at : at + LANES] * image_ref[parity, here, wide + at : wide + at + LANES]
             grads.append(lane_sum(grad, plan) * 2.0)
-        lane = lax.broadcasted_iota(jnp.int32, (CHUNK, LANES), 1)
-        grad_ref[0, here, :] = jnp.where(lane < width, grads[0], grads[1])
-
-    total = jnp.sum(total, axis=0, keepdims=True) / plan.copies + jnp.sum(flow_ref[...], axis=0, keepdims=True)
-    rows = [total, prev_ref[0:1, :], next_ref[plan.shard - 1 : plan.shard, :]]
+        grad_ref[here, :] = jnp.where(lane < plan.width, grads[0], grads[1])
+
+
+def send_kernel(plan, steps, *refs):
+    half = plan.half
+    totals, (grad_ref, prev_ref, next_ref), outs = refs[:steps], refs[steps : steps + 3], refs[steps + 3 :]
+    me = place_on("mod")
+    total = totals[0][...]
+    for other in totals[1:]:
+        total += other[...]
+    rows = [jnp.sum(total, axis=0, keepdims=True), prev_ref[0:1, :], next_ref[plan.shard - 1 : plan.shard, :]]
     rows += [jnp.zeros((1, LANES), jnp.float32)] * (SUB - len(rows))
     tail = jnp.concatenate(rows, axis=0)
     for k, out in enumerate(outs):
         place = pl.ds(pl.multiple_of((me ^ k) * half, SUB), half)
-        out[0:half, :] = grad_ref[0, place, :]
+        out[0:half, :] = grad_ref[place, :]
         out[half : half + SUB, :] = tail
 
 
@@ -266,11 +332,12 @@
     return (1.0 - ahead_x) * (1.0 - ahead_r), ahead_x * (1.0 - ahead_r), (1.0 - ahead_x) * ahead_r, ahead_x * ahead_r
 
 
-def prior_kernel(plan, total_frames, place_ref, *refs):
+def prior_kernel(plan, steps, *refs):
     mods, shard, frames = plan.mods, plan.shard, plan.frames
-    pieces = refs[: mods - 1]
-    direction_ref, prev_ref, next_ref, codes_ref, prior_ref, flow_ref, coef_ref = refs[mods - 1 :]
-    me, first_frame = place_ref[0], place_ref[1]
+    pieces, refs = refs[: mods - 1], refs[mods - 1 :]
+    direction_ref, first_ref, second_ref, coef_ref, edge_ref, prior_ref, flow_ref, prev_ref, next_ref = refs
+    me, step = place_on("mod"), place_on("tm")
+    first_frame, total_frames = step * frames, steps * frames
     zero_row = jnp.zeros((1, LANES), jnp.float32)
 
     below = [zero_row] * (frames + 2)
@@ -282,6 +349,9 @@
             above[f + 1] = jnp.where(source == me + 1, pieces[k - 1][at : at + 1, :], above[f + 1])
             below[f + 1] = jnp.where(source == me - 1, pieces[k - 1][at + 1 : at + 2, :], below[f + 1])
 
+    even = step % 2 == 0
+    prev_ref[...] = jnp.where(even, second_ref[...], first_ref[...])
+    next_ref[...] = jnp.where(even, first_ref[...], second_ref[...])
     cells = [prev_ref[...]] + [direction_ref[f] for f in range(frames)] + [next_ref[...]]
     row_id = lax.broadcasted_iota(jnp.int32, (shard, LANES), 0)
 
@@ -291,13 +361,14 @@
     def from_last(body, first):
         return jnp.where(row_id == 0, first, pltpu.roll(body, 1, 0))
 
-    begin = pl.multiple_of(me * shard, SUB)
-    coef = shares(codes_ref[pl.ds(begin, shard), :])
-    before = pl.multiple_of(jnp.maximum(begin - SUB, 0), SUB)
-    edge = [jnp.where(me > 0, c[SUB - 1 : SUB], 0.0) for c in shares(codes_ref[pl.ds(before, SUB), :])]
+    coef = [coef_ref[i] for i in range(4)]
+    edge = [edge_ref[i, SUB - 1 : SUB, :] for i in range(4)]
 
     def moved(share, base, ahead):
-        return share[0] * base + share[1] * ahead + share[2] * row_ahead(base) + share[3] * row_ahead(ahead)
+        return share[0] * base + share[1] * ahead + row_ahead_sum(share, base, ahead)
+
+    def row_ahead_sum(share, base, ahead):
+        return share[2] * row_ahead(base) + share[3] * row_ahead(ahead)
 
     flow, flow_edge = [], []
     for t in range(frames + 1):
@@ -321,16 +392,13 @@
         )
         prior_ref[t] = flow[t] - spread_to
     flow_ref[...] = total
-    rows = [coef[1][shard - 1 : shard], coef[3][shard - 1 : shard], edge[1], edge[3]]
-    rows += [zero_row] * (SUB - len(rows))
-    coef_ref[...] = jnp.concatenate(rows, axis=0)
-
-
-def final_kernel(plan, me_ref, *refs):
+
+
+def final_kernel(plan, entries, *refs):
     mods, half, width, shard = plan.mods, plan.half, plan.width, plan.shard
     pieces = refs[:mods]
-    prior_ref, coef_ref, hess_ref, sum_ref = refs[mods : mods + 4]
-    me = me_ref[0]
+    prior_ref, coef_ref, edge_ref, hess_ref, curvature_ref = refs[mods:]
+    me = place_on("mod")
     lane = lax.broadcasted_iota(jnp.int32, (half, LANES), 1)
     for parity in range(2):
         own = pl.ds(parity, half, stride=2)
@@ -349,9 +417,11 @@
         total += piece[half : half + 1, :]
         above = jnp.where(source == me + 1, piece[half + 1 : half + 2, :], above)
         below = jnp.where(source == me - 1, piece[half + 2 : half + 3, :], below)
-    hess_ref[0, shard - 1 : shard, :] -= coef_ref[0:1, :] * above + coef_ref[1:2, :] * row_ahead(above)
-    hess_ref[plan.frames - 1, 0:1, :] -= coef_ref[2:3, :] * below + row_behind(coef_ref[3:4, :] * below)
-    sum_ref[...] = jnp.broadcast_to(total, (SUB, LANES))
+    last = slice(shard - 1, shard)
+    rim = slice(SUB - 1, SUB)
+    hess_ref[0, last, :] -= coef_ref[1, last, :] * above + coef_ref[3, last, :] * row_ahead(above)
+    hess_ref[plan.frames - 1, 0:1, :] -= edge_ref[1, rim, :] * below + row_behind(edge_ref[3, rim, :] * below)
+    curvature_ref[0] = jnp.sum(total) / entries
 
 
 def exchange(arrays, axis):
@@ -365,68 +435,105 @@
     frames, shard, rows = phase.shape
     mods, steps = lax.axis_size("mod"), lax.axis_size("tm")
     plan = Plan(frames, shard, rows, mod_tilts.shape[0], mods)
-    f32 = jnp.float32
-    me = lax.axis_index("mod").astype(jnp.int32).reshape(1)
-    place = jnp.stack([lax.axis_index("mod"), lax.axis_index("tm") * frames]).astype(jnp.int32)
     total_frames = frames * steps
-
-    packed = pl.pallas_call(
+    cells, wide = plan.cells, plan.tiles * LANES
+    tables = [jnp.asarray(t) for t in roof_tables(plan)]
+    phase, direction, pupil_mask, wind_codes, noise_weight, *tables = [
+        pltpu.with_memory_space_constraint(array, pltpu.HBM)
+        for array in (phase, direction, pupil_mask, wind_codes, noise_weight, *tables)
+    ]
+
+    def f32(*shape):
+        return jax.ShapeDtypeStruct(shape, jnp.float32)
+
+    def bf16(*shape):
+        return jax.ShapeDtypeStruct(shape, jnp.bfloat16)
+
+    def scratch(shape):
+        return pltpu.VMEM(shape.shape, shape.dtype)
+
+    def call(kernel, name, outs, in_specs, out_specs=None, scratch_shapes=()):
+        return pl.pallas_call(
+            kernel,
+            out_shape=outs,
+            in_specs=in_specs,
+            out_specs=out_specs or [VMEM] * len(outs),
+            scratch_shapes=list(scratch_shapes),
+            compiler_params=params(),
+            name=name,
+        )
+
+    packed = call(
         functools.partial(pack_kernel, plan),
-        out_shape=[jax.ShapeDtypeStruct((shard + plan.extra, LANES), f32)] * mods,
-        in_specs=[SMEM, SMEM, VMEM, VMEM],
-        out_specs=[VMEM] * mods,
-        compiler_params=params(),
-        name="pack",
-    )(me, mod_tilts, phase, direction)
+        "pack",
+        [f32(shard + plan.extra, LANES)] * mods + [f32(*phase.shape), f32(shard, LANES), f32(shard, LANES)],
+        [HBM] * 3,
+        scratch_shapes=[scratch(phase), pltpu.SMEM(mod_tilts.shape, jnp.int32), pltpu.SemaphoreType.DMA((3,))],
+    )(mod_tilts, phase, direction)
+    packed, (direction_near, first_frame, second_frame) = packed[:mods], packed[mods:]
     pieces = exchange(packed, "mod")
-    prev_frame = lax.ppermute(direction[-1], "tm", [(i, i + 1) for i in range(steps - 1)])
-    next_frame = lax.ppermute(direction[0], "tm", [(i + 1, i) for i in range(steps - 1)])
-
-    prior, flow_total, coef = pl.pallas_call(
-        functools.partial(prior_kernel, plan, total_frames),
-        out_shape=[
-            jax.ShapeDtypeStruct(phase.shape, f32),
-            jax.ShapeDtypeStruct((SUB, LANES), f32),
-            jax.ShapeDtypeStruct((SUB, LANES), f32),
+    first_frame = lax.ppermute(first_frame, "tm", [(i, i ^ 1) for i in range(steps) if i ^ 1 < steps])
+    second_frame = lax.ppermute(
+        second_frame, "tm", [p for i in range(1, steps - 1, 2) for p in ((i, i + 1), (i + 1, i))]
+    )
+
+    prepared = call(
+        functools.partial(prep_kernel, plan),
+        "prepare",
+        [bf16(*t.shape) for t in tables]
+        + [f32(2, cells, LANES), f32(2, 2, cells, LANES), f32(4, shard, LANES), f32(4, SUB, LANES)],
+        [VMEM] + [HBM] * 7,
+        scratch_shapes=[
+            pltpu.VMEM(pupil_mask.shape, jnp.int32),
+            pltpu.VMEM(noise_weight.shape[1:], jnp.float32),
+            pltpu.VMEM((shard + SUB, LANES), jnp.int32),
+            pltpu.SemaphoreType.DMA((8,)),
         ],
-        in_specs=[SMEM] + [VMEM] * (mods + 3),
-        out_specs=[VMEM] * 3,
-        compiler_params=params(),
-        name="prior",
-    )(place, *pieces[1:], direction, prev_frame, next_frame, wind_codes)
-
-    tables = [jnp.asarray(t) for t in roof_tables(plan)]
-    cells, wide = plan.cells, plan.tiles * LANES
-    grads = pl.pallas_call(
-        functools.partial(main_kernel, plan),
-        out_shape=[jax.ShapeDtypeStruct((plan.half + SUB, LANES), f32)] * mods,
-        in_specs=[SMEM] + [VMEM] * (mods + 9),
-        out_specs=[VMEM] * mods,
+    )(packed[0], pupil_mask, noise_weight, wind_codes, *tables)
+    even, odd, even_back, odd_back, mask, noise, coef, edge = prepared
+
+    prior, flow_total, prev_frame, next_frame = call(
+        functools.partial(prior_kernel, plan, steps),
+        "prior",
+        [f32(*phase.shape), f32(SUB, LANES), f32(shard, LANES), f32(shard, LANES)],
+        [VMEM] * (mods + 4),
+    )(*pieces[1:], direction_near, first_frame, second_frame, coef, edge)
+
+    cosine, sine, fold, start, total = call(
+        functools.partial(forward_kernel, plan),
+        "forward",
+        [f32(2, cells, wide), f32(2, cells, wide), bf16(2, 3 * cells, 2 * wide), f32(2, cells, LANES), f32(SUB, LANES)],
+        [VMEM] * (mods + 5),
         scratch_shapes=[
-            pltpu.VMEM((2, cells, LANES), f32),
-            pltpu.VMEM((2, cells, LANES), f32),
-            pltpu.VMEM((2, cells, wide), f32),
-            pltpu.VMEM((2, cells, wide), f32),
-            pltpu.VMEM((2, 3 * cells, 4 * wide), jnp.bfloat16),
-            pltpu.VMEM((2, cells, 4 * wide), f32),
-            pltpu.VMEM((2, 3 * cells, 2 * wide), jnp.bfloat16),
-            pltpu.VMEM((2, cells, LANES), f32),
+            scratch(s)
+            for s in (f32(2, cells, LANES), f32(2, cells, LANES), bf16(2, 3 * cells, 4 * wide), f32(2, cells, 4 * wide))
         ],
-        compiler_params=params(),
-        name="data_term",
-    )(me, *pieces, pupil_mask, noise_weight, *tables, prev_frame, next_frame, flow_total)
-    returned = exchange(grads, "mod")
-
-    hess_vec, mod_total = pl.pallas_call(
-        functools.partial(final_kernel, plan),
-        out_shape=[jax.ShapeDtypeStruct(phase.shape, f32), jax.ShapeDtypeStruct((SUB, LANES), f32)],
-        in_specs=[SMEM] + [VMEM] * (mods + 2),
-        out_specs=[VMEM] * 2,
-        compiler_params=params(),
-        name="join",
-    )(me, *returned, prior, coef)
-    group_total = sum(exchange([mod_total] * steps, "tm"))
-    curvature = (jnp.sum(group_total[0]) / float(total_frames * plan.pupil * rows)).reshape(1)
+    )(*pieces, mask, noise, even, odd, flow_total)
+    totals = exchange([total] * steps, "tm")
+
+    grad = call(
+        functools.partial(backward_kernel, plan),
+        "backward",
+        [f32(cells, LANES)],
+        [VMEM] * 6,
+        scratch_shapes=[scratch(f32(2, cells, 2 * wide))],
+    )(cosine, sine, fold, start, even_back, odd_back)[0]
+
+    sent = call(
+        functools.partial(send_kernel, plan, steps),
+        "send_back",
+        [f32(plan.half + SUB, LANES)] * mods,
+        [VMEM] * (steps + 3),
+    )(*totals, grad, prev_frame, next_frame)
+    returned = exchange(sent, "mod")
+
+    hess_vec, curvature = call(
+        functools.partial(final_kernel, plan, float(total_frames * plan.pupil * rows)),
+        "join",
+        [f32(*phase.shape), f32(1)],
+        [VMEM] * (mods + 3),
+        out_specs=[VMEM, SMEM],
+    )(*returned, prior, coef, edge)
     return hess_vec, curvature
 
 

time: 42.2 us -> 29.7 us (0.70)
  local copies, waits for them, and re-layouts: 7.76 us -> 0 us
  waiting for transfers between devices: 9.74 us -> 6.07 us
  Pallas kernels: 5.09 us -> 8.56 us
  starting transfers between devices: 15.3 us -> 13.5 us
  between operations: 3.17 us -> 1.39 us
  other arithmetic: 0.68 us -> 0 us
    unnamed x18 -> x0, local copies, waits for them, and re-layouts: 6.78 us -> none
    ppermute x2, starting transfers between devices: 6.85 us -> 2.46 us  [the longest x1 1.81 us: per_device(): lax.ppermute(first_frame, 'tm', [(i, i ^ 1) for i in range(steps) if i ^...]
    ppermute x9, waiting for transfers between devices: 9.73 us -> 6.06 us  [exchange(): lax.ppermute(arrays[k], axis, [(i, i ^ k) for i in range(count)])]
    pallas_call x4 -> x7, Pallas kernels: 5.09 us -> 8.56 us  [the longest x1 2.79 us: per_device(): call(functools.partial(forward_kernel, plan), 'forward', [f32(2, cells, w...]
    ppermute x9, starting transfers between devices: 8.45 us -> 11 us  [exchange(): lax.ppermute(arrays[k], axis, [(i, i ^ k) for i in range(count)])]
    squeeze x1 -> x0, local copies, waits for them, and re-layouts: 0.98 us -> none  [per_device(): direction[0]]
    reduce_sum x1 -> x0, other arithmetic: 0.6 us -> none  [per_device(): jnp.sum(group_total[0]) / float(total_frames * plan.pupil * rows)]
  transfers between devices with their start and end apart: 11 -> 11, of which waited for: 7 -> 4; matrix products, arithmetic and copies ran while one was open for 0% -> 0% of each run, Pallas kernels for 0% -> 12%
where the time goes in v2:
time: 29.7 us; the launch traced here: 29.5 us
  starting transfers between devices  13.5 us (45%)
  Pallas kernels  8.56 us (29%)
  waiting for transfers between devices  6.07 us (20%)
  between operations  1.39 us (5%)
    ppermute x9, starting transfers between devices, exchange(): lax.ppermute(arrays[k], axis, [(i, i ^ k) for i in range(count)])  11 us
    ppermute x9, waiting for transfers between devices, exchange(): lax.ppermute(arrays[k], axis, [(i, i ^ k) for i in range(count)])  6.06 us
    pallas_call x1, Pallas kernels, per_device(): call(functools.partial(forward_kernel, plan), 'forward', [f32(2, cells, w...  2.79 us
    pallas_call x1, Pallas kernels, per_device(): call(functools.partial(prep_kernel, plan), 'prepare', [bf16(*t.shape) for...  2.74 us
    ppermute x1, starting transfers between devices, per_device(): lax.ppermute(first_frame, 'tm', [(i, i ^ 1) for i in range(steps) if i ^...  1.81 us
    pallas_call x1, Pallas kernels, per_device(): call(functools.partial(pack_kernel, plan), 'pack', [f32(shard + plan.extr...  1.22 us
    pallas_call x1, Pallas kernels, per_device(): call(functools.partial(final_kernel, plan, float(total_frames * plan.pupi...  0.83 us
    pallas_call x1, Pallas kernels, per_device(): call(functools.partial(backward_kernel, plan), 'backward', [f32(cells, LA...  0.66 us
  transfers between devices with their start and end apart: 11, of which 4 were waited for; matrix products, arithmetic and copies ran while one was open for 0% of the time, Pallas kernels for 12%

profile of v2, /device:TPU:0, one launch (start us, length us, event | category | flops | bytes accessed | tf_op | source)
XLA Modules:
  0.0 29.5 jit_solution(3389184647183112583)
XLA Ops:
  1.3 1.2 %pack.1 = (f32[136,128]{1,0:T(8,128)S(1)}, f32[136,128]{1,0:T(8,128)S(1)}, f32[136,128]{1,0:T(8,128)S(1)}, f32[136,128]{1,0:T(8,128)S(1)}, f32[2,128,128]{2,1,0:...) custom-call(s32[1]{0:T(128)S(6)} %copy.12.tilt_hbm, f32[2,128,128]{2,1,0:T(8,128)} %phase_hbm.1, ...), custom_call_target="tpu_custom_call" | custom-call | tf_op jit(solution)/shard_map/pack/pallas_call | solution.py:466
  2.5 0.5 %collective-permute-start = (f32[136,128]{1,0:T(8,128)S(1)}, f32[136,128]{1,0:T(8,128)S(1)}, u32[]{:S(2)}, u32[]{:S(2)}) collective-permute-start(f32[136,128]{1,0:T(8,128)S(1)} %get-tuple-element.31), channel_id=1, source_target_pairs={{0,1},{1,0},{2,3},{3,2},{4,5},{5,4},{6,7},{7,6},{8,9},{9,8},{10,11... | collective-permute-start | bytes 208904 | tf_op jit(solution)/shard_map/ppermute | solution.py:430
  3.0 2.6 %collective-permute-start.1 = (f32[136,128]{1,0:T(8,128)S(1)}, f32[136,128]{1,0:T(8,128)S(1)}, u32[]{:S(2)}, u32[]{:S(2)}) collective-permute-start(f32[136,128]{1,0:T(8,128)S(1)} %get-tuple-element.32), channel_id=1, source_target_pairs={{0,2},{1,3},{2,0},{3,1},{4,6},{5,7},{6,4},{7,5},{8,10},{9,11},{10,... | collective-permute-start | bytes 208904 | tf_op jit(solution)/shard_map/ppermute | solution.py:430
  5.6 0.1 collective-permute-start.2
  5.7 1.8 %collective-permute-start.3 = (f32[128,128]{1,0:T(8,128)S(1)}, f32[128,128]{1,0:T(8,128)S(1)}, u32[]{:S(2)}, u32[]{:S(2)}) collective-permute-start(f32[128,128]{1,0:T(8,128)S(1)} %get-tuple-element.39), channel_id=1, source_target_pairs={{0,4},{4,0},{8,12},{12,8},{1,5},{5,1},{9,13},{13,9},{2,6},{6,2},{1... | collective-permute-start | bytes 196616 | tf_op jit(solution)/shard_map/ppermute | solution.py:475
  7.5 0.7 %collective-permute-start.4 = (f32[128,128]{1,0:T(8,128)S(1)}, f32[128,128]{1,0:T(8,128)S(1)}, u32[]{:S(2)}, u32[]{:S(2)}) collective-permute-start(f32[128,128]{1,0:T(8,128)S(1)} %get-tuple-element.40), channel_id=1, source_target_pairs={{4,8},{8,4},{5,9},{9,5},{6,10},{10,6},{7,11},{11,7},{20,24},{24,20... | collective-permute-start | bytes 196616 | tf_op jit(solution)/shard_map/ppermute | solution.py:476
  8.1 2.7 %prepare.1 = (bf16[256,768]{1,0:T(8,128)(2,1)S(1)}, bf16[256,768]{1,0:T(8,128)(2,1)S(1)}, bf16[256,768]{1,0:T(8,128)(2,1)S(1)}, bf16[256,768]{1,0:T(8,128)(2,1)S...) custom-call(f32[136,128]{1,0:T(8,128)S(1)} %get-tuple-element.30.see, ...), custom_call_target="tpu_custom_call" | custom-call | tf_op jit(solution)/shard_map/prepare/pallas_call | solution.py:480
  10.9 0.0 collective-permute-done.3.refs_4_
  10.9 0.0 collective-permute-done.4.refs_5_
  10.9 0.0 collective-permute-done.refs_0_.refs_1_
  10.9 0.0 collective-permute-done.1.refs_1_.refs_2_
  10.9 0.0 collective-permute-done.2.refs_2_.refs_3_
  10.9 0.3 %prior.1 = (f32[2,128,128]{2,1,0:T(8,128)S(1)}, f32[8,128]{1,0:T(8,128)S(1)}, f32[128,128]{1,0:T(8,128)S(1)}, f32[128,128]{1,0:T(8,128)S(1)}) custom-call(f32[136,128]{1,0:T(8,128)S(1)} %collective-permute-done.refs_0_.refs_1_, f32[136,128]{1,0:T(8,128)S(1)} %collective-permute-done.1.refs_1_.refs_2_, f32[136,128]{1,0:T(8,128)S(1)} %collective-permute-done.2.refs_2_.refs_3_, ...), custom_call_target="tpu_custom_call" | custom-call | tf_op jit(solution)/shard_map/prior/pallas_call | solution.py:495
  11.2 2.8 %forward.1 = (f32[2,256,256]{2,1,0:T(8,128)S(1)}, f32[2,256,256]{2,1,0:T(8,128)S(1)}, bf16[2,768,512]{2,1,0:T(8,128)(2,1)S(1)}, f32[2,256,128]{2,1,0:T(8,128)S(1)}, f32[8,128]{1,0:T(8,128)S(1)}) custom-call(f32[136,128]{1,0:T(8,128)S(1)} %get-tuple-element.30.seed_ref.refs_0_, f32[136,128]{1,0:T(8,128)S(1)} %collective-permute-done.refs_0_.refs_1_, ...), custom_call_target="tpu_custom_call" | custom-call | tf_op jit(solution)/shard_map/forward/pallas_call | solution.py:502
  14.0 3.0 %collective-permute-start.7 = (f32[8,128]{1,0:T(8,128)S(1)}, f32[8,128]{1,0:T(8,128)S(1)}, u32[]{:S(2)}, u32[]{:S(2)}) collective-permute-start(f32[8,128]{1,0:T(8,128)S(1)} %get-tuple-element.44.refs_0_), channel_id=1, source_target_pairs={{0,12},{4,8},{8,4},{12,0},{1,13},{5,9},{9,5},{13,1},{2,14},{6,10},... | collective-permute-start | bytes 12296 | tf_op jit(solution)/shard_map/ppermute | solution.py:430
  17.0 2.9 %collective-permute-start.6 = (f32[8,128]{1,0:T(8,128)S(1)}, f32[8,128]{1,0:T(8,128)S(1)}, u32[]{:S(2)}, u32[]{:S(2)}) collective-permute-start(f32[8,128]{1,0:T(8,128)S(1)} %get-tuple-element.44.refs_0_), channel_id=1, source_target_pairs={{0,8},{4,12},{8,0},{12,4},{1,9},{5,13},{9,1},{13,5},{2,10},{6,14},... | collective-permute-start | bytes 12296 | tf_op jit(solution)/shard_map/ppermute | solution.py:430
  20.0 0.0 collective-permute-start.5
  20.0 0.7 %backward.1.refs_4_ = f32[256,128]{1,0:T(8,128)S(1)} custom-call(f32[2,256,256]{2,1,0:T(8,128)S(1)} %get-tuple-element.45.cos_ref, f32[2,256,256]{2,1,0:T(8,128)S(1)} %get-tuple-element.46.sin_ref, bf16[2,768,512]{2,1,0:T(8,128)(2,1)S(1)} %get-tuple-element.47.fold_ref, f32[2,256,128]{2,1,0:T(8,128)S(1)} %get-tuple-element.48.start_ref, ...), custom_call_target="tpu_custom_call" | custom-call | tf_op jit(solution)/shard_map/backward/pallas_call | solution.py:514
  20.6 0.0 collective-permute-done.7.refs_3_
  20.6 1.0 %collective-permute-done.6.refs_2_ = f32[8,128]{1,0:T(8,128)S(1)} collective-permute-done((f32[8,128]{1,0:T(8,128)S(1)}, f32[8,128]{1,0:T(8,128)S(1)}, u32[]{:S(2)}, u32[]{:S(2)}) %collective-permute-start.6) | collective-permute-done | bytes 4128 | tf_op jit(solution)/shard_map/ppermute | solution.py:430
  21.6 2.0 %collective-permute-done.5.refs_1_ = f32[8,128]{1,0:T(8,128)S(1)} collective-permute-done((f32[8,128]{1,0:T(8,128)S(1)}, f32[8,128]{1,0:T(8,128)S(1)}, u32[]{:S(2)}, u32[]{:S(2)}) %collective-permute-start.5) | collective-permute-done | bytes 4128 | tf_op jit(solution)/shard_map/ppermute | solution.py:430
  23.6 0.1 collective-permute-start.8
  23.7 1.6 %collective-permute-start.9 = (f32[72,128]{1,0:T(8,128)S(1)}, f32[72,128]{1,0:T(8,128)S(1)}, u32[]{:S(2)}, u32[]{:S(2)}) collective-permute-start(f32[72,128]{1,0:T(8,128)S(1)} %get-tuple-element.55), channel_id=1, source_target_pairs={{0,2},{1,3},{2,0},{3,1},{4,6},{5,7},{6,4},{7,5},{8,10},{9,11},{10,... | collective-permute-start | bytes 110600 | tf_op jit(solution)/shard_map/ppermute | solution.py:430
  25.2 0.3 %collective-permute-start.10 = (f32[72,128]{1,0:T(8,128)S(1)}, f32[72,128]{1,0:T(8,128)S(1)}, u32[]{:S(2)}, u32[]{:S(2)}) collective-permute-start(f32[72,128]{1,0:T(8,128)S(1)} %get-tuple-element.56), channel_id=1, source_target_pairs={{0,3},{1,2},{2,1},{3,0},{4,7},{5,6},{6,5},{7,4},{8,11},{9,10},{10,... | collective-permute-start | bytes 110600 | tf_op jit(solution)/shard_map/ppermute | solution.py:430
  25.5 0.0 collective-permute-done.8.refs_1_
  25.5 2.2 %collective-permute-done.9.refs_2_ = f32[72,128]{1,0:T(8,128)S(1)} collective-permute-done((f32[72,128]{1,0:T(8,128)S(1)}, f32[72,128]{1,0:T(8,128)S(1)}, u32[]{:S(2)}, u32[]{:S(2)}) %collective-permute-start.9) | collective-permute-done | bytes 36896 | tf_op jit(solution)/shard_map/ppermute | solution.py:430
  27.7 1.0 %collective-permute-done.10.refs_3_ = f32[72,128]{1,0:T(8,128)S(1)} collective-permute-done((f32[72,128]{1,0:T(8,128)S(1)}, f32[72,128]{1,0:T(8,128)S(1)}, u32[]{:S(2)}, u32[]{:S(2)}) %collective-permute-start.10) | collective-permute-done | bytes 36896 | tf_op jit(solution)/shard_map/ppermute | solution.py:430
  28.7 0.8 %join.1 = (f32[2,128,128]{2,1,0:T(8,128)}, f32[1]{0:T(128)}) custom-call(f32[72,128]{1,0:T(8,128)S(1)} %get-tuple-element.53.refs_0_, f32[72,128]{1,0:T(8,128)S(1)} %collective-permute-done.8.refs_1_, f32[72,128]{1,0:T(8,128)S(1)} %collective-permute-done.9.refs_2_, f32[72,128]{1,0:T(8,128)S(1)} %collective-permute-done.10.refs_3_, ...), custom_call_target="tpu_custom_call" | custom-call | tf_op jit(solution)/shard_map/join/pallas_call | solution.py:530
  (1 shorter events, 0.0 us)
Async XLA Ops:
  2.5 8.4 %collective-permute-start = (f32[136,128]{1,0:T(8,128)S(1)}, f32[136,128]{1,0:T(8,128)S(1)}, u32[]{:S(2)}, u32[]{:S(2)}) collective-permute-start(f32[136,128]{1,0:T(8,128)S(1)} %get-tuple-element.31), channel_id=1, source_target_pairs={{0,1},{1,0},{2,3},{3,2},{4,5},{5,4},{6,7},{7,6},{8,9},{9,8},{10,11... | collective-permute-start | bytes 208904 | tf_op jit(solution)/shard_map/ppermute | solution.py:430
  3.0 7.9 %collective-permute-start.1 = (f32[136,128]{1,0:T(8,128)S(1)}, f32[136,128]{1,0:T(8,128)S(1)}, u32[]{:S(2)}, u32[]{:S(2)}) collective-permute-start(f32[136,128]{1,0:T(8,128)S(1)} %get-tuple-element.32), channel_id=1, source_target_pairs={{0,2},{1,3},{2,0},{3,1},{4,6},{5,7},{6,4},{7,5},{8,10},{9,11},{10,... | collective-permute-start | bytes 208904 | tf_op jit(solution)/shard_map/ppermute | solution.py:430
  5.6 5.3 %collective-permute-start.2 = (f32[136,128]{1,0:T(8,128)S(1)}, f32[136,128]{1,0:T(8,128)S(1)}, u32[]{:S(2)}, u32[]{:S(2)}) collective-permute-start(f32[136,128]{1,0:T(8,128)S(1)} %get-tuple-element.33), channel_id=1, source_target_pairs={{0,3},{1,2},{2,1},{3,0},{4,7},{5,6},{6,5},{7,4},{8,11},{9,10},{10,... | collective-permute-start | bytes 208904 | tf_op jit(solution)/shard_map/ppermute | solution.py:430
  5.7 5.2 %collective-permute-start.3 = (f32[128,128]{1,0:T(8,128)S(1)}, f32[128,128]{1,0:T(8,128)S(1)}, u32[]{:S(2)}, u32[]{:S(2)}) collective-permute-start(f32[128,128]{1,0:T(8,128)S(1)} %get-tuple-element.39), channel_id=1, source_target_pairs={{0,4},{4,0},{8,12},{12,8},{1,5},{5,1},{9,13},{13,9},{2,6},{6,2},{1... | collective-permute-start | bytes 196616 | tf_op jit(solution)/shard_map/ppermute | solution.py:475
  7.5 3.4 %collective-permute-start.4 = (f32[128,128]{1,0:T(8,128)S(1)}, f32[128,128]{1,0:T(8,128)S(1)}, u32[]{:S(2)}, u32[]{:S(2)}) collective-permute-start(f32[128,128]{1,0:T(8,128)S(1)} %get-tuple-element.40), channel_id=1, source_target_pairs={{4,8},{8,4},{5,9},{9,5},{6,10},{10,6},{7,11},{11,7},{20,24},{24,20... | collective-permute-start | bytes 196616 | tf_op jit(solution)/shard_map/ppermute | solution.py:476
  14.0 6.6 %collective-permute-start.7 = (f32[8,128]{1,0:T(8,128)S(1)}, f32[8,128]{1,0:T(8,128)S(1)}, u32[]{:S(2)}, u32[]{:S(2)}) collective-permute-start(f32[8,128]{1,0:T(8,128)S(1)} %get-tuple-element.44.refs_0_), channel_id=1, source_target_pairs={{0,12},{4,8},{8,4},{12,0},{1,13},{5,9},{9,5},{13,1},{2,14},{6,10},... | collective-permute-start | bytes 12296 | tf_op jit(solution)/shard_map/ppermute | solution.py:430
  17.0 4.6 %collective-permute-start.6 = (f32[8,128]{1,0:T(8,128)S(1)}, f32[8,128]{1,0:T(8,128)S(1)}, u32[]{:S(2)}, u32[]{:S(2)}) collective-permute-start(f32[8,128]{1,0:T(8,128)S(1)} %get-tuple-element.44.refs_0_), channel_id=1, source_target_pairs={{0,8},{4,12},{8,0},{12,4},{1,9},{5,13},{9,1},{13,5},{2,10},{6,14},... | collective-permute-start | bytes 12296 | tf_op jit(solution)/shard_map/ppermute | solution.py:430
  20.0 3.6 %collective-permute-start.5 = (f32[8,128]{1,0:T(8,128)S(1)}, f32[8,128]{1,0:T(8,128)S(1)}, u32[]{:S(2)}, u32[]{:S(2)}) collective-permute-start(f32[8,128]{1,0:T(8,128)S(1)} %get-tuple-element.44.refs_0_), channel_id=1, source_target_pairs={{0,4},{4,0},{8,12},{12,8},{1,5},{5,1},{9,13},{13,9},{2,6},{6,2},{1... | collective-permute-start | bytes 12296 | tf_op jit(solution)/shard_map/ppermute | solution.py:430
  23.6 1.9 %collective-permute-start.8 = (f32[72,128]{1,0:T(8,128)S(1)}, f32[72,128]{1,0:T(8,128)S(1)}, u32[]{:S(2)}, u32[]{:S(2)}) collective-permute-start(f32[72,128]{1,0:T(8,128)S(1)} %get-tuple-element.54), channel_id=1, source_target_pairs={{0,1},{1,0},{2,3},{3,2},{4,5},{5,4},{6,7},{7,6},{8,9},{9,8},{10,11... | collective-permute-start | bytes 110600 | tf_op jit(solution)/shard_map/ppermute | solution.py:430
  23.7 4.0 %collective-permute-start.9 = (f32[72,128]{1,0:T(8,128)S(1)}, f32[72,128]{1,0:T(8,128)S(1)}, u32[]{:S(2)}, u32[]{:S(2)}) collective-permute-start(f32[72,128]{1,0:T(8,128)S(1)} %get-tuple-element.55), channel_id=1, source_target_pairs={{0,2},{1,3},{2,0},{3,1},{4,6},{5,7},{6,4},{7,5},{8,10},{9,11},{10,... | collective-permute-start | bytes 110600 | tf_op jit(solution)/shard_map/ppermute | solution.py:430
  25.2 3.4 %collective-permute-start.10 = (f32[72,128]{1,0:T(8,128)S(1)}, f32[72,128]{1,0:T(8,128)S(1)}, u32[]{:S(2)}, u32[]{:S(2)}) collective-permute-start(f32[72,128]{1,0:T(8,128)S(1)} %get-tuple-element.56), channel_id=1, source_target_pairs={{0,3},{1,2},{2,1},{3,0},{4,7},{5,6},{6,5},{7,4},{8,11},{9,10},{10,... | collective-permute-start | bytes 110600 | tf_op jit(solution)/shard_map/ppermute | solution.py:430

commit v3 on v2

v3 whole, which is shorter than its diff:
```python
import functools

import jax
import jax.numpy as jnp
import ml_dtypes
import numpy as np
from jax import lax
from jax.experimental import pallas as pl
from jax.experimental.pallas import tpu as pltpu
from jax.sharding import PartitionSpec as P

LANES = 128
SUB = 8
CHUNK = 32
VMEM = pl.BlockSpec(memory_space=pltpu.VMEM)
SMEM = pl.BlockSpec(memory_space=pltpu.SMEM)
HBM = pl.BlockSpec(memory_space=pltpu.HBM)


def params():
    return pltpu.CompilerParams(vmem_limit_bytes=48 * 1024 * 1024)


class Plan:
    def __init__(self, frames, shard, rows, points, mods):
        self.frames, self.shard, self.rows, self.mods = frames, shard, rows, mods
        self.points = points
        self.pupil = shard * mods
        self.length = 2 * self.pupil
        assert rows == LANES and mods % frames == 0 and frames % 2 == 0 and mods % 2 == 0
        self.groups = mods // frames
        self.width = rows // self.groups
        assert 2 * self.width <= LANES
        self.copies = LANES // self.width
        self.total_points = points * mods
        assert self.total_points % self.copies == 0
        self.tiles = self.total_points // self.copies
        self.half = shard // 2
        self.cells = self.pupil // 2
        self.extra = -(-(points + 2 * frames) // SUB) * SUB


def roof_tables(plan):
    cells, length = plan.cells, plan.length
    index = np.arange(cells)
    turned = (index + cells // 2) % cells

    def kernel(gap):
        return 2.0 / length / np.cos(2.0 * np.pi * gap / length)

    even = kernel(2 * turned[:, None] - (2 * index[None, :] + 1))
    odd = kernel(2 * turned[:, None] + 1 - 2 * index[None, :])

    def split(table):
        high = table.astype(ml_dtypes.bfloat16)
        low = (table - high.astype(np.float64)).astype(ml_dtypes.bfloat16)
        return np.concatenate([high, high, low], axis=1)

    return split(even), split(odd), split(even.T), split(odd.T)


def spread(cells, plan, first):
    lane = lax.broadcasted_iota(jnp.int32, cells.shape, 1)
    width = plan.width
    if 2 * width == LANES:
        other = pltpu.roll(cells, width, 1)
        keep = (lane < width) if first == 0 else (lane >= width)
        return jnp.where(keep, cells, other)
    if first:
        cells = pltpu.roll(cells, LANES - first, 1)
    cells = jnp.where(lane < width, cells, 0.0)
    step = width
    while step < LANES:
        cells = cells + pltpu.roll(cells, step, 1)
        step *= 2
    return cells


def lane_sum(cells, plan):
    step = plan.width
    while step < LANES:
        cells = cells + pltpu.roll(cells, step, 1)
        step *= 2
    return cells


def place_on(axis):
    return lax.axis_index(axis)


def place_on(axis):
    return lax.axis_index(axis)


def pack_kernel(plan, phase_hbm, direction_hbm, *refs):
    outs = refs[: plan.mods]
    direction_ref, phase_ref, sems = refs[plan.mods :]
    loads = [
        pltpu.make_async_copy(source, target, sems.at[i])
        for i, (source, target) in enumerate(((direction_hbm, direction_ref), (phase_hbm, phase_ref)))
    ]
    for load in loads:
        load.start()
    me = place_on("mod")
    width, half, shard, frames = plan.width, plan.half, plan.shard, plan.frames
    lane = lax.broadcasted_iota(jnp.int32, (half, LANES), 1)
    for load in loads:
        load.wait()
    for k, out in enumerate(outs):
        dest = me ^ k
        frame, group = dest // plan.groups, dest % plan.groups
        back = (LANES - group * width) % LANES
        ahead = (LANES + width - group * width) % LANES
        for parity in range(2):
            own = pl.ds(parity, half, stride=2)
            one = pltpu.roll(phase_ref[frame, own, :], back, 1)
            two = pltpu.roll(direction_ref[frame, own, :], ahead, 1)
            out[parity * half : (parity + 1) * half, :] = jnp.where(lane < width, one, two)
        rows = []
        for f in range(frames):
            rows += [direction_ref[f, 0:1, :], direction_ref[f, shard - 1 : shard, :]]
        rows += [jnp.zeros((1, LANES), jnp.float32)] * (plan.extra - len(rows))
        out[shard : shard + plan.extra, :] = jnp.concatenate(rows, axis=0)
    for f in range(frames):
        start = shard + plan.extra + f * shard
        outs[1][start : start + shard, :] = direction_ref[f]


def relay_kernel(plan, own_ref, piece_ref, after_ref, pair_ref, send_ref):
    shard, frames = plan.shard, plan.frames
    side = place_on("mod") % 2
    for f in range(frames):
        start = shard + plan.extra + f * shard
        pair_ref[f, pl.ds(pl.multiple_of(side * shard, SUB), shard), :] = own_ref[f]
        pair_ref[f, pl.ds(pl.multiple_of((1 - side) * shard, SUB), shard), :] = piece_ref[start : start + shard, :]
    send_ref[...] = pair_ref[side * (frames - 1)]


def label_kernel(plan, tilt_ref, *refs):
    at = plan.shard + 2 * plan.frames
    for out in refs[plan.mods :]:
        out[at : at + plan.points, :] = tilt_ref[...]


def prep_kernel(plan, seed_ref, mask_hbm, noise_hbm, codes_hbm, *refs):
    mask_out, noise_out, coef_out, edge_out, mask_ref, noise_ref, codes_ref, sems = refs
    me = place_on("mod")
    shard, cells, quarter_line = plan.shard, plan.cells, plan.pupil // 2
    frame, group = me // plan.groups, me % plan.groups
    group_back = (LANES - group * plan.width) % LANES
    reach = 2 * shard
    begin = pl.multiple_of((me // 2) * reach, SUB)
    before = pl.multiple_of(jnp.maximum(begin - SUB, 0), SUB)
    pairs = [
        (mask_hbm, mask_ref),
        (noise_hbm.at[frame], noise_ref),
        (codes_hbm.at[pl.ds(before, SUB)], codes_ref.at[0:SUB]),
        (codes_hbm.at[pl.ds(begin, reach)], codes_ref.at[SUB : SUB + reach]),
    ]
    loads = [pltpu.make_async_copy(source, target, sems.at[i]) for i, (source, target) in enumerate(pairs)]
    for load in loads:
        load.start()

    lane_group = lax.broadcasted_iota(jnp.int32, (CHUNK, LANES), 1) // plan.width

    def own_rows(cells_in):
        if plan.copies == 2:
            return jnp.where(lane_group == group, cells_in, pltpu.roll(cells_in, plan.width, 1))
        return spread(pltpu.roll(cells_in, group_back, 1), plan, 0)

    loads[0].wait()
    for parity in range(2):
        for row in range(0, cells, CHUNK):
            picked = mask_ref[pl.ds(2 * row + parity, CHUNK, stride=2), :].astype(jnp.float32)
            mask_out[parity, row : row + CHUNK, :] = own_rows(picked)
    loads[1].wait()
    for parity in range(2):
        for row in range(0, cells, CHUNK):
            low_half = row < cells // 2
            inner = 2 * (row % (cells // 2)) + parity
            for side, block in enumerate((2, 0) if low_half else (1, 3)):
                picked = noise_ref[pl.ds(block * quarter_line + inner, CHUNK, stride=2), :]
                noise_out[side, parity, row : row + CHUNK, :] = own_rows(picked)
    loads[2].wait()
    loads[3].wait()
    for i, share in enumerate(shares(codes_ref[SUB : SUB + reach, :])):
        coef_out[i] = share
    for i, share in enumerate(shares(codes_ref[0:SUB, :])):
        edge_out[i] = jnp.where(me > 1, share, 0.0)


def wave(turns):
    quarters = jnp.round(turns * 4.0)
    angle = (turns - quarters * 0.25) * (2.0 * np.pi)
    square = angle * angle
    sin_part = ((-1.9515295891e-4 * square + 8.3321608736e-3) * square - 1.6666654611e-1) * square * angle + angle
    cos_part = (
        (2.443315711809948e-5 * square - 1.388731625493765e-3) * square + 4.166664568298827e-2
    ) * (square * square) + (1.0 - 0.5 * square)
    count = quarters.astype(jnp.int32)
    odd = (count & 1) != 0
    cosine = jnp.where(odd, sin_part, cos_part)
    sine = jnp.where(odd, cos_part, sin_part)
    cosine = jnp.where(((count + 1) & 2) != 0, -cosine, cosine)
    sine = jnp.where((count & 2) != 0, -sine, sine)
    return cosine, sine


def put_split(ref, row, rows, cells, column, value):
    high = value.astype(jnp.bfloat16)
    low = (value - high.astype(jnp.float32)).astype(jnp.bfloat16)
    where = slice(column, column + LANES)
    ref[row : row + rows, where] = high
    ref[cells + row : cells + row + rows, where] = low
    ref[2 * cells + row : 2 * cells + row + rows, where] = high


def forward_kernel(plan, *refs):
    mods, half, cells = plan.mods, plan.half, plan.cells
    tiles, wide = plan.tiles, plan.tiles * LANES
    pieces = refs[:mods]
    mask_ref, noise_ref = refs[mods : mods + 2]
    tables_hbm = refs[mods + 2 : mods + 6]
    cos_ref, sin_ref, image_ref, weight_ref, total_ref, even_back_ref, odd_back_ref = refs[mods + 6 : mods + 13]
    turn_ref, dir_ref, even_in_ref, odd_in_ref, even_ref, odd_ref, sems = refs[mods + 13 :]
    loads = [
        pltpu.make_async_copy(source, target, sems.at[i])
        for i, (source, target) in enumerate(zip(tables_hbm, (even_ref, odd_ref, even_back_ref, odd_back_ref)))
    ]
    for load in (loads[1], loads[0], loads[2], loads[3]):
        load.start()
    me = place_on("mod")
    lane_row = lax.broadcasted_iota(jnp.int32, (1, LANES), 1)

    for k, piece in enumerate(pieces):
        place = pl.ds(pl.multiple_of((me ^ k) * half, SUB), half)
        for parity in range(2):
            cells_in = piece[parity * half : (parity + 1) * half, :]
            turn_ref[parity, place, :] = spread(cells_in, plan, 0) * (0.5 / np.pi)
            dir_ref[parity, place, :] = spread(cells_in, plan, plan.width)

    tilt_rows = [jnp.zeros((1, LANES), jnp.float32)] * tiles
    for k, piece in enumerate(pieces):
        for p in range(plan.points):
            tile, slot = divmod(k * plan.points + p, plan.copies)
            at = plan.shard + 2 * plan.frames + p
            row = piece[at : at + 1, :]
            tilt_rows[tile] = jnp.where(lane_row // plan.width == slot, row, tilt_rows[tile])

    def tilted(tile, spots):
        tilt = spots.astype(jnp.float32) / plan.length * tilt_rows[tile]
        return wave(tilt - jnp.round(tilt))

    steps = [tilted(tile, jnp.full((1, LANES), 2 * CHUNK, jnp.int32)) for tile in range(tiles)]
    spots = lax.broadcasted_iota(jnp.int32, (CHUNK, LANES), 0) * 2 + plan.pupil // 2

    def fields(parity, ref):
        tilts = [tilted(tile, spots + parity) for tile in range(tiles)]
        for row in range(0, cells, CHUNK):
            here = slice(row, row + CHUNK)
            mask = mask_ref[parity, here, :]
            push = dir_ref[parity, here, :]
            turns = turn_ref[parity, here, :]
            flat_cos, flat_sin = wave(turns)
            flat_cos, flat_sin = flat_cos * mask, flat_sin * mask
            for tile in range(tiles):
                tilt_cos, tilt_sin = tilts[tile]
                cosine = flat_cos * tilt_cos - flat_sin * tilt_sin
                sine = flat_sin * tilt_cos + flat_cos * tilt_sin
                step_cos, step_sin = steps[tile]
                tilts[tile] = (
                    tilt_cos * step_cos - tilt_sin * step_sin,
                    tilt_sin * step_cos + tilt_cos * step_sin,
                )
                at = tile * LANES
                cos_ref[parity, here, at : at + LANES] = cosine
                sin_ref[parity, here, at : at + LANES] = sine
                put_split(ref, row, CHUNK, cells, at, cosine)
                put_split(ref, row, CHUNK, cells, wide + at, sine)
                put_split(ref, row, CHUNK, cells, 2 * wide + at, -sine * push)
                put_split(ref, row, CHUNK, cells, 3 * wide + at, cosine * push)

    def signals(parity, total):
        for row in range(0, cells, CHUNK):
            here = slice(row, row + CHUNK)
            push = dir_ref[parity, here, :]
            even_sum = odd_sum = shift = 0.0
            for tile in range(tiles):
                at = tile * LANES
                cosine = cos_ref[parity, here, at : at + LANES]
                sine = sin_ref[parity, here, at : at + LANES]
                image_cos, image_sin, push_real, push_imag = [
                    image_ref[parity, here, q * wide + at : q * wide + at + LANES] for q in range(4)
                ]
                even_sum += image_sin * push_imag + image_cos * push_real
                odd_sum += cosine * (push_imag - push * image_cos) - sine * (push_real + push * image_sin)
                shift += cosine * image_cos + sine * image_sin
            even_sum = lane_sum(even_sum, plan) * 2.0
            odd_sum = lane_sum(odd_sum, plan)
            signal_after, signal_before = even_sum + odd_sum, even_sum - odd_sum
            weighted_after = noise_ref[0, parity, here, :] * signal_after
            weighted_before = noise_ref[1, parity, here, :] * signal_before
            squares = weighted_after * signal_after + weighted_before * signal_before
            for r in range(0, CHUNK, SUB):
                total += squares[r : r + SUB]
            gap = (weighted_after - weighted_before) * 0.5
            weight_ref[0, parity, here, :] = weighted_after + weighted_before
            weight_ref[1, parity, here, :] = gap
            weight_ref[2, parity, here, :] = -gap * shift
        return total

    def image(parity, table, ref):
        image_ref[parity] = jnp.dot(table[...], ref[...], preferred_element_type=jnp.float32)

    fields(0, even_in_ref)
    fields(1, odd_in_ref)
    loads[1].wait()
    image(1, odd_ref, even_in_ref)
    loads[0].wait()
    image(0, even_ref, odd_in_ref)
    total = signals(1, jnp.zeros((SUB, LANES), jnp.float32))
    total = signals(0, total)
    total_ref[...] = total / plan.copies
    for load in loads[2:]:
        load.wait()


def backward_kernel(plan, *refs):
    cos_ref, sin_ref, image_ref, weight_ref, even_ref, odd_ref, halo_ref, prior_ref = refs[:8]
    outs, (grad_ref, even_in_ref, odd_in_ref, back_ref) = refs[8:-4], refs[-4:]
    half, cells, shard, tiles, wide = plan.half, plan.cells, plan.shard, plan.tiles, plan.tiles * LANES
    me = place_on("mod")

    def fold(parity, ref):
        for row in range(0, cells, CHUNK):
            here = slice(row, row + CHUNK)
            both, gap = weight_ref[0, parity, here, :], weight_ref[1, parity, here, :]
            for tile in range(tiles):
                at = tile * LANES
                cosine = cos_ref[parity, here, at : at + LANES]
                sine = sin_ref[parity, here, at : at + LANES]
                image_cos = image_ref[parity, here, at : at + LANES]
                image_sin = image_ref[parity, here, wide + at : wide + at + LANES]
                put_split(ref, row, CHUNK, cells, at, gap * cosine + both * image_sin)
                put_split(ref, row, CHUNK, cells, wide + at, gap * sine - both * image_cos)

    def back(parity, table, ref):
        back_ref[parity] = jnp.dot(table[...], ref[...], preferred_element_type=jnp.float32)

    fold(0, even_in_ref)
    fold(1, odd_in_ref)
    back(1, even_ref, even_in_ref)
    back(0, odd_ref, odd_in_ref)
    lane = lax.broadcasted_iota(jnp.int32, (CHUNK, LANES), 1)
    for row in range(0, cells, CHUNK):
        here = slice(row, row + CHUNK)
        grads = []
        for parity in range(2):
            grad = weight_ref[2, parity, here, :]
            for tile in range(tiles):
                at = tile * LANES
                grad += cos_ref[parity, here, at : at + LANES] * back_ref[parity, here, at : at + LANES]
                grad += sin_ref[parity, here, at : at + LANES] * back_ref[parity, here, wide + at : wide + at + LANES]
            grads.append(lane_sum(grad, plan) * 2.0)
        grad_ref[here, :] = jnp.where(lane < plan.width, grads[0], grads[1])
    rows = [halo_ref[0:1, :], halo_ref[2 * shard - 1 : 2 * shard, :]]
    rows += [jnp.zeros((1, LANES), jnp.float32)] * (SUB - len(rows))
    tail = jnp.concatenate(rows, axis=0)
    for k, out in enumerate(outs):
        place = pl.ds(pl.multiple_of((me ^ k) * half, SUB), half)
        out[0:half, :] = grad_ref[place, :]
        out[half : half + SUB, :] = tail
    for f in range(plan.frames // 2):
        start = half + SUB + f * shard
        theirs = pl.ds(pl.multiple_of((1 - me % 2) * shard, SUB), shard)
        outs[1][start : start + shard, :] = prior_ref[f, theirs, :]


def seal_kernel(plan, steps, *refs):
    total = refs[0][...]
    for ref in refs[1:steps]:
        total += ref[...]
    for out in refs[steps + plan.mods :]:
        out[plan.half + 2 : plan.half + 3, :] = jnp.sum(total, axis=0, keepdims=True)


def row_ahead(cells):
    lane = lax.broadcasted_iota(jnp.int32, cells.shape, 1)
    return jnp.where(lane == LANES - 1, 0.0, pltpu.roll(cells, LANES - 1, 1))


def row_behind(cells):
    lane = lax.broadcasted_iota(jnp.int32, cells.shape, 1)
    return jnp.where(lane == 0, 0.0, pltpu.roll(cells, 1, 1))


def shares(codes):
    ahead_x = ((codes & 3).astype(jnp.float32) + 0.5) / 4.0
    ahead_r = ((codes >> 2).astype(jnp.float32) + 0.5) / 4.0
    return (1.0 - ahead_x) * (1.0 - ahead_r), ahead_x * (1.0 - ahead_r), (1.0 - ahead_x) * ahead_r, ahead_x * ahead_r


def prior_kernel(plan, steps, *refs):
    mods, shard, frames = plan.mods, plan.shard, plan.frames
    pieces, refs = refs[: mods - 1], refs[mods - 1 :]
    pair_ref, halo_ref, coef_ref, edge_ref, data_ref, prior_ref, total_ref = refs
    me, step = place_on("mod"), place_on("tm")
    side, base, reach, held = me % 2, me - me % 2, 2 * shard, frames // 2
    first_frame, total_frames = step * frames + side * held, steps * frames
    zero_row = jnp.zeros((1, LANES), jnp.float32)

    halo = halo_ref[...]
    cells, below, above = [], [], []
    for t in range(held + 2):
        frame = side * held + t - 1
        inside = (frame >= 0) & (frame < frames)
        cells.append(jnp.where(inside, pair_ref[jnp.clip(frame, 0, frames - 1)], halo))
        low, high = zero_row, zero_row
        for k in range(2, mods):
            source = me ^ k
            for f in range(frames):
                at = shard + 2 * f
                here = frame == f
                high = jnp.where((source == base + 2) & here, pieces[k - 1][at : at + 1, :], high)
                low = jnp.where((source == base - 1) & here, pieces[k - 1][at + 1 : at + 2, :], low)
        below.append(low)
        above.append(high)

    row_id = lax.broadcasted_iota(jnp.int32, (reach, LANES), 0)

    def from_next(body, last):
        return jnp.where(row_id == reach - 1, last, pltpu.roll(body, reach - 1, 0))

    def from_last(body, first):
        return jnp.where(row_id == 0, first, pltpu.roll(body, 1, 0))

    coef = [coef_ref[i] for i in range(4)]
    edge = [edge_ref[i, SUB - 1 : SUB, :] for i in range(4)]

    def moved(share, base, ahead):
        return share[0] * base + share[1] * ahead + share[2] * row_ahead(base) + share[3] * row_ahead(ahead)

    flow, flow_edge = [], []
    for t in range(held + 1):
        frame = first_frame + t - 1
        valid = (frame >= 0) & (frame <= total_frames - 2)
        ahead = from_next(cells[t], above[t])
        flow.append(jnp.where(valid, cells[t + 1] - moved(coef, cells[t], ahead), 0.0))
        if t > 0:
            value = below[t + 1] - moved(edge, below[t], cells[t][0:1])
            flow_edge.append(jnp.where(valid & (me > 1), value, 0.0))
    total = data_ref[...]
    for t in range(held):
        square = flow[t + 1] * flow[t + 1]
        for r in range(0, reach, SUB):
            total += square[r : r + SUB]
        own, rim = flow[t + 1], flow_edge[t]
        spread_to = (
            coef[0] * own
            + from_last(coef[1] * own, edge[1] * rim)
            + row_behind(coef[2] * own + from_last(coef[3] * own, edge[3] * rim))
        )
        prior_ref[t] = flow[t] - spread_to
    total_ref[...] = total


def final_kernel(plan, entries, *refs):
    mods, half, width, shard = plan.mods, plan.half, plan.width, plan.shard
    pieces = refs[:mods]
    prior_ref, coef_ref, edge_ref, hess_ref, curvature_ref = refs[mods:]
    me = place_on("mod")
    side, held = me % 2, plan.frames // 2
    mine = pl.ds(pl.multiple_of(side * shard, SUB), shard)
    for f in range(held):
        start = half + SUB + f * shard
        hess_ref[side * held + f] = prior_ref[f, mine, :]
        hess_ref[(1 - side) * held + f] = pieces[1][start : start + shard, :]
    lane = lax.broadcasted_iota(jnp.int32, (half, LANES), 1)
    for parity in range(2):
        own = pl.ds(parity, half, stride=2)
        for k, piece in enumerate(pieces):
            source = me ^ k
            frame, group = source // plan.groups, source % plan.groups
            turn = (group * width - parity * width + LANES) % LANES
            moved = pltpu.roll(piece[0:half, :], turn, 1)
            hess_ref[frame, own, :] += jnp.where(lane // width == group, moved, 0.0)
    zero_row = jnp.zeros((1, LANES), jnp.float32)
    total, above, below = zero_row, zero_row, zero_row
    for k, piece in enumerate(pieces):
        source = me ^ k
        total += piece[half + 2 : half + 3, :]
        above = jnp.where((source == me + 1) & (side == 1), piece[half : half + 1, :], above)
        below = jnp.where((source == me - 1) & (side == 0), piece[half + 1 : half + 2, :], below)
    last, top, rim = slice(shard - 1, shard), slice(2 * shard - 1, 2 * shard), slice(SUB - 1, SUB)
    hess_ref[0, last, :] -= coef_ref[1, top, :] * above + coef_ref[3, top, :] * row_ahead(above)
    hess_ref[plan.frames - 1, 0:1, :] -= edge_ref[1, rim, :] * below + row_behind(edge_ref[3, rim, :] * below)
    curvature_ref[0] = jnp.sum(total) / entries


def exchange(arrays, axis):
    count = lax.axis_size(axis)
    came = {0: arrays[0]}
    for k in reversed(range(1, count)):
        came[k] = lax.ppermute(arrays[k], axis, [(i, i ^ k) for i in range(count)])
    return [came[k] for k in range(count)]


def per_device(phase, direction, pupil_mask, mod_tilts, wind_codes, noise_weight):
    frames, shard, rows = phase.shape
    mods, steps = lax.axis_size("mod"), lax.axis_size("tm")
    plan = Plan(frames, shard, rows, mod_tilts.shape[0], mods)
    total_frames = frames * steps
    cells, wide = plan.cells, plan.tiles * LANES
    tables = [jnp.asarray(t) for t in roof_tables(plan)]
    phase, direction, pupil_mask, wind_codes, noise_weight, *tables = [
        pltpu.with_memory_space_constraint(array, pltpu.HBM)
        for array in (phase, direction, pupil_mask, wind_codes, noise_weight, *tables)
    ]

    def f32(*shape):
        return jax.ShapeDtypeStruct(shape, jnp.float32)

    def bf16(*shape):
        return jax.ShapeDtypeStruct(shape, jnp.bfloat16)

    def scratch(shape):
        return pltpu.VMEM(shape.shape, shape.dtype)

    def call(kernel, name, outs, in_specs, out_specs=None, scratch_shapes=(), aliases=None, work=0.02):
        return pl.pallas_call(
            kernel,
            out_shape=outs,
            in_specs=in_specs,
            out_specs=out_specs or [VMEM] * len(outs),
            scratch_shapes=list(scratch_shapes),
            input_output_aliases=aliases or {},
            compiler_params=params(),
            cost_estimate=pl.CostEstimate(
                flops=int(work * 1.1e9), bytes_accessed=int(work * 3.6e6), transcendentals=0
            ),
            name=name,
        )

    rows_in = shard + plan.extra
    *packed, direction_near = call(
        functools.partial(pack_kernel, plan),
        "pack",
        [f32(rows_in + (frames * shard if k == 1 else 0), LANES) for k in range(mods)] + [f32(*phase.shape)],
        [HBM] * 2,
        scratch_shapes=[scratch(phase), pltpu.SemaphoreType.DMA((2,))],
        work=1.2,
    )(phase, direction)
    tilts = jnp.broadcast_to(mod_tilts.astype(jnp.float32)[:, None], (plan.points, LANES))
    packed = call(
        functools.partial(label_kernel, plan),
        "label",
        [f32(*p.shape) for p in packed],
        [VMEM] * (mods + 1),
        aliases={k + 1: k for k in range(mods)},
    )(tilts, *packed)
    pieces = exchange(packed, "mod")

    mask, noise, coef, edge = call(
        functools.partial(prep_kernel, plan),
        "prepare",
        [f32(2, cells, LANES), f32(2, 2, cells, LANES), f32(4, 2 * shard, LANES), f32(4, SUB, LANES)],
        [VMEM] + [HBM] * 3,
        scratch_shapes=[
            pltpu.VMEM(pupil_mask.shape, jnp.int32),
            pltpu.VMEM(noise_weight.shape[1:], jnp.float32),
            pltpu.VMEM((2 * shard + SUB, LANES), jnp.int32),
            pltpu.SemaphoreType.DMA((4,)),
        ],
        work=1.5,
    )(packed[0], pupil_mask, noise_weight, wind_codes)

    pair, edge_frame = call(
        functools.partial(relay_kernel, plan),
        "relay",
        [f32(frames, 2 * shard, LANES), f32(2 * shard, LANES)],
        [VMEM] * 3,
        work=0.05,
    )(direction_near, pieces[1], edge)
    ends = [(t * mods + m, (t + 1) * mods + m - 1) for t in range(steps - 1) for m in range(1, mods, 2)]
    halo = lax.ppermute(edge_frame, ("tm", "mod"), ends + [(b, a) for a, b in ends])

    table = bf16(*tables[0].shape)
    cosine, sine, image, weights, data_total, even_back, odd_back = call(
        functools.partial(forward_kernel, plan),
        "forward",
        [f32(2, cells, wide), f32(2, cells, wide), f32(2, cells, 4 * wide), f32(3, 2, cells, LANES), f32(SUB, LANES)]
        + [table] * 2,
        [VMEM] * (mods + 2) + [HBM] * 4,
        scratch_shapes=[
            scratch(s)
            for s in (f32(2, cells, LANES),) * 2 + (bf16(3 * cells, 4 * wide),) * 2 + (table,) * 2
        ]
        + [pltpu.SemaphoreType.DMA((4,))],
        work=2.8,
    )(*pieces, mask, noise, *tables)

    prior, total = call(
        functools.partial(prior_kernel, plan, steps),
        "prior",
        [f32(frames // 2, 2 * shard, LANES), f32(SUB, LANES)],
        [VMEM] * (mods + 4),
        work=0.4,
    )(*pieces[1:], pair, halo, coef, edge, data_total)
    totals = exchange([total] * steps, "tm")

    sent = call(
        functools.partial(backward_kernel, plan),
        "backward",
        [f32(plan.half + SUB + (frames // 2 * shard if k == 1 else 0), LANES) for k in range(mods)],
        [VMEM] * 8,
        scratch_shapes=[
            scratch(s)
            for s in (f32(cells, LANES),) + (bf16(3 * cells, 2 * wide),) * 2 + (f32(2, cells, 2 * wide),)
        ],
        work=0.8,
    )(cosine, sine, image, weights, even_back, odd_back, halo, prior)
    sent = call(
        functools.partial(seal_kernel, plan, steps),
        "seal",
        [f32(*p.shape) for p in sent],
        [VMEM] * (steps + mods),
        aliases={steps + k: k for k in range(mods)},
    )(*reversed(totals), *sent)
    returned = exchange(sent, "mod")

    hess_vec, curvature = call(
        functools.partial(final_kernel, plan, float(total_frames * plan.pupil * rows)),
        "join",
        [f32(*phase.shape), f32(1)],
        [VMEM] * (mods + 3),
        out_specs=[VMEM, SMEM],
        work=0.8,
    )(*returned, prior, coef, edge)
    return hess_vec, curvature


def solution(mesh):
    return jax.shard_map(
        per_device,
        mesh=mesh,
        in_specs=(
            P(("grp", "tm"), "mod", None),
            P(("grp", "tm"), "mod", None),
            P(),
            P("mod"),
            P("grp", None),
            P(("grp", "tm"), None, None),
        ),
        out_specs=(P(("grp", "tm"), "mod", None), P("grp")),
        check_vma=False,
    )
```

time: 29.7 us -> 28.3 us (0.953)
  starting transfers between devices: 13.5 us -> 11.3 us
  waiting for transfers between devices: 6.07 us -> 8.03 us
  Pallas kernels: 8.56 us -> 7.4 us
    ppermute x11 -> x10, starting transfers between devices: 13.5 us -> 11.3 us  [the longest x9 10.7 us: exchange(): came[k] = lax.ppermute(arrays[k], axis, [(i, i ^ k) for i in range(count)])]
    ppermute x11 -> x10, waiting for transfers between devices: 6.07 us -> 8.03 us  [the longest x9 8.02 us: exchange(): came[k] = lax.ppermute(arrays[k], axis, [(i, i ^ k) for i in range(count)])]
    pallas_call x5 -> x7, Pallas kernels: 4.94 us -> 3.91 us  [the longest x1 1.44 us: per_device(): call(functools.partial(prep_kernel, plan), 'prepare', [f32(2, cells, LANE...]
  transfers between devices with their start and end apart: 11 -> 10, of which waited for: 4 -> 6; matrix products, arithmetic and copies ran while one was open for 0% -> 0% of each run, Pallas kernels for 12% -> 18%
where the time goes in v3:
time: 28.3 us; the launch traced here: 28.2 us
  starting transfers between devices  11.3 us (40%)
  waiting for transfers between devices  8.03 us (28%)
  Pallas kernels  7.4 us (26%)
  between operations  1.38 us (5%)
    ppermute x9, starting transfers between devices, exchange(): came[k] = lax.ppermute(arrays[k], axis, [(i, i ^ k) for i in range(count)])  10.7 us
    ppermute x9, waiting for transfers between devices, exchange(): came[k] = lax.ppermute(arrays[k], axis, [(i, i ^ k) for i in range(count)])  8.02 us
    pallas_call x1, Pallas kernels, per_device(): call(functools.partial(forward_kernel, plan), 'forward', [f32(2, cells, w...  2.65 us
    pallas_call x1, Pallas kernels, per_device(): call(functools.partial(prep_kernel, plan), 'prepare', [f32(2, cells, LANE...  1.44 us
    pallas_call x1, Pallas kernels, per_device(): call(functools.partial(pack_kernel, plan), 'pack', [f32(rows_in + (frames...  1.2 us
    pallas_call x1, Pallas kernels, per_device(): call(functools.partial(backward_kernel, plan), 'backward', [f32(plan.half...  0.84 us
    pallas_call x1, Pallas kernels, per_device(): call(functools.partial(final_kernel, plan, float(total_frames * plan.pupi...  0.84 us
    ppermute x1, starting transfers between devices, per_device(): lax.ppermute(edge_frame, ('tm', 'mod'), ends + [(b, a) for a, b in ends])  0.67 us
  transfers between devices with their start and end apart: 10, of which 6 were waited for; matrix products, arithmetic and copies ran while one was open for 0% of the time, Pallas kernels for 18%

profile of v3, /device:TPU:0, one launch (start us, length us, event | category | flops | bytes accessed | tf_op | source)
XLA Modules:
  0.0 28.2 jit_solution(10171955224851140972)
XLA Ops:
  1.3 1.2 %pack.1 = (f32[136,128]{1,0:T(8,128)S(1)}, f32[392,128]{1,0:T(8,128)S(1)}, f32[136,128]{1,0:T(8,128)S(1)}, f32[136,128]{1,0:T(8,128)S(1)}, f32[2,128,128]{2,1,0:T(8,128)S(1)}) custom-call(f32[2,128,128]{2,1,0:T(8,128)} %phase_hbm.1, f32[2,128,128]{2,1,0:T(8,128)} %direction_hbm.1), custom_call_target="tpu_custom_call" | custom-call | flops 1320000000 | bytes 4320000 | tf_op jit(solution)/shard_map/pack/pallas_call | solution.py:545
  2.5 0.5 %collective-permute-start = (f32[392,128]{1,0:T(8,128)S(1)}, f32[392,128]{1,0:T(8,128)S(1)}, u32[]{:S(2)}, u32[]{:S(2)}) collective-permute-start(f32[392,128]{1,0:T(8,128)S(1)} %get-tuple-element.38), channel_id=1, source_target_pairs={{0,1},{1,0},{2,3},{3,2},{4,5},{5,4},{6,7},{7,6},{8,9},{9,8},{10,11... | collective-permute-start | bytes 602120 | tf_op jit(solution)/shard_map/ppermute | solution.py:504
  3.0 2.6 %collective-permute-start.1 = (f32[136,128]{1,0:T(8,128)S(1)}, f32[136,128]{1,0:T(8,128)S(1)}, u32[]{:S(2)}, u32[]{:S(2)}) collective-permute-start(f32[136,128]{1,0:T(8,128)S(1)} %get-tuple-element.39), channel_id=1, source_target_pairs={{0,2},{1,3},{2,0},{3,1},{4,6},{5,7},{6,4},{7,5},{8,10},{9,11},{10,... | collective-permute-start | bytes 208904 | tf_op jit(solution)/shard_map/ppermute | solution.py:504
  5.6 0.1 collective-permute-start.2
  5.7 1.4 %prepare.1 = (f32[2,256,128]{2,1,0:T(8,128)S(1)}, f32[2,2,256,128]{3,2,1,0:T(8,128)S(1)}, f32[4,256,128]{2,1,0:T(8,128)S(1)}, f32[4,8,128]{2,1,0:T(8,128)S(1)}) custom-call(f32[136,128]{1,0:T(8,128)S(1)} %get-tuple-element.42.seed_ref.refs_0_, s32[512,128]{1,0:T(8,128)} %mask_hbm.1, f32[2,1024,128]{2,1,0:T(8,128)} %noise_hbm.1, s32[512,128]{1,0:T(8,128)} %codes_hbm.1), custom_call_target="tpu_custom_call" | custom-call | flops 1650000000 | bytes 5400000 | tf_op jit(solution)/shard_map/prepare/pallas_call | solution.py:563
  7.1 0.0 collective-permute-done.piece_ref.refs_1_.refs_0_
  7.2 0.7 %collective-permute-start.3 = (f32[256,128]{1,0:T(8,128)S(1)}, f32[256,128]{1,0:T(8,128)S(1)}, u32[]{:S(2)}, u32[]{:S(2)}) collective-permute-start(f32[256,128]{1,0:T(8,128)S(1)} %get-tuple-element.45), channel_id=1, source_target_pairs={{1,4},{3,6},{5,8},{7,10},{9,12},{11,14},{4,1},{6,3},{8,5},{10,7},{... | collective-permute-start | bytes 393224 | tf_op jit(solution)/shard_map/ppermute | solution.py:585
  7.8 0.5 %collective-permute-done.1.refs_2_.refs_1_ = f32[136,128]{1,0:T(8,128)S(1)} collective-permute-done((f32[136,128]{1,0:T(8,128)S(1)}, f32[136,128]{1,0:T(8,128)S(1)}, u32[]{:S(2)}, u32[]{:S(2)}) %collective-permute-start.1) | collective-permute-done | bytes 69664 | tf_op jit(solution)/shard_map/ppermute | solution.py:504
  8.4 1.4 %collective-permute-done.2.refs_3_.refs_2_ = f32[136,128]{1,0:T(8,128)S(1)} collective-permute-done((f32[136,128]{1,0:T(8,128)S(1)}, f32[136,128]{1,0:T(8,128)S(1)}, u32[]{:S(2)}, u32[]{:S(2)}) %collective-permute-start.2) | collective-permute-done | bytes 69664 | tf_op jit(solution)/shard_map/ppermute | solution.py:504
  9.7 2.7 %forward.1 = (f32[2,256,256]{2,1,0:T(8,128)S(1)}, f32[2,256,256]{2,1,0:T(8,128)S(1)}, f32[2,256,1024]{2,1,0:T(8,128)S(1)}, f32[3,2,256,128]{3,2,1,0:T(8,128)S(1)...) custom-call(f32[136,128]{1,0:T(8,128)S(1)} %get-tuple-element.42.seed_ref.refs_0_, ...), custom_call_target="tpu_custom_call" | custom-call | flops 3080000000 | bytes 10080000 | tf_op jit(solution)/shard_map/forward/pallas_call | solution.py:588
  12.4 0.0 collective-permute-done.3.refs_4_.refs_6_
  12.4 0.4 %prior.1 = (f32[1,256,128]{2,1,0:T(8,128)S(1)}, f32[8,128]{1,0:T(8,128)S(1)}) custom-call(f32[392,128]{1,0:T(8,128)S(1)} %collective-permute-done.piece_ref.refs_1_.refs_0_, f32[136,128]{1,0:T(8,128)S(1)} %collective-permute-done.1.refs_2_.refs_1_, f32[136,128]{1,0:T(8,128)S(1)} %collective-permute-done.2.refs_3_.refs_2_, ...), custom_call_target="tpu_custom_call" | custom-call | flops 440000000 | bytes 1440000 | tf_op jit(solution)/shard_map/prior/pallas_call | solution.py:602
  12.8 5.0 %collective-permute-start.4 = (f32[8,128]{1,0:T(8,128)S(1)}, f32[8,128]{1,0:T(8,128)S(1)}, u32[]{:S(2)}, u32[]{:S(2)}) collective-permute-start(f32[8,128]{1,0:T(8,128)S(1)} %get-tuple-element.50.refs_3_), channel_id=1, source_target_pairs={{0,12},{4,8},{8,4},{12,0},{1,13},{5,9},{9,5},{13,1},{2,14},{6,10},... | collective-permute-start | bytes 12296 | tf_op jit(solution)/shard_map/ppermute | solution.py:504
  17.7 0.0 collective-permute-start.5
  17.7 0.6 %collective-permute-start.6 = (f32[8,128]{1,0:T(8,128)S(1)}, f32[8,128]{1,0:T(8,128)S(1)}, u32[]{:S(2)}, u32[]{:S(2)}) collective-permute-start(f32[8,128]{1,0:T(8,128)S(1)} %get-tuple-element.50.refs_3_), channel_id=1, source_target_pairs={{0,4},{4,0},{8,12},{12,8},{1,5},{5,1},{9,13},{13,9},{2,6},{6,2},{1... | collective-permute-start | bytes 12296 | tf_op jit(solution)/shard_map/ppermute | solution.py:504
  18.4 0.8 %backward.1 = (f32[72,128]{1,0:T(8,128)S(1)}, f32[200,128]{1,0:T(8,128)S(1)}, f32[72,128]{1,0:T(8,128)S(1)}, f32[72,128]{1,0:T(8,128)S(1)}) custom-call(f32[2,256,256]{2,1,0:T(8,128)S(1)} %get-tuple-element.51.refs_0_, f32[2,256,256]{2,1,0:T(8,128)S(1)} %get-tuple-element.52.refs_1_, f32[2,256,1024]{2,1,0:T(8,128)S(1)} %get-tuple-element.53.refs_2_, ...), custom_call_target="tpu_custom_call" | custom-call | flops 880000000 | bytes 2880000 | tf_op jit(solution)/shard_map/backward/pallas_call | solution.py:611
  19.2 0.1 collective-permute-done.4.refs_0_
  19.3 2.9 %collective-permute-done.5.refs_1_ = f32[8,128]{1,0:T(8,128)S(1)} collective-permute-done((f32[8,128]{1,0:T(8,128)S(1)}, f32[8,128]{1,0:T(8,128)S(1)}, u32[]{:S(2)}, u32[]{:S(2)}) %collective-permute-start.5) | collective-permute-done | bytes 4128 | tf_op jit(solution)/shard_map/ppermute | solution.py:504
  22.2 0.0 collective-permute-done.6.refs_2_
  22.2 0.1 collective-permute-start.7
  22.3 1.6 %collective-permute-start.8 = (f32[72,128]{1,0:T(8,128)S(1)}, f32[72,128]{1,0:T(8,128)S(1)}, u32[]{:S(2)}, u32[]{:S(2)}) collective-permute-start(f32[72,128]{1,0:T(8,128)S(1)} %get-tuple-element.64), channel_id=1, source_target_pairs={{0,2},{1,3},{2,0},{3,1},{4,6},{5,7},{6,4},{7,5},{8,10},{9,11},{10,... | collective-permute-start | bytes 110600 | tf_op jit(solution)/shard_map/ppermute | solution.py:504
  23.9 0.3 %collective-permute-start.9 = (f32[72,128]{1,0:T(8,128)S(1)}, f32[72,128]{1,0:T(8,128)S(1)}, u32[]{:S(2)}, u32[]{:S(2)}) collective-permute-start(f32[72,128]{1,0:T(8,128)S(1)} %get-tuple-element.65), channel_id=1, source_target_pairs={{0,3},{1,2},{2,1},{3,0},{4,7},{5,6},{6,5},{7,4},{8,11},{9,10},{10,... | collective-permute-start | bytes 110600 | tf_op jit(solution)/shard_map/ppermute | solution.py:504
  24.2 2.2 %collective-permute-done.8.refs_2_ = f32[72,128]{1,0:T(8,128)S(1)} collective-permute-done((f32[72,128]{1,0:T(8,128)S(1)}, f32[72,128]{1,0:T(8,128)S(1)}, u32[]{:S(2)}, u32[]{:S(2)}) %collective-permute-start.8) | collective-permute-done | bytes 36896 | tf_op jit(solution)/shard_map/ppermute | solution.py:504
  26.4 1.0 %collective-permute-done.9.refs_3_ = f32[72,128]{1,0:T(8,128)S(1)} collective-permute-done((f32[72,128]{1,0:T(8,128)S(1)}, f32[72,128]{1,0:T(8,128)S(1)}, u32[]{:S(2)}, u32[]{:S(2)}) %collective-permute-start.9) | collective-permute-done | bytes 36896 | tf_op jit(solution)/shard_map/ppermute | solution.py:504
  27.3 0.0 collective-permute-done.7.refs_1_
  27.3 0.8 %join.1 = (f32[2,128,128]{2,1,0:T(8,128)}, f32[1]{0:T(128)}) custom-call(f32[72,128]{1,0:T(8,128)S(1)} %get-tuple-element.62.refs_0_, f32[200,128]{1,0:T(8,128)S(1)} %collective-permute-done.7.refs_1_, f32[72,128]{1,0:T(8,128)S(1)} %collective-permute-done.8.refs_2_, f32[72,128]{1,0:T(8,128)S(1)} %collective-permute-done.9.refs_3_, ...), custom_call_target="tpu_custom_call" | custom-call | flops 880000000 | bytes 2880000 | tf_op jit(solution)/shard_map/join/pallas_call | solution.py:631
  (4 shorter events, 0.1 us)
Async XLA Ops:
  2.5 4.6 %collective-permute-start = (f32[392,128]{1,0:T(8,128)S(1)}, f32[392,128]{1,0:T(8,128)S(1)}, u32[]{:S(2)}, u32[]{:S(2)}) collective-permute-start(f32[392,128]{1,0:T(8,128)S(1)} %get-tuple-element.38), channel_id=1, source_target_pairs={{0,1},{1,0},{2,3},{3,2},{4,5},{5,4},{6,7},{7,6},{8,9},{9,8},{10,11... | collective-permute-start | bytes 602120 | tf_op jit(solution)/shard_map/ppermute | solution.py:504
  3.0 5.3 %collective-permute-start.1 = (f32[136,128]{1,0:T(8,128)S(1)}, f32[136,128]{1,0:T(8,128)S(1)}, u32[]{:S(2)}, u32[]{:S(2)}) collective-permute-start(f32[136,128]{1,0:T(8,128)S(1)} %get-tuple-element.39), channel_id=1, source_target_pairs={{0,2},{1,3},{2,0},{3,1},{4,6},{5,7},{6,4},{7,5},{8,10},{9,11},{10,... | collective-permute-start | bytes 208904 | tf_op jit(solution)/shard_map/ppermute | solution.py:504
  5.6 4.1 %collective-permute-start.2 = (f32[136,128]{1,0:T(8,128)S(1)}, f32[136,128]{1,0:T(8,128)S(1)}, u32[]{:S(2)}, u32[]{:S(2)}) collective-permute-start(f32[136,128]{1,0:T(8,128)S(1)} %get-tuple-element.40), channel_id=1, source_target_pairs={{0,3},{1,2},{2,1},{3,0},{4,7},{5,6},{6,5},{7,4},{8,11},{9,10},{10,... | collective-permute-start | bytes 208904 | tf_op jit(solution)/shard_map/ppermute | solution.py:504
  7.2 5.2 %collective-permute-start.3 = (f32[256,128]{1,0:T(8,128)S(1)}, f32[256,128]{1,0:T(8,128)S(1)}, u32[]{:S(2)}, u32[]{:S(2)}) collective-permute-start(f32[256,128]{1,0:T(8,128)S(1)} %get-tuple-element.45), channel_id=1, source_target_pairs={{1,4},{3,6},{5,8},{7,10},{9,12},{11,14},{4,1},{6,3},{8,5},{10,7},{... | collective-permute-start | bytes 393224 | tf_op jit(solution)/shard_map/ppermute | solution.py:585
  12.8 6.5 %collective-permute-start.4 = (f32[8,128]{1,0:T(8,128)S(1)}, f32[8,128]{1,0:T(8,128)S(1)}, u32[]{:S(2)}, u32[]{:S(2)}) collective-permute-start(f32[8,128]{1,0:T(8,128)S(1)} %get-tuple-element.50.refs_3_), channel_id=1, source_target_pairs={{0,12},{4,8},{8,4},{12,0},{1,13},{5,9},{9,5},{13,1},{2,14},{6,10},... | collective-permute-start | bytes 12296 | tf_op jit(solution)/shard_map/ppermute | solution.py:504
  17.7 4.5 %collective-permute-start.5 = (f32[8,128]{1,0:T(8,128)S(1)}, f32[8,128]{1,0:T(8,128)S(1)}, u32[]{:S(2)}, u32[]{:S(2)}) collective-permute-start(f32[8,128]{1,0:T(8,128)S(1)} %get-tuple-element.50.refs_3_), channel_id=1, source_target_pairs={{0,8},{4,12},{8,0},{12,4},{1,9},{5,13},{9,1},{13,5},{2,10},{6,14},... | collective-permute-start | bytes 12296 | tf_op jit(solution)/shard_map/ppermute | solution.py:504
  17.7 4.5 %collective-permute-start.6 = (f32[8,128]{1,0:T(8,128)S(1)}, f32[8,128]{1,0:T(8,128)S(1)}, u32[]{:S(2)}, u32[]{:S(2)}) collective-permute-start(f32[8,128]{1,0:T(8,128)S(1)} %get-tuple-element.50.refs_3_), channel_id=1, source_target_pairs={{0,4},{4,0},{8,12},{12,8},{1,5},{5,1},{9,13},{13,9},{2,6},{6,2},{1... | collective-permute-start | bytes 12296 | tf_op jit(solution)/shard_map/ppermute | solution.py:504
  22.2 5.1 %collective-permute-start.7 = (f32[200,128]{1,0:T(8,128)S(1)}, f32[200,128]{1,0:T(8,128)S(1)}, u32[]{:S(2)}, u32[]{:S(2)}) collective-permute-start(f32[200,128]{1,0:T(8,128)S(1)} %get-tuple-element.63), channel_id=1, source_target_pairs={{0,1},{1,0},{2,3},{3,2},{4,5},{5,4},{6,7},{7,6},{8,9},{9,8},{10,11... | collective-permute-start | bytes 307208 | tf_op jit(solution)/shard_map/ppermute | solution.py:504
  22.3 4.0 %collective-permute-start.8 = (f32[72,128]{1,0:T(8,128)S(1)}, f32[72,128]{1,0:T(8,128)S(1)}, u32[]{:S(2)}, u32[]{:S(2)}) collective-permute-start(f32[72,128]{1,0:T(8,128)S(1)} %get-tuple-element.64), channel_id=1, source_target_pairs={{0,2},{1,3},{2,0},{3,1},{4,6},{5,7},{6,4},{7,5},{8,10},{9,11},{10,... | collective-permute-start | bytes 110600 | tf_op jit(solution)/shard_map/ppermute | solution.py:504
  23.9 3.4 %collective-permute-start.9 = (f32[72,128]{1,0:T(8,128)S(1)}, f32[72,128]{1,0:T(8,128)S(1)}, u32[]{:S(2)}, u32[]{:S(2)}) collective-permute-start(f32[72,128]{1,0:T(8,128)S(1)} %get-tuple-element.65), channel_id=1, source_target_pairs={{0,3},{1,2},{2,1},{3,0},{4,7},{5,6},{6,5},{7,4},{8,11},{9,10},{10,... | collective-permute-start | bytes 110600 | tf_op jit(solution)/shard_map/ppermute | solution.py:504

commit v4 on v3

--- a/solution.py
+++ b/solution.py
@@ -363,7 +363,9 @@
                 grad += sin_ref[parity, here, at : at + LANES] * back_ref[parity, here, wide + at : wide + at + LANES]
             grads.append(lane_sum(grad, plan) * 2.0)
         grad_ref[here, :] = jnp.where(lane < plan.width, grads[0], grads[1])
-    rows = [halo_ref[0:1, :], halo_ref[2 * shard - 1 : 2 * shard, :]]
+    step, side = place_on("tm"), me % 2
+    alone = jnp.where(side == 0, step == 0, step == lax.axis_size("tm") - 1)
+    rows = [jnp.where(alone, 0.0, r) for r in (halo_ref[0:1, :], halo_ref[2 * shard - 1 : 2 * shard, :])]
     rows += [jnp.zeros((1, LANES), jnp.float32)] * (SUB - len(rows))
     tail = jnp.concatenate(rows, axis=0)
     for k, out in enumerate(outs):
@@ -409,7 +411,8 @@
     first_frame, total_frames = step * frames + side * held, steps * frames
     zero_row = jnp.zeros((1, LANES), jnp.float32)
 
-    halo = halo_ref[...]
+    alone = jnp.where(side == 0, step == 0, step == steps - 1)
+    halo = jnp.where(alone, 0.0, halo_ref[...])
     cells, below, above = [], [], []
     for t in range(held + 2):
         frame = side * held + t - 1
@@ -582,6 +585,7 @@
         work=0.05,
     )(direction_near, pieces[1], edge)
     ends = [(t * mods + m, (t + 1) * mods + m - 1) for t in range(steps - 1) for m in range(1, mods, 2)]
+    ends += [((steps - 1) * mods + m, m - 1) for m in range(1, mods, 2)]
     halo = lax.ppermute(edge_frame, ("tm", "mod"), ends + [(b, a) for a, b in ends])
 
     table = bf16(*tables[0].shape)
@@ -625,7 +629,7 @@
         [f32(*p.shape) for p in sent],
         [VMEM] * (steps + mods),
         aliases={steps + k: k for k in range(mods)},
-    )(*reversed(totals), *sent)
+    )(*totals[2:], *totals[:2], *sent)
     returned = exchange(sent, "mod")
 
     hess_vec, curvature = call(

time: 28.3 us -> 26.9 us (0.951)
  waiting for transfers between devices: 8.03 us -> 5.46 us
  starting transfers between devices: 11.3 us -> 12.5 us
    ppermute x9, waiting for transfers between devices: 8.02 us -> 4.77 us  [exchange(): came[k] = lax.ppermute(arrays[k], axis, [(i, i ^ k) for i in range(count)])]
    ppermute x1, starting transfers between devices: 0.67 us -> 3.85 us  [per_device(): lax.ppermute(edge_frame, ('tm', 'mod'), ends + [(b, a) for a, b in ends])]
    ppermute x9, starting transfers between devices: 10.7 us -> 8.64 us  [exchange(): came[k] = lax.ppermute(arrays[k], axis, [(i, i ^ k) for i in range(count)])]
    ppermute x1, waiting for transfers between devices: 0.01 us -> 0.69 us  [per_device(): lax.ppermute(edge_frame, ('tm', 'mod'), ends + [(b, a) for a, b in ends])]
  transfers between devices with their start and end apart: 10 -> 10, of which waited for: 6 -> 5; matrix products, arithmetic and copies ran while one was open for 0% -> 0% of each run, Pallas kernels for 18% -> 19%
where the time goes in v4:
time: 26.9 us; the launch traced here: 26.7 us
  starting transfers between devices  12.5 us (46%)
  Pallas kernels  7.38 us (27%)
  waiting for transfers between devices  5.46 us (20%)
  between operations  1.37 us (5%)
    ppermute x9, starting transfers between devices, exchange(): came[k] = lax.ppermute(arrays[k], axis, [(i, i ^ k) for i in range(count)])  8.64 us
    ppermute x9, waiting for transfers between devices, exchange(): came[k] = lax.ppermute(arrays[k], axis, [(i, i ^ k) for i in range(count)])  4.77 us
    ppermute x1, starting transfers between devices, per_device(): lax.ppermute(edge_frame, ('tm', 'mod'), ends + [(b, a) for a, b in ends])  3.85 us
    pallas_call x1, Pallas kernels, per_device(): call(functools.partial(forward_kernel, plan), 'forward', [f32(2, cells, w...  2.66 us
    pallas_call x1, Pallas kernels, per_device(): call(functools.partial(prep_kernel, plan), 'prepare', [f32(2, cells, LANE...  1.44 us
    pallas_call x1, Pallas kernels, per_device(): call(functools.partial(pack_kernel, plan), 'pack', [f32(rows_in + (frames...  1.2 us
    pallas_call x1, Pallas kernels, per_device(): call(functools.partial(backward_kernel, plan), 'backward', [f32(plan.half...  0.84 us
    pallas_call x1, Pallas kernels, per_device(): call(functools.partial(final_kernel, plan, float(total_frames * plan.pupi...  0.84 us
  transfers between devices with their start and end apart: 10, of which 5 were waited for; matrix products, arithmetic and copies ran while one was open for 0% of the time, Pallas kernels for 19%

profile of v4, /device:TPU:0, one launch (start us, length us, event | category | flops | bytes accessed | tf_op | source)
XLA Modules:
  0.0 26.7 jit_solution(7117619450820059367)
XLA Ops:
  1.3 1.2 %pack.1 = (f32[136,128]{1,0:T(8,128)S(1)}, f32[392,128]{1,0:T(8,128)S(1)}, f32[136,128]{1,0:T(8,128)S(1)}, f32[136,128]{1,0:T(8,128)S(1)}, f32[2,128,128]{2,1,0:T(8,128)S(1)}) custom-call(f32[2,128,128]{2,1,0:T(8,128)} %phase_hbm.1, f32[2,128,128]{2,1,0:T(8,128)} %direction_hbm.1), custom_call_target="tpu_custom_call" | custom-call | flops 1320000000 | bytes 4320000 | tf_op jit(solution)/shard_map/pack/pallas_call | solution.py:548
  2.5 0.5 %collective-permute-start = (f32[392,128]{1,0:T(8,128)S(1)}, f32[392,128]{1,0:T(8,128)S(1)}, u32[]{:S(2)}, u32[]{:S(2)}) collective-permute-start(f32[392,128]{1,0:T(8,128)S(1)} %get-tuple-element.38), channel_id=1, source_target_pairs={{0,1},{1,0},{2,3},{3,2},{4,5},{5,4},{6,7},{7,6},{8,9},{9,8},{10,11... | collective-permute-start | bytes 602120 | tf_op jit(solution)/shard_map/ppermute | solution.py:507
  3.0 2.6 %collective-permute-start.1 = (f32[136,128]{1,0:T(8,128)S(1)}, f32[136,128]{1,0:T(8,128)S(1)}, u32[]{:S(2)}, u32[]{:S(2)}) collective-permute-start(f32[136,128]{1,0:T(8,128)S(1)} %get-tuple-element.39), channel_id=1, source_target_pairs={{0,2},{1,3},{2,0},{3,1},{4,6},{5,7},{6,4},{7,5},{8,10},{9,11},{10,... | collective-permute-start | bytes 208904 | tf_op jit(solution)/shard_map/ppermute | solution.py:507
  5.6 0.1 collective-permute-start.2
  5.7 1.4 %prepare.1 = (f32[2,256,128]{2,1,0:T(8,128)S(1)}, f32[2,2,256,128]{3,2,1,0:T(8,128)S(1)}, f32[4,256,128]{2,1,0:T(8,128)S(1)}, f32[4,8,128]{2,1,0:T(8,128)S(1)}) custom-call(f32[136,128]{1,0:T(8,128)S(1)} %get-tuple-element.42.seed_ref.refs_0_, s32[512,128]{1,0:T(8,128)} %mask_hbm.1, f32[2,1024,128]{2,1,0:T(8,128)} %noise_hbm.1, s32[512,128]{1,0:T(8,128)} %codes_hbm.1), custom_call_target="tpu_custom_call" | custom-call | flops 1650000000 | bytes 5400000 | tf_op jit(solution)/shard_map/prepare/pallas_call | solution.py:566
  7.1 0.0 collective-permute-done.piece_ref.refs_1_.refs_0_
  7.2 3.9 %collective-permute-start.3 = (f32[256,128]{1,0:T(8,128)S(1)}, f32[256,128]{1,0:T(8,128)S(1)}, u32[]{:S(2)}, u32[]{:S(2)}) collective-permute-start(f32[256,128]{1,0:T(8,128)S(1)} %get-tuple-element.45), channel_id=1, source_target_pairs={{1,4},{3,6},{5,8},{7,10},{9,12},{11,14},{13,0},{15,2},{4,1},{6,3},... | collective-permute-start | bytes 393224 | tf_op jit(solution)/shard_map/ppermute | solution.py:589
  11.0 0.0 collective-permute-done.1.refs_2_.refs_1_
  11.0 0.0 collective-permute-done.2.refs_3_.refs_2_
  11.0 2.7 %forward.1 = (f32[2,256,256]{2,1,0:T(8,128)S(1)}, f32[2,256,256]{2,1,0:T(8,128)S(1)}, f32[2,256,1024]{2,1,0:T(8,128)S(1)}, f32[3,2,256,128]{3,2,1,0:T(8,128)S(1)...) custom-call(f32[136,128]{1,0:T(8,128)S(1)} %get-tuple-element.42.seed_ref.refs_0_, ...), custom_call_target="tpu_custom_call" | custom-call | flops 3080000000 | bytes 10080000 | tf_op jit(solution)/shard_map/forward/pallas_call | solution.py:592
  13.7 0.7 %collective-permute-done.3.refs_4_.refs_6_ = f32[256,128]{1,0:T(8,128)S(1)} collective-permute-done((f32[256,128]{1,0:T(8,128)S(1)}, f32[256,128]{1,0:T(8,128)S(1)}, u32[]{:S(2)}, u32[]{:S(2)}) %collective-permute-start.3) | collective-permute-done | bytes 131104 | tf_op jit(solution)/shard_map/ppermute | solution.py:589
  14.4 0.3 %prior.1 = (f32[1,256,128]{2,1,0:T(8,128)S(1)}, f32[8,128]{1,0:T(8,128)S(1)}) custom-call(f32[392,128]{1,0:T(8,128)S(1)} %collective-permute-done.piece_ref.refs_1_.refs_0_, f32[136,128]{1,0:T(8,128)S(1)} %collective-permute-done.1.refs_2_.refs_1_, f32[136,128]{1,0:T(8,128)S(1)} %collective-permute-done.2.refs_3_.refs_2_, ...), custom_call_target="tpu_custom_call" | custom-call | flops 440000000 | bytes 1440000 | tf_op jit(solution)/shard_map/prior/pallas_call | solution.py:606
  14.7 0.8 %collective-permute-start.4 = (f32[8,128]{1,0:T(8,128)S(1)}, f32[8,128]{1,0:T(8,128)S(1)}, u32[]{:S(2)}, u32[]{:S(2)}) collective-permute-start(f32[8,128]{1,0:T(8,128)S(1)} %get-tuple-element.50.refs_2_), channel_id=1, source_target_pairs={{0,8},{4,12},{8,0},{12,4},{1,9},{5,13},{9,1},{13,5},{2,10},{6,14},... | collective-permute-start | bytes 12296 | tf_op jit(solution)/shard_map/ppermute | solution.py:507
  15.5 1.3 %collective-permute-start.5 = (f32[8,128]{1,0:T(8,128)S(1)}, f32[8,128]{1,0:T(8,128)S(1)}, u32[]{:S(2)}, u32[]{:S(2)}) collective-permute-start(f32[8,128]{1,0:T(8,128)S(1)} %get-tuple-element.50.refs_2_), channel_id=1, source_target_pairs={{0,12},{4,8},{8,4},{12,0},{1,13},{5,9},{9,5},{13,1},{2,14},{6,10},... | collective-permute-start | bytes 12296 | tf_op jit(solution)/shard_map/ppermute | solution.py:507
  16.9 1.4 %collective-permute-start.6 = (f32[8,128]{1,0:T(8,128)S(1)}, f32[8,128]{1,0:T(8,128)S(1)}, u32[]{:S(2)}, u32[]{:S(2)}) collective-permute-start(f32[8,128]{1,0:T(8,128)S(1)} %get-tuple-element.50.refs_2_), channel_id=1, source_target_pairs={{0,4},{4,0},{8,12},{12,8},{1,5},{5,1},{9,13},{13,9},{2,6},{6,2},{1... | collective-permute-start | bytes 12296 | tf_op jit(solution)/shard_map/ppermute | solution.py:507
  18.3 0.8 %backward.1 = (f32[72,128]{1,0:T(8,128)S(1)}, f32[200,128]{1,0:T(8,128)S(1)}, f32[72,128]{1,0:T(8,128)S(1)}, f32[72,128]{1,0:T(8,128)S(1)}) custom-call(f32[2,256,256]{2,1,0:T(8,128)S(1)} %get-tuple-element.51.refs_0_, f32[2,256,256]{2,1,0:T(8,128)S(1)} %get-tuple-element.52.refs_1_, f32[2,256,1024]{2,1,0:T(8,128)S(1)} %get-tuple-element.53.refs_2_, ...), custom_call_target="tpu_custom_call" | custom-call | flops 880000000 | bytes 2880000 | tf_op jit(solution)/shard_map/backward/pallas_call | solution.py:615
  19.1 0.2 collective-permute-done.4.refs_0_
  19.3 1.6 %collective-permute-done.5.refs_1_ = f32[8,128]{1,0:T(8,128)S(1)} collective-permute-done((f32[8,128]{1,0:T(8,128)S(1)}, f32[8,128]{1,0:T(8,128)S(1)}, u32[]{:S(2)}, u32[]{:S(2)}) %collective-permute-start.5) | collective-permute-done | bytes 4128 | tf_op jit(solution)/shard_map/ppermute | solution.py:507
  20.9 0.0 collective-permute-done.6.refs_3_
  21.0 0.1 collective-permute-start.7
  21.0 1.4 %collective-permute-start.8 = (f32[72,128]{1,0:T(8,128)S(1)}, f32[72,128]{1,0:T(8,128)S(1)}, u32[]{:S(2)}, u32[]{:S(2)}) collective-permute-start(f32[72,128]{1,0:T(8,128)S(1)} %get-tuple-element.64), channel_id=1, source_target_pairs={{0,2},{1,3},{2,0},{3,1},{4,6},{5,7},{6,4},{7,5},{8,10},{9,11},{10,... | collective-permute-start | bytes 110600 | tf_op jit(solution)/shard_map/ppermute | solution.py:507
  22.4 0.5 %collective-permute-start.9 = (f32[72,128]{1,0:T(8,128)S(1)}, f32[72,128]{1,0:T(8,128)S(1)}, u32[]{:S(2)}, u32[]{:S(2)}) collective-permute-start(f32[72,128]{1,0:T(8,128)S(1)} %get-tuple-element.65), channel_id=1, source_target_pairs={{0,3},{1,2},{2,1},{3,0},{4,7},{5,6},{6,5},{7,4},{8,11},{9,10},{10,... | collective-permute-start | bytes 110600 | tf_op jit(solution)/shard_map/ppermute | solution.py:507
  22.9 2.2 %collective-permute-done.8.refs_2_ = f32[72,128]{1,0:T(8,128)S(1)} collective-permute-done((f32[72,128]{1,0:T(8,128)S(1)}, f32[72,128]{1,0:T(8,128)S(1)}, u32[]{:S(2)}, u32[]{:S(2)}) %collective-permute-start.8) | collective-permute-done | bytes 36896 | tf_op jit(solution)/shard_map/ppermute | solution.py:507
  25.1 0.8 %collective-permute-done.9.refs_3_ = f32[72,128]{1,0:T(8,128)S(1)} collective-permute-done((f32[72,128]{1,0:T(8,128)S(1)}, f32[72,128]{1,0:T(8,128)S(1)}, u32[]{:S(2)}, u32[]{:S(2)}) %collective-permute-start.9) | collective-permute-done | bytes 36896 | tf_op jit(solution)/shard_map/ppermute | solution.py:507
  25.9 0.0 collective-permute-done.7.refs_1_
  25.9 0.8 %join.1 = (f32[2,128,128]{2,1,0:T(8,128)}, f32[1]{0:T(128)}) custom-call(f32[72,128]{1,0:T(8,128)S(1)} %get-tuple-element.62.refs_0_, f32[200,128]{1,0:T(8,128)S(1)} %collective-permute-done.7.refs_1_, f32[72,128]{1,0:T(8,128)S(1)} %collective-permute-done.8.refs_2_, f32[72,128]{1,0:T(8,128)S(1)} %collective-permute-done.9.refs_3_, ...), custom_call_target="tpu_custom_call" | custom-call | flops 880000000 | bytes 2880000 | tf_op jit(solution)/shard_map/join/pallas_call | solution.py:635
  (4 shorter events, 0.1 us)
Async XLA Ops:
  2.5 4.6 %collective-permute-start = (f32[392,128]{1,0:T(8,128)S(1)}, f32[392,128]{1,0:T(8,128)S(1)}, u32[]{:S(2)}, u32[]{:S(2)}) collective-permute-start(f32[392,128]{1,0:T(8,128)S(1)} %get-tuple-element.38), channel_id=1, source_target_pairs={{0,1},{1,0},{2,3},{3,2},{4,5},{5,4},{6,7},{7,6},{8,9},{9,8},{10,11... | collective-permute-start | bytes 602120 | tf_op jit(solution)/shard_map/ppermute | solution.py:507
  3.0 8.0 %collective-permute-start.1 = (f32[136,128]{1,0:T(8,128)S(1)}, f32[136,128]{1,0:T(8,128)S(1)}, u32[]{:S(2)}, u32[]{:S(2)}) collective-permute-start(f32[136,128]{1,0:T(8,128)S(1)} %get-tuple-element.39), channel_id=1, source_target_pairs={{0,2},{1,3},{2,0},{3,1},{4,6},{5,7},{6,4},{7,5},{8,10},{9,11},{10,... | collective-permute-start | bytes 208904 | tf_op jit(solution)/shard_map/ppermute | solution.py:507
  5.6 5.4 %collective-permute-start.2 = (f32[136,128]{1,0:T(8,128)S(1)}, f32[136,128]{1,0:T(8,128)S(1)}, u32[]{:S(2)}, u32[]{:S(2)}) collective-permute-start(f32[136,128]{1,0:T(8,128)S(1)} %get-tuple-element.40), channel_id=1, source_target_pairs={{0,3},{1,2},{2,1},{3,0},{4,7},{5,6},{6,5},{7,4},{8,11},{9,10},{10,... | collective-permute-start | bytes 208904 | tf_op jit(solution)/shard_map/ppermute | solution.py:507
  7.2 7.2 %collective-permute-start.3 = (f32[256,128]{1,0:T(8,128)S(1)}, f32[256,128]{1,0:T(8,128)S(1)}, u32[]{:S(2)}, u32[]{:S(2)}) collective-permute-start(f32[256,128]{1,0:T(8,128)S(1)} %get-tuple-element.45), channel_id=1, source_target_pairs={{1,4},{3,6},{5,8},{7,10},{9,12},{11,14},{13,0},{15,2},{4,1},{6,3},... | collective-permute-start | bytes 393224 | tf_op jit(solution)/shard_map/ppermute | solution.py:589
  14.7 4.6 %collective-permute-start.4 = (f32[8,128]{1,0:T(8,128)S(1)}, f32[8,128]{1,0:T(8,128)S(1)}, u32[]{:S(2)}, u32[]{:S(2)}) collective-permute-start(f32[8,128]{1,0:T(8,128)S(1)} %get-tuple-element.50.refs_2_), channel_id=1, source_target_pairs={{0,8},{4,12},{8,0},{12,4},{1,9},{5,13},{9,1},{13,5},{2,10},{6,14},... | collective-permute-start | bytes 12296 | tf_op jit(solution)/shard_map/ppermute | solution.py:507
  15.5 5.4 %collective-permute-start.5 = (f32[8,128]{1,0:T(8,128)S(1)}, f32[8,128]{1,0:T(8,128)S(1)}, u32[]{:S(2)}, u32[]{:S(2)}) collective-permute-start(f32[8,128]{1,0:T(8,128)S(1)} %get-tuple-element.50.refs_2_), channel_id=1, source_target_pairs={{0,12},{4,8},{8,4},{12,0},{1,13},{5,9},{9,5},{13,1},{2,14},{6,10},... | collective-permute-start | bytes 12296 | tf_op jit(solution)/shard_map/ppermute | solution.py:507
  16.9 4.1 %collective-permute-start.6 = (f32[8,128]{1,0:T(8,128)S(1)}, f32[8,128]{1,0:T(8,128)S(1)}, u32[]{:S(2)}, u32[]{:S(2)}) collective-permute-start(f32[8,128]{1,0:T(8,128)S(1)} %get-tuple-element.50.refs_2_), channel_id=1, source_target_pairs={{0,4},{4,0},{8,12},{12,8},{1,5},{5,1},{9,13},{13,9},{2,6},{6,2},{1... | collective-permute-start | bytes 12296 | tf_op jit(solution)/shard_map/ppermute | solution.py:507
  21.0 4.9 %collective-permute-start.7 = (f32[200,128]{1,0:T(8,128)S(1)}, f32[200,128]{1,0:T(8,128)S(1)}, u32[]{:S(2)}, u32[]{:S(2)}) collective-permute-start(f32[200,128]{1,0:T(8,128)S(1)} %get-tuple-element.63), channel_id=1, source_target_pairs={{0,1},{1,0},{2,3},{3,2},{4,5},{5,4},{6,7},{7,6},{8,9},{9,8},{10,11... | collective-permute-start | bytes 307208 | tf_op jit(solution)/shard_map/ppermute | solution.py:507
  21.0 4.0 %collective-permute-start.8 = (f32[72,128]{1,0:T(8,128)S(1)}, f32[72,128]{1,0:T(8,128)S(1)}, u32[]{:S(2)}, u32[]{:S(2)}) collective-permute-start(f32[72,128]{1,0:T(8,128)S(1)} %get-tuple-element.64), channel_id=1, source_target_pairs={{0,2},{1,3},{2,0},{3,1},{4,6},{5,7},{6,4},{7,5},{8,10},{9,11},{10,... | collective-permute-start | bytes 110600 | tf_op jit(solution)/shard_map/ppermute | solution.py:507
  22.4 3.4 %collective-permute-start.9 = (f32[72,128]{1,0:T(8,128)S(1)}, f32[72,128]{1,0:T(8,128)S(1)}, u32[]{:S(2)}, u32[]{:S(2)}) collective-permute-start(f32[72,128]{1,0:T(8,128)S(1)} %get-tuple-element.65), channel_id=1, source_target_pairs={{0,3},{1,2},{2,1},{3,0},{4,7},{5,6},{6,5},{7,4},{8,11},{9,10},{10,... | collective-permute-start | bytes 110600 | tf_op jit(solution)/shard_map/ppermute | solution.py:507

commit v5 on v4

--- a/solution.py
+++ b/solution.py
@@ -143,7 +143,8 @@
 
 
 def prep_kernel(plan, seed_ref, mask_hbm, noise_hbm, codes_hbm, *refs):
-    mask_out, noise_out, coef_out, edge_out, mask_ref, noise_ref, codes_ref, sems = refs
+    tables_hbm, refs = refs[:4], refs[4:]
+    mask_out, noise_out, coef_out, edge_out, *tables, mask_ref, noise_ref, codes_ref, sems = refs
     me = place_on("mod")
     shard, cells, quarter_line = plan.shard, plan.cells, plan.pupil // 2
     frame, group = me // plan.groups, me % plan.groups
@@ -156,6 +157,7 @@
         (noise_hbm.at[frame], noise_ref),
         (codes_hbm.at[pl.ds(before, SUB)], codes_ref.at[0:SUB]),
         (codes_hbm.at[pl.ds(begin, reach)], codes_ref.at[SUB : SUB + reach]),
+        *zip(tables_hbm, tables),
     ]
     loads = [pltpu.make_async_copy(source, target, sems.at[i]) for i, (source, target) in enumerate(pairs)]
     for load in loads:
@@ -187,6 +189,8 @@
         coef_out[i] = share
     for i, share in enumerate(shares(codes_ref[0:SUB, :])):
         edge_out[i] = jnp.where(me > 1, share, 0.0)
+    for load in loads[4:]:
+        load.wait()
 
 
 def wave(turns):
@@ -219,16 +223,9 @@
     mods, half, cells = plan.mods, plan.half, plan.cells
     tiles, wide = plan.tiles, plan.tiles * LANES
     pieces = refs[:mods]
-    mask_ref, noise_ref = refs[mods : mods + 2]
-    tables_hbm = refs[mods + 2 : mods + 6]
-    cos_ref, sin_ref, image_ref, weight_ref, total_ref, even_back_ref, odd_back_ref = refs[mods + 6 : mods + 13]
-    turn_ref, dir_ref, even_in_ref, odd_in_ref, even_ref, odd_ref, sems = refs[mods + 13 :]
-    loads = [
-        pltpu.make_async_copy(source, target, sems.at[i])
-        for i, (source, target) in enumerate(zip(tables_hbm, (even_ref, odd_ref, even_back_ref, odd_back_ref)))
-    ]
-    for load in (loads[1], loads[0], loads[2], loads[3]):
-        load.start()
+    mask_ref, noise_ref, even_ref, odd_ref = refs[mods : mods + 4]
+    cos_ref, sin_ref, image_ref, weight_ref, total_ref = refs[mods + 4 : mods + 9]
+    turn_ref, dir_ref, even_in_ref, odd_in_ref = refs[mods + 9 :]
     me = place_on("mod")
     lane_row = lax.broadcasted_iota(jnp.int32, (1, LANES), 1)
 
@@ -314,20 +311,16 @@
 
     fields(0, even_in_ref)
     fields(1, odd_in_ref)
-    loads[1].wait()
     image(1, odd_ref, even_in_ref)
-    loads[0].wait()
     image(0, even_ref, odd_in_ref)
     total = signals(1, jnp.zeros((SUB, LANES), jnp.float32))
     total = signals(0, total)
     total_ref[...] = total / plan.copies
-    for load in loads[2:]:
-        load.wait()
 
 
 def backward_kernel(plan, *refs):
-    cos_ref, sin_ref, image_ref, weight_ref, even_ref, odd_ref, halo_ref, prior_ref = refs[:8]
-    outs, (grad_ref, even_in_ref, odd_in_ref, back_ref) = refs[8:-4], refs[-4:]
+    cos_ref, sin_ref, image_ref, weight_ref, even_ref, odd_ref, halo_ref, flow_ref, rim_ref, coef_ref, edge_ref = refs[:11]
+    outs, prior_ref, (grad_ref, even_in_ref, odd_in_ref, back_ref) = refs[11:-5], refs[-5], refs[-4:]
     half, cells, shard, tiles, wide = plan.half, plan.cells, plan.shard, plan.tiles, plan.tiles * LANES
     me = place_on("mod")
 
@@ -372,10 +365,26 @@
         place = pl.ds(pl.multiple_of((me ^ k) * half, SUB), half)
         out[0:half, :] = grad_ref[place, :]
         out[half : half + SUB, :] = tail
+    prior_terms(plan, flow_ref, rim_ref, coef_ref, edge_ref, prior_ref)
     for f in range(plan.frames // 2):
         start = half + SUB + f * shard
         theirs = pl.ds(pl.multiple_of((1 - me % 2) * shard, SUB), shard)
         outs[1][start : start + shard, :] = prior_ref[f, theirs, :]
+
+
+def prior_terms(plan, flow_ref, rim_ref, coef_ref, edge_ref, prior_ref):
+    reach = 2 * plan.shard
+    row_id = lax.broadcasted_iota(jnp.int32, (reach, LANES), 0)
+
+    def from_last(body, first):
+        return jnp.where(row_id == 0, first, pltpu.roll(body, 1, 0))
+
+    for t in range(plan.frames // 2):
+        own, rim = flow_ref[t + 1], rim_ref[t : t + 1, :]
+        ahead, both = [
+            from_last(coef_ref[i] * own, edge_ref[i, SUB - 1 : SUB, :] * rim) for i in (1, 3)
+        ]
+        prior_ref[t] = flow_ref[t] - (coef_ref[0] * own + ahead + row_behind(coef_ref[2] * own + both))
 
 
 def seal_kernel(plan, steps, *refs):
@@ -405,7 +414,7 @@
 def prior_kernel(plan, steps, *refs):
     mods, shard, frames = plan.mods, plan.shard, plan.frames
     pieces, refs = refs[: mods - 1], refs[mods - 1 :]
-    pair_ref, halo_ref, coef_ref, edge_ref, data_ref, prior_ref, total_ref = refs
+    pair_ref, halo_ref, coef_ref, edge_ref, data_ref, flow_ref, rim_ref, total_ref = refs
     me, step = place_on("mod"), place_on("tm")
     side, base, reach, held = me % 2, me - me % 2, 2 * shard, frames // 2
     first_frame, total_frames = step * frames + side * held, steps * frames
@@ -434,9 +443,6 @@
     def from_next(body, last):
         return jnp.where(row_id == reach - 1, last, pltpu.roll(body, reach - 1, 0))
 
-    def from_last(body, first):
-        return jnp.where(row_id == 0, first, pltpu.roll(body, 1, 0))
-
     coef = [coef_ref[i] for i in range(4)]
     edge = [edge_ref[i, SUB - 1 : SUB, :] for i in range(4)]
 
@@ -457,13 +463,9 @@
         square = flow[t + 1] * flow[t + 1]
         for r in range(0, reach, SUB):
             total += square[r : r + SUB]
-        own, rim = flow[t + 1], flow_edge[t]
-        spread_to = (
-            coef[0] * own
-            + from_last(coef[1] * own, edge[1] * rim)
-            + row_behind(coef[2] * own + from_last(coef[3] * own, edge[3] * rim))
-        )
-        prior_ref[t] = flow[t] - spread_to
+    for t in range(held + 1):
+        flow_ref[t] = flow[t]
+    rim_ref[...] = jnp.concatenate(flow_edge + [zero_row] * (SUB - held), axis=0)
     total_ref[...] = total
 
 
@@ -563,19 +565,21 @@
     )(tilts, *packed)
     pieces = exchange(packed, "mod")
 
-    mask, noise, coef, edge = call(
+    table = bf16(*tables[0].shape)
+    mask, noise, coef, edge, even, odd, even_back, odd_back = call(
         functools.partial(prep_kernel, plan),
         "prepare",
-        [f32(2, cells, LANES), f32(2, 2, cells, LANES), f32(4, 2 * shard, LANES), f32(4, SUB, LANES)],
-        [VMEM] + [HBM] * 3,
+        [f32(2, cells, LANES), f32(2, 2, cells, LANES), f32(4, 2 * shard, LANES), f32(4, SUB, LANES)]
+        + [table] * 4,
+        [VMEM] + [HBM] * 7,
         scratch_shapes=[
             pltpu.VMEM(pupil_mask.shape, jnp.int32),
             pltpu.VMEM(noise_weight.shape[1:], jnp.float32),
             pltpu.VMEM((2 * shard + SUB, LANES), jnp.int32),
-            pltpu.SemaphoreType.DMA((4,)),
+            pltpu.SemaphoreType.DMA((8,)),
         ],
         work=1.5,
-    )(packed[0], pupil_mask, noise_weight, wind_codes)
+    )(packed[0], pupil_mask, noise_weight, wind_codes, *tables)
 
     pair, edge_frame = call(
         functools.partial(relay_kernel, plan),
@@ -588,41 +592,39 @@
     ends += [((steps - 1) * mods + m, m - 1) for m in range(1, mods, 2)]
     halo = lax.ppermute(edge_frame, ("tm", "mod"), ends + [(b, a) for a, b in ends])
 
-    table = bf16(*tables[0].shape)
-    cosine, sine, image, weights, data_total, even_back, odd_back = call(
+    cosine, sine, image, weights, data_total = call(
         functools.partial(forward_kernel, plan),
         "forward",
-        [f32(2, cells, wide), f32(2, cells, wide), f32(2, cells, 4 * wide), f32(3, 2, cells, LANES), f32(SUB, LANES)]
-        + [table] * 2,
-        [VMEM] * (mods + 2) + [HBM] * 4,
+        [f32(2, cells, wide), f32(2, cells, wide), f32(2, cells, 4 * wide), f32(3, 2, cells, LANES), f32(SUB, LANES)],
+        [VMEM] * (mods + 4),
         scratch_shapes=[
             scratch(s)
-            for s in (f32(2, cells, LANES),) * 2 + (bf16(3 * cells, 4 * wide),) * 2 + (table,) * 2
-        ]
-        + [pltpu.SemaphoreType.DMA((4,))],
+            for s in (f32(2, cells, LANES),) * 2 + (bf16(3 * cells, 4 * wide),) * 2
+        ],
         work=2.8,
-    )(*pieces, mask, noise, *tables)
-
-    prior, total = call(
+    )(*pieces, mask, noise, even, odd)
+
+    flow, rim, total = call(
         functools.partial(prior_kernel, plan, steps),
         "prior",
-        [f32(frames // 2, 2 * shard, LANES), f32(SUB, LANES)],
+        [f32(frames // 2 + 1, 2 * shard, LANES), f32(SUB, LANES), f32(SUB, LANES)],
         [VMEM] * (mods + 4),
         work=0.4,
     )(*pieces[1:], pair, halo, coef, edge, data_total)
     totals = exchange([total] * steps, "tm")
 
-    sent = call(
+    *sent, prior = call(
         functools.partial(backward_kernel, plan),
         "backward",
-        [f32(plan.half + SUB + (frames // 2 * shard if k == 1 else 0), LANES) for k in range(mods)],
-        [VMEM] * 8,
+        [f32(plan.half + SUB + (frames // 2 * shard if k == 1 else 0), LANES) for k in range(mods)]
+        + [f32(frames // 2, 2 * shard, LANES)],
+        [VMEM] * 11,
         scratch_shapes=[
             scratch(s)
             for s in (f32(cells, LANES),) + (bf16(3 * cells, 2 * wide),) * 2 + (f32(2, cells, 2 * wide),)
         ],
         work=0.8,
-    )(cosine, sine, image, weights, even_back, odd_back, halo, prior)
+    )(cosine, sine, image, weights, even_back, odd_back, halo, flow, rim, coef, edge)
     sent = call(
         functools.partial(seal_kernel, plan, steps),
         "seal",

time: 26.9 us -> 26.6 us (0.989)
    ppermute x9, waiting for transfers between devices: 4.77 us -> 4.3 us  [exchange(): came[k] = lax.ppermute(arrays[k], axis, [(i, i ^ k) for i in range(count)])]
    ppermute x1, waiting for transfers between devices: 0.69 us -> 1.04 us  [per_device(): lax.ppermute(edge_frame, ('tm', 'mod'), ends + [(b, a) for a, b in ends])]
    pallas_call x1, Pallas kernels: 2.66 us -> 2.3 us  [per_device(): call(functools.partial(forward_kernel, plan), 'forward', [f32(2, cells, w...]
    pallas_call x1, Pallas kernels: 1.44 us -> 1.72 us  [per_device(): call(functools.partial(prep_kernel, plan), 'prepare', [f32(2, cells, LANE...]
where the time goes in v5:
time: 26.6 us; the launch traced here: 26.4 us
  starting transfers between devices  12.5 us (47%)
  Pallas kernels  7.2 us (27%)
  waiting for transfers between devices  5.33 us (20%)
  between operations  1.36 us (5%)
    ppermute x9, starting transfers between devices, exchange(): came[k] = lax.ppermute(arrays[k], axis, [(i, i ^ k) for i in range(count)])  8.66 us
    ppermute x9, waiting for transfers between devices, exchange(): came[k] = lax.ppermute(arrays[k], axis, [(i, i ^ k) for i in range(count)])  4.3 us
    ppermute x1, starting transfers between devices, per_device(): lax.ppermute(edge_frame, ('tm', 'mod'), ends + [(b, a) for a, b in ends])  3.85 us
    pallas_call x1, Pallas kernels, per_device(): call(functools.partial(forward_kernel, plan), 'forward', [f32(2, cells, w...  2.3 us
    pallas_call x1, Pallas kernels, per_device(): call(functools.partial(prep_kernel, plan), 'prepare', [f32(2, cells, LANE...  1.72 us
    pallas_call x1, Pallas kernels, per_device(): call(functools.partial(pack_kernel, plan), 'pack', [f32(rows_in + (frames...  1.2 us
    ppermute x1, waiting for transfers between devices, per_device(): lax.ppermute(edge_frame, ('tm', 'mod'), ends + [(b, a) for a, b in ends])  1.04 us
    pallas_call x1, Pallas kernels, per_device(): call(functools.partial(backward_kernel, plan), 'backward', [f32(plan.half...  0.86 us
  transfers between devices with their start and end apart: 10, of which 5 were waited for; matrix products, arithmetic and copies ran while one was open for 0% of the time, Pallas kernels for 19%

profile of v5, /device:TPU:0, one launch (start us, length us, event | category | flops | bytes accessed | tf_op | source)
XLA Modules:
  0.0 26.4 jit_solution(14204677345495961147)
XLA Ops:
  1.3 1.2 %pack.1 = (f32[136,128]{1,0:T(8,128)S(1)}, f32[392,128]{1,0:T(8,128)S(1)}, f32[136,128]{1,0:T(8,128)S(1)}, f32[136,128]{1,0:T(8,128)S(1)}, f32[2,128,128]{2,1,0:T(8,128)S(1)}) custom-call(f32[2,128,128]{2,1,0:T(8,128)} %phase_hbm.1, f32[2,128,128]{2,1,0:T(8,128)} %direction_hbm.1), custom_call_target="tpu_custom_call" | custom-call | flops 1320000000 | bytes 4320000 | tf_op jit(solution)/shard_map/pack/pallas_call | solution.py:550
  2.5 0.5 %collective-permute-start = (f32[392,128]{1,0:T(8,128)S(1)}, f32[392,128]{1,0:T(8,128)S(1)}, u32[]{:S(2)}, u32[]{:S(2)}) collective-permute-start(f32[392,128]{1,0:T(8,128)S(1)} %get-tuple-element.42), channel_id=1, source_target_pairs={{0,1},{1,0},{2,3},{3,2},{4,5},{5,4},{6,7},{7,6},{8,9},{9,8},{10,11... | collective-permute-start | bytes 602120 | tf_op jit(solution)/shard_map/ppermute | solution.py:509
  3.0 2.6 %collective-permute-start.1 = (f32[136,128]{1,0:T(8,128)S(1)}, f32[136,128]{1,0:T(8,128)S(1)}, u32[]{:S(2)}, u32[]{:S(2)}) collective-permute-start(f32[136,128]{1,0:T(8,128)S(1)} %get-tuple-element.43), channel_id=1, source_target_pairs={{0,2},{1,3},{2,0},{3,1},{4,6},{5,7},{6,4},{7,5},{8,10},{9,11},{10,... | collective-permute-start | bytes 208904 | tf_op jit(solution)/shard_map/ppermute | solution.py:509
  5.6 0.1 collective-permute-start.2
  5.7 1.7 %prepare.1 = (f32[2,256,128]{2,1,0:T(8,128)S(1)}, f32[2,2,256,128]{3,2,1,0:T(8,128)S(1)}, f32[4,256,128]{2,1,0:T(8,128)S(1)}, f32[4,8,128]{2,1,0:T(8,128)S(1)}, ...) custom-call(f32[136,128]{1,0:T(8,128)S(1)} %get-tuple-element.46.see, ...), custom_call_target="tpu_custom_call" | custom-call | flops 1650000000 | bytes 5400000 | tf_op jit(solution)/shard_map/prepare/pallas_call | solution.py:569
  7.4 0.0 collective-permute-done.piece_ref.refs_1_.refs_0_
  7.4 3.9 %collective-permute-start.3 = (f32[256,128]{1,0:T(8,128)S(1)}, f32[256,128]{1,0:T(8,128)S(1)}, u32[]{:S(2)}, u32[]{:S(2)}) collective-permute-start(f32[256,128]{1,0:T(8,128)S(1)} %get-tuple-element.49), channel_id=1, source_target_pairs={{1,4},{3,6},{5,8},{7,10},{9,12},{11,14},{13,0},{15,2},{4,1},{6,3},... | collective-permute-start | bytes 393224 | tf_op jit(solution)/shard_map/ppermute | solution.py:593
  11.3 0.0 collective-permute-done.1.refs_2_.refs_1_
  11.3 0.0 collective-permute-done.2.refs_3_.refs_2_
  11.3 2.3 %forward.1 = (f32[2,256,256]{2,1,0:T(8,128)S(1)}, f32[2,256,256]{2,1,0:T(8,128)S(1)}, f32[2,256,1024]{2,1,0:T(8,128)S(1)}, f32[3,2,256,128]{3,2,1,0:T(8,128)S(1)}, f32[8,128]{1,0:T(8,128)S(1)}) custom-call(f32[136,128]{1,0:T(8,128)S(1)} %get-tuple-element.46.seed_ref.refs_0_, f32[392,128]{1,0:T(8,128)S(1)} %collective-permute-done.piece_ref.refs_1_.refs_0_, ...), custom_call_target="tpu_custom_call" | custom-call | flops 3080000000 | bytes 10080000 | tf_op jit(solution)/shard_map/forward/pallas_call | solution.py:595
  13.6 1.0 %collective-permute-done.3.refs_4_.refs_6_ = f32[256,128]{1,0:T(8,128)S(1)} collective-permute-done((f32[256,128]{1,0:T(8,128)S(1)}, f32[256,128]{1,0:T(8,128)S(1)}, u32[]{:S(2)}, u32[]{:S(2)}) %collective-permute-start.3) | collective-permute-done | bytes 131104 | tf_op jit(solution)/shard_map/ppermute | solution.py:593
  14.7 0.2 prior.1
  14.9 0.2 collective-permute-start.4
  15.1 1.4 %collective-permute-start.5 = (f32[8,128]{1,0:T(8,128)S(1)}, f32[8,128]{1,0:T(8,128)S(1)}, u32[]{:S(2)}, u32[]{:S(2)}) collective-permute-start(f32[8,128]{1,0:T(8,128)S(1)} %get-tuple-element.56.refs_2_), channel_id=1, source_target_pairs={{0,12},{4,8},{8,4},{12,0},{1,13},{5,9},{9,5},{13,1},{2,14},{6,10},... | collective-permute-start | bytes 12296 | tf_op jit(solution)/shard_map/ppermute | solution.py:509
  16.4 2.0 %collective-permute-start.6 = (f32[8,128]{1,0:T(8,128)S(1)}, f32[8,128]{1,0:T(8,128)S(1)}, u32[]{:S(2)}, u32[]{:S(2)}) collective-permute-start(f32[8,128]{1,0:T(8,128)S(1)} %get-tuple-element.56.refs_2_), channel_id=1, source_target_pairs={{0,4},{4,0},{8,12},{12,8},{1,5},{5,1},{9,13},{13,9},{2,6},{6,2},{1... | collective-permute-start | bytes 12296 | tf_op jit(solution)/shard_map/ppermute | solution.py:509
  18.4 0.9 %backward.1 = (f32[72,128]{1,0:T(8,128)S(1)}, f32[200,128]{1,0:T(8,128)S(1)}, f32[72,128]{1,0:T(8,128)S(1)}, f32[72,128]{1,0:T(8,128)S(1)}, f32[1,256,128]{2,1,0:T(8,128)S(1)}) custom-call(f32[2,256,256]{2,1,0:T(8,128)S(1)} %get-tuple-element.57.refs_0_, f32[2,256,256]{2,1,0:T(8,128)S(1)} %get-tuple-element.58.refs_1_, ...), custom_call_target="tpu_custom_call" | custom-call | flops 880000000 | bytes 2880000 | tf_op jit(solution)/shard_map/backward/pallas_call | solution.py:616
  19.3 0.1 collective-permute-done.4.refs_0_
  19.5 1.0 %collective-permute-done.5.refs_1_ = f32[8,128]{1,0:T(8,128)S(1)} collective-permute-done((f32[8,128]{1,0:T(8,128)S(1)}, f32[8,128]{1,0:T(8,128)S(1)}, u32[]{:S(2)}, u32[]{:S(2)}) %collective-permute-start.5) | collective-permute-done | bytes 4128 | tf_op jit(solution)/shard_map/ppermute | solution.py:509
  20.5 0.0 collective-permute-done.6.refs_3_
  20.5 0.2 collective-permute-start.7
  20.7 1.5 %collective-permute-start.8 = (f32[72,128]{1,0:T(8,128)S(1)}, f32[72,128]{1,0:T(8,128)S(1)}, u32[]{:S(2)}, u32[]{:S(2)}) collective-permute-start(f32[72,128]{1,0:T(8,128)S(1)} %get-tuple-element.71), channel_id=1, source_target_pairs={{0,2},{1,3},{2,0},{3,1},{4,6},{5,7},{6,4},{7,5},{8,10},{9,11},{10,... | collective-permute-start | bytes 110600 | tf_op jit(solution)/shard_map/ppermute | solution.py:509
  22.1 0.3 %collective-permute-start.9 = (f32[72,128]{1,0:T(8,128)S(1)}, f32[72,128]{1,0:T(8,128)S(1)}, u32[]{:S(2)}, u32[]{:S(2)}) collective-permute-start(f32[72,128]{1,0:T(8,128)S(1)} %get-tuple-element.72), channel_id=1, source_target_pairs={{0,3},{1,2},{2,1},{3,0},{4,7},{5,6},{6,5},{7,4},{8,11},{9,10},{10,... | collective-permute-start | bytes 110600 | tf_op jit(solution)/shard_map/ppermute | solution.py:509
  22.4 2.2 %collective-permute-done.8.refs_2_ = f32[72,128]{1,0:T(8,128)S(1)} collective-permute-done((f32[72,128]{1,0:T(8,128)S(1)}, f32[72,128]{1,0:T(8,128)S(1)}, u32[]{:S(2)}, u32[]{:S(2)}) %collective-permute-start.8) | collective-permute-done | bytes 36896 | tf_op jit(solution)/shard_map/ppermute | solution.py:509
  24.6 1.0 %collective-permute-done.9.refs_3_ = f32[72,128]{1,0:T(8,128)S(1)} collective-permute-done((f32[72,128]{1,0:T(8,128)S(1)}, f32[72,128]{1,0:T(8,128)S(1)}, u32[]{:S(2)}, u32[]{:S(2)}) %collective-permute-start.9) | collective-permute-done | bytes 36896 | tf_op jit(solution)/shard_map/ppermute | solution.py:509
  25.6 0.0 collective-permute-done.7.refs_1_
  25.6 0.8 %join.1 = (f32[2,128,128]{2,1,0:T(8,128)}, f32[1]{0:T(128)}) custom-call(f32[72,128]{1,0:T(8,128)S(1)} %get-tuple-element.69.refs_0_, f32[200,128]{1,0:T(8,128)S(1)} %collective-permute-done.7.refs_1_, f32[72,128]{1,0:T(8,128)S(1)} %collective-permute-done.8.refs_2_, f32[72,128]{1,0:T(8,128)S(1)} %collective-permute-done.9.refs_3_, ...), custom_call_target="tpu_custom_call" | custom-call | flops 880000000 | bytes 2880000 | tf_op jit(solution)/shard_map/join/pallas_call | solution.py:637
  (4 shorter events, 0.1 us)
Async XLA Ops:
  2.5 4.9 %collective-permute-start = (f32[392,128]{1,0:T(8,128)S(1)}, f32[392,128]{1,0:T(8,128)S(1)}, u32[]{:S(2)}, u32[]{:S(2)}) collective-permute-start(f32[392,128]{1,0:T(8,128)S(1)} %get-tuple-element.42), channel_id=1, source_target_pairs={{0,1},{1,0},{2,3},{3,2},{4,5},{5,4},{6,7},{7,6},{8,9},{9,8},{10,11... | collective-permute-start | bytes 602120 | tf_op jit(solution)/shard_map/ppermute | solution.py:509
  3.0 8.3 %collective-permute-start.1 = (f32[136,128]{1,0:T(8,128)S(1)}, f32[136,128]{1,0:T(8,128)S(1)}, u32[]{:S(2)}, u32[]{:S(2)}) collective-permute-start(f32[136,128]{1,0:T(8,128)S(1)} %get-tuple-element.43), channel_id=1, source_target_pairs={{0,2},{1,3},{2,0},{3,1},{4,6},{5,7},{6,4},{7,5},{8,10},{9,11},{10,... | collective-permute-start | bytes 208904 | tf_op jit(solution)/shard_map/ppermute | solution.py:509
  5.6 5.7 %collective-permute-start.2 = (f32[136,128]{1,0:T(8,128)S(1)}, f32[136,128]{1,0:T(8,128)S(1)}, u32[]{:S(2)}, u32[]{:S(2)}) collective-permute-start(f32[136,128]{1,0:T(8,128)S(1)} %get-tuple-element.44), channel_id=1, source_target_pairs={{0,3},{1,2},{2,1},{3,0},{4,7},{5,6},{6,5},{7,4},{8,11},{9,10},{10,... | collective-permute-start | bytes 208904 | tf_op jit(solution)/shard_map/ppermute | solution.py:509
  7.4 7.2 %collective-permute-start.3 = (f32[256,128]{1,0:T(8,128)S(1)}, f32[256,128]{1,0:T(8,128)S(1)}, u32[]{:S(2)}, u32[]{:S(2)}) collective-permute-start(f32[256,128]{1,0:T(8,128)S(1)} %get-tuple-element.49), channel_id=1, source_target_pairs={{1,4},{3,6},{5,8},{7,10},{9,12},{11,14},{13,0},{15,2},{4,1},{6,3},... | collective-permute-start | bytes 393224 | tf_op jit(solution)/shard_map/ppermute | solution.py:593
  14.9 4.6 %collective-permute-start.4 = (f32[8,128]{1,0:T(8,128)S(1)}, f32[8,128]{1,0:T(8,128)S(1)}, u32[]{:S(2)}, u32[]{:S(2)}) collective-permute-start(f32[8,128]{1,0:T(8,128)S(1)} %get-tuple-element.56.refs_2_), channel_id=1, source_target_pairs={{0,8},{4,12},{8,0},{12,4},{1,9},{5,13},{9,1},{13,5},{2,10},{6,14},... | collective-permute-start | bytes 12296 | tf_op jit(solution)/shard_map/ppermute | solution.py:509
  15.1 5.4 %collective-permute-start.5 = (f32[8,128]{1,0:T(8,128)S(1)}, f32[8,128]{1,0:T(8,128)S(1)}, u32[]{:S(2)}, u32[]{:S(2)}) collective-permute-start(f32[8,128]{1,0:T(8,128)S(1)} %get-tuple-element.56.refs_2_), channel_id=1, source_target_pairs={{0,12},{4,8},{8,4},{12,0},{1,13},{5,9},{9,5},{13,1},{2,14},{6,10},... | collective-permute-start | bytes 12296 | tf_op jit(solution)/shard_map/ppermute | solution.py:509
  16.4 4.1 %collective-permute-start.6 = (f32[8,128]{1,0:T(8,128)S(1)}, f32[8,128]{1,0:T(8,128)S(1)}, u32[]{:S(2)}, u32[]{:S(2)}) collective-permute-start(f32[8,128]{1,0:T(8,128)S(1)} %get-tuple-element.56.refs_2_), channel_id=1, source_target_pairs={{0,4},{4,0},{8,12},{12,8},{1,5},{5,1},{9,13},{13,9},{2,6},{6,2},{1... | collective-permute-start | bytes 12296 | tf_op jit(solution)/shard_map/ppermute | solution.py:509
  20.5 5.1 %collective-permute-start.7 = (f32[200,128]{1,0:T(8,128)S(1)}, f32[200,128]{1,0:T(8,128)S(1)}, u32[]{:S(2)}, u32[]{:S(2)}) collective-permute-start(f32[200,128]{1,0:T(8,128)S(1)} %get-tuple-element.70), channel_id=1, source_target_pairs={{0,1},{1,0},{2,3},{3,2},{4,5},{5,4},{6,7},{7,6},{8,9},{9,8},{10,11... | collective-permute-start | bytes 307208 | tf_op jit(solution)/shard_map/ppermute | solution.py:509
  20.7 4.0 %collective-permute-start.8 = (f32[72,128]{1,0:T(8,128)S(1)}, f32[72,128]{1,0:T(8,128)S(1)}, u32[]{:S(2)}, u32[]{:S(2)}) collective-permute-start(f32[72,128]{1,0:T(8,128)S(1)} %get-tuple-element.71), channel_id=1, source_target_pairs={{0,2},{1,3},{2,0},{3,1},{4,6},{5,7},{6,4},{7,5},{8,10},{9,11},{10,... | collective-permute-start | bytes 110600 | tf_op jit(solution)/shard_map/ppermute | solution.py:509
  22.1 3.4 %collective-permute-start.9 = (f32[72,128]{1,0:T(8,128)S(1)}, f32[72,128]{1,0:T(8,128)S(1)}, u32[]{:S(2)}, u32[]{:S(2)}) collective-permute-start(f32[72,128]{1,0:T(8,128)S(1)} %get-tuple-element.72), channel_id=1, source_target_pairs={{0,3},{1,2},{2,1},{3,0},{4,7},{5,6},{6,5},{7,4},{8,11},{9,10},{10,... | collective-permute-start | bytes 110600 | tf_op jit(solution)/shard_map/ppermute | solution.py:509

commit v6 on v5

--- a/solution.py
+++ b/solution.py
@@ -54,7 +54,7 @@
     def split(table):
         high = table.astype(ml_dtypes.bfloat16)
         low = (table - high.astype(np.float64)).astype(ml_dtypes.bfloat16)
-        return np.concatenate([high, high, low], axis=1)
+        return np.concatenate([high, low], axis=0)
 
     return split(even), split(odd), split(even.T), split(odd.T)
 
@@ -210,13 +210,19 @@
     return cosine, sine
 
 
+def product(table_ref, ref):
+    cells = ref.shape[0] // 2
+    first = jnp.dot(table_ref[...], ref[:cells], preferred_element_type=jnp.float32)
+    second = jnp.dot(table_ref[:cells], ref[cells:], preferred_element_type=jnp.float32)
+    return first[:cells] + first[cells:] + second
+
+
 def put_split(ref, row, rows, cells, column, value):
     high = value.astype(jnp.bfloat16)
     low = (value - high.astype(jnp.float32)).astype(jnp.bfloat16)
     where = slice(column, column + LANES)
     ref[row : row + rows, where] = high
     ref[cells + row : cells + row + rows, where] = low
-    ref[2 * cells + row : 2 * cells + row + rows, where] = high
 
 
 def forward_kernel(plan, *refs):
@@ -307,7 +313,7 @@
         return total
 
     def image(parity, table, ref):
-        image_ref[parity] = jnp.dot(table[...], ref[...], preferred_element_type=jnp.float32)
+        image_ref[parity] = product(table, ref)
 
     fields(0, even_in_ref)
     fields(1, odd_in_ref)
@@ -338,7 +344,7 @@
                 put_split(ref, row, CHUNK, cells, wide + at, gap * sine - both * image_cos)
 
     def back(parity, table, ref):
-        back_ref[parity] = jnp.dot(table[...], ref[...], preferred_element_type=jnp.float32)
+        back_ref[parity] = product(table, ref)
 
     fold(0, even_in_ref)
     fold(1, odd_in_ref)
@@ -361,15 +367,21 @@
     rows = [jnp.where(alone, 0.0, r) for r in (halo_ref[0:1, :], halo_ref[2 * shard - 1 : 2 * shard, :])]
     rows += [jnp.zeros((1, LANES), jnp.float32)] * (SUB - len(rows))
     tail = jnp.concatenate(rows, axis=0)
-    for k, out in enumerate(outs):
+    def put(out, at, k):
         place = pl.ds(pl.multiple_of((me ^ k) * half, SUB), half)
-        out[0:half, :] = grad_ref[place, :]
-        out[half : half + SUB, :] = tail
+        out[at : at + half, :] = grad_ref[place, :]
+        out[at + half : at + half + SUB, :] = tail
+
+    *even_outs, near_out = outs
+    for k in range(0, plan.mods, 2):
+        put(even_outs[k // 2], 0, k)
+    for k in range(1, plan.mods, 2):
+        put(near_out, (k // 2) * (half + SUB), k)
     prior_terms(plan, flow_ref, rim_ref, coef_ref, edge_ref, prior_ref)
+    theirs = pl.ds(pl.multiple_of((1 - me % 2) * shard, SUB), shard)
     for f in range(plan.frames // 2):
-        start = half + SUB + f * shard
-        theirs = pl.ds(pl.multiple_of((1 - me % 2) * shard, SUB), shard)
-        outs[1][start : start + shard, :] = prior_ref[f, theirs, :]
+        start = plan.mods // 2 * (half + SUB) + f * shard
+        near_out[start : start + shard, :] = prior_ref[f, theirs, :]
 
 
 def prior_terms(plan, flow_ref, rim_ref, coef_ref, edge_ref, prior_ref):
@@ -387,12 +399,20 @@
         prior_ref[t] = flow_ref[t] - (coef_ref[0] * own + ahead + row_behind(coef_ref[2] * own + both))
 
 
-def seal_kernel(plan, steps, *refs):
+def sum_kernel(*refs):
     total = refs[0][...]
-    for ref in refs[1:steps]:
+    for ref in refs[1:-1]:
         total += ref[...]
-    for out in refs[steps + plan.mods :]:
-        out[plan.half + 2 : plan.half + 3, :] = jnp.sum(total, axis=0, keepdims=True)
+    refs[-1][...] = jnp.broadcast_to(jnp.sum(total, axis=0, keepdims=True), total.shape)
+
+
+def seal_kernel(plan, total_ref, *refs):
+    size, count = plan.half + SUB, plan.mods // 2 - 1
+    own, near_ref, outs = refs[:count], refs[count], refs[count + 1 :]
+    for i, out in enumerate(outs):
+        out[0:size, :] = own[i][...]
+        out[plan.half + 2 : plan.half + 3, :] = total_ref[0:1, :]
+        out[size : 2 * size, :] = near_ref[(i + 1) * size : (i + 2) * size, :]
 
 
 def row_ahead(cells):
@@ -471,31 +491,39 @@
 
 def final_kernel(plan, entries, *refs):
     mods, half, width, shard = plan.mods, plan.half, plan.width, plan.shard
-    pieces = refs[:mods]
-    prior_ref, coef_ref, edge_ref, hess_ref, curvature_ref = refs[mods:]
+    size, pairs = half + SUB, plan.mods // 2
+    own_ref, near_ref, far = refs[0], refs[1], refs[2 : pairs + 1]
+    sums, refs = refs[pairs + 1 : 2 * pairs + 2], refs[2 * pairs + 2 :]
+    prior_ref, coef_ref, edge_ref, hess_ref, curvature_ref = refs
+    pieces = [(own_ref, 0), (near_ref, 0)]
+    for ref in far:
+        pieces += [(ref, 0), (ref, size)]
     me = place_on("mod")
     side, held = me % 2, plan.frames // 2
     mine = pl.ds(pl.multiple_of(side * shard, SUB), shard)
     for f in range(held):
-        start = half + SUB + f * shard
+        start = pairs * size + f * shard
         hess_ref[side * held + f] = prior_ref[f, mine, :]
-        hess_ref[(1 - side) * held + f] = pieces[1][start : start + shard, :]
+        hess_ref[(1 - side) * held + f] = near_ref[start : start + shard, :]
     lane = lax.broadcasted_iota(jnp.int32, (half, LANES), 1)
     for parity in range(2):
         own = pl.ds(parity, half, stride=2)
-        for k, piece in enumerate(pieces):
+        for k, (piece, at) in enumerate(pieces):
             source = me ^ k
             frame, group = source // plan.groups, source % plan.groups
             turn = (group * width - parity * width + LANES) % LANES
-            moved = pltpu.roll(piece[0:half, :], turn, 1)
+            moved = pltpu.roll(piece[at : at + half, :], turn, 1)
             hess_ref[frame, own, :] += jnp.where(lane // width == group, moved, 0.0)
     zero_row = jnp.zeros((1, LANES), jnp.float32)
     total, above, below = zero_row, zero_row, zero_row
-    for k, piece in enumerate(pieces):
-        source = me ^ k
-        total += piece[half + 2 : half + 3, :]
-        above = jnp.where((source == me + 1) & (side == 1), piece[half : half + 1, :], above)
-        below = jnp.where((source == me - 1) & (side == 0), piece[half + 1 : half + 2, :], below)
+    for ref in sums:
+        total += ref[0:1, :]
+    for ref in far:
+        total += ref[half + 2 : half + 3, :]
+    for k, (piece, at) in enumerate(pieces):
+        source, at = me ^ k, at + half
+        above = jnp.where((source == me + 1) & (side == 1), piece[at : at + 1, :], above)
+        below = jnp.where((source == me - 1) & (side == 0), piece[at + 1 : at + 2, :], below)
     last, top, rim = slice(shard - 1, shard), slice(2 * shard - 1, 2 * shard), slice(SUB - 1, SUB)
     hess_ref[0, last, :] -= coef_ref[1, top, :] * above + coef_ref[3, top, :] * row_ahead(above)
     hess_ref[plan.frames - 1, 0:1, :] -= edge_ref[1, rim, :] * below + row_behind(edge_ref[3, rim, :] * below)
@@ -504,10 +532,9 @@
 
 def exchange(arrays, axis):
     count = lax.axis_size(axis)
-    came = {0: arrays[0]}
-    for k in reversed(range(1, count)):
-        came[k] = lax.ppermute(arrays[k], axis, [(i, i ^ k) for i in range(count)])
-    return [came[k] for k in range(count)]
+    return [arrays[0]] + [
+        lax.ppermute(arrays[k], axis, [(i, i ^ k) for i in range(count)]) for k in range(1, count)
+    ]
 
 
 def per_device(phase, direction, pupil_mask, mod_tilts, wind_codes, noise_weight):
@@ -589,7 +616,11 @@
         work=0.05,
     )(direction_near, pieces[1], edge)
     ends = [(t * mods + m, (t + 1) * mods + m - 1) for t in range(steps - 1) for m in range(1, mods, 2)]
-    ends += [((steps - 1) * mods + m, m - 1) for m in range(1, mods, 2)]
+    lone = [m for m in range(0, mods, 2)] + [(steps - 1) * mods + m for m in range(1, mods, 2)]
+    if mods % 4 == 0:
+        ends += [(a, a ^ 2) for a in lone if a & 2]
+    else:
+        ends += list(zip(lone[: mods // 2], lone[mods // 2 :]))
     halo = lax.ppermute(edge_frame, ("tm", "mod"), ends + [(b, a) for a, b in ends])
 
     cosine, sine, image, weights, data_total = call(
@@ -599,7 +630,7 @@
         [VMEM] * (mods + 4),
         scratch_shapes=[
             scratch(s)
-            for s in (f32(2, cells, LANES),) * 2 + (bf16(3 * cells, 4 * wide),) * 2
+            for s in (f32(2, cells, LANES),) * 2 + (bf16(2 * cells, 4 * wide),) * 2
         ],
         work=2.8,
     )(*pieces, mask, noise, even, odd)
@@ -611,37 +642,46 @@
         [VMEM] * (mods + 4),
         work=0.4,
     )(*pieces[1:], pair, halo, coef, edge, data_total)
-    totals = exchange([total] * steps, "tm")
-
-    *sent, prior = call(
+    totals = [
+        lax.ppermute(total, "tm", [(i, (i + k) % steps) for i in range(steps)]) for k in range(1, steps)
+    ]
+
+    size, pairs = plan.half + SUB, mods // 2
+    *sent, near, prior = call(
         functools.partial(backward_kernel, plan),
         "backward",
-        [f32(plan.half + SUB + (frames // 2 * shard if k == 1 else 0), LANES) for k in range(mods)]
-        + [f32(frames // 2, 2 * shard, LANES)],
+        [f32(size, LANES)] * pairs
+        + [f32(pairs * size + frames // 2 * shard, LANES), f32(frames // 2, 2 * shard, LANES)],
         [VMEM] * 11,
         scratch_shapes=[
             scratch(s)
-            for s in (f32(cells, LANES),) + (bf16(3 * cells, 2 * wide),) * 2 + (f32(2, cells, 2 * wide),)
+            for s in (f32(cells, LANES),) + (bf16(2 * cells, 2 * wide),) * 2 + (f32(2, cells, 2 * wide),)
         ],
         work=0.8,
     )(cosine, sine, image, weights, even_back, odd_back, halo, flow, rim, coef, edge)
-    sent = call(
-        functools.partial(seal_kernel, plan, steps),
+
+    def swap(array, k):
+        return lax.ppermute(array, "mod", [(i, i ^ k) for i in range(mods)])
+
+    near = swap(near, 1)
+    total = call(sum_kernel, "sum", [f32(SUB, LANES)], [VMEM] * steps, work=3.0)(*totals, total)[0]
+    joined = call(
+        functools.partial(seal_kernel, plan),
         "seal",
-        [f32(*p.shape) for p in sent],
-        [VMEM] * (steps + mods),
-        aliases={steps + k: k for k in range(mods)},
-    )(*totals[2:], *totals[:2], *sent)
-    returned = exchange(sent, "mod")
+        [f32(2 * size, LANES)] * (pairs - 1),
+        [VMEM] * (pairs + 1),
+    )(total, *sent[1:], near)
+    far = [swap(array, 2 * k + 2) for k, array in enumerate(joined)]
+    sums = [total] + [swap(total, k) for k in range(mods - 1, 0, -2)]
 
     hess_vec, curvature = call(
         functools.partial(final_kernel, plan, float(total_frames * plan.pupil * rows)),
         "join",
         [f32(*phase.shape), f32(1)],
-        [VMEM] * (mods + 3),
+        [VMEM] * (2 * pairs + 5),
         out_specs=[VMEM, SMEM],
         work=0.8,
-    )(*returned, prior, coef, edge)
+    )(sent[0], near, *far, *sums, prior, coef, edge)
     return hess_vec, curvature
 
 

time: 26.6 us -> 25.7 us (0.966)
  waiting for transfers between devices: 5.33 us -> 4.89 us
  Pallas kernels: 7.2 us -> 6.77 us
    ppermute x1, starting transfers between devices: 3.85 us -> 1.79 us  [per_device(): lax.ppermute(edge_frame, ('tm', 'mod'), ends + [(b, a) for a, b in ends])]
    ppermute x9 -> x10, starting transfers between devices: 8.66 us -> 10.7 us  [the longest x3 5.23 us: per_device(): lax.ppermute(total, 'tm', [(i, (i + k) % steps) for i in range(steps)])]
    ppermute x1, waiting for transfers between devices: 1.04 us -> 0.52 us  [per_device(): lax.ppermute(edge_frame, ('tm', 'mod'), ends + [(b, a) for a, b in ends])]
    ppermute x9 -> x10, waiting for transfers between devices: 4.3 us -> 4.36 us  [the longest x4 2.4 us: swap(): return lax.ppermute(array, 'mod', [(i, i ^ k) for i in range(mods)])]
    pallas_call x2 -> x3, Pallas kernels: 0.87 us -> 0.87 us  [the longest x1 0.85 us: per_device(): call(functools.partial(backward_kernel, plan), 'backward', [f32(size, LAN...]
  transfers between devices with their start and end apart: 10 -> 11, of which waited for: 5 -> 5; matrix products, arithmetic and copies ran while one was open for 0% -> 0% of each run, Pallas kernels for 19% -> 18%
where the time goes in v6:
time: 25.7 us; the launch traced here: 25.5 us
  starting transfers between devices  12.4 us (48%)
  Pallas kernels  6.77 us (26%)
  waiting for transfers between devices  4.89 us (19%)
  between operations  1.39 us (5%)
    ppermute x3, starting transfers between devices, per_device(): lax.ppermute(total, 'tm', [(i, (i + k) % steps) for i in range(steps)])  5.23 us
    ppermute x3, starting transfers between devices, exchange(): lax.ppermute(arrays[k], axis, [(i, i ^ k) for i in range(count)])  3.15 us
    ppermute x4, waiting for transfers between devices, swap(): return lax.ppermute(array, 'mod', [(i, i ^ k) for i in range(mods)])  2.4 us
    ppermute x4, starting transfers between devices, swap(): return lax.ppermute(array, 'mod', [(i, i ^ k) for i in range(mods)])  2.28 us
    pallas_call x1, Pallas kernels, per_device(): call(functools.partial(forward_kernel, plan), 'forward', [f32(2, cells, w...  2.06 us
    ppermute x1, starting transfers between devices, per_device(): lax.ppermute(edge_frame, ('tm', 'mod'), ends + [(b, a) for a, b in ends])  1.79 us
    pallas_call x1, Pallas kernels, per_device(): call(functools.partial(prep_kernel, plan), 'prepare', [f32(2, cells, LANE...  1.55 us
    ppermute x3, waiting for transfers between devices, per_device(): lax.ppermute(total, 'tm', [(i, (i + k) % steps) for i in range(steps)])  1.31 us
  transfers between devices with their start and end apart: 11, of which 5 were waited for; matrix products, arithmetic and copies ran while one was open for 0% of the time, Pallas kernels for 18%

profile of v6, /device:TPU:0, one launch (start us, length us, event | category | flops | bytes accessed | tf_op | source)
XLA Modules:
  0.0 25.5 jit_solution(3293490909321617755)
XLA Ops:
  1.3 1.2 %pack.1 = (f32[136,128]{1,0:T(8,128)S(1)}, f32[392,128]{1,0:T(8,128)S(1)}, f32[136,128]{1,0:T(8,128)S(1)}, f32[136,128]{1,0:T(8,128)S(1)}, f32[2,128,128]{2,1,0:T(8,128)S(1)}) custom-call(f32[2,128,128]{2,1,0:T(8,128)} %phase_hbm.1, f32[2,128,128]{2,1,0:T(8,128)} %direction_hbm.1), custom_call_target="tpu_custom_call" | custom-call | flops 1320000000 | bytes 4320000 | tf_op jit(solution)/shard_map/pack/pallas_call | solution.py:577
  2.5 0.5 %collective-permute-start = (f32[392,128]{1,0:T(8,128)S(1)}, f32[392,128]{1,0:T(8,128)S(1)}, u32[]{:S(2)}, u32[]{:S(2)}) collective-permute-start(f32[392,128]{1,0:T(8,128)S(1)} %get-tuple-element.38), channel_id=1, source_target_pairs={{0,1},{1,0},{2,3},{3,2},{4,5},{5,4},{6,7},{7,6},{8,9},{9,8},{10,11... | collective-permute-start | bytes 602120 | tf_op jit(solution)/shard_map/ppermute | solution.py:536
  3.0 2.6 %collective-permute-start.1 = (f32[136,128]{1,0:T(8,128)S(1)}, f32[136,128]{1,0:T(8,128)S(1)}, u32[]{:S(2)}, u32[]{:S(2)}) collective-permute-start(f32[136,128]{1,0:T(8,128)S(1)} %get-tuple-element.39), channel_id=1, source_target_pairs={{0,2},{1,3},{2,0},{3,1},{4,6},{5,7},{6,4},{7,5},{8,10},{9,11},{10,... | collective-permute-start | bytes 208904 | tf_op jit(solution)/shard_map/ppermute | solution.py:536
  5.6 0.1 collective-permute-start.2
  5.7 1.5 %prepare.1 = (f32[2,256,128]{2,1,0:T(8,128)S(1)}, f32[2,2,256,128]{3,2,1,0:T(8,128)S(1)}, f32[4,256,128]{2,1,0:T(8,128)S(1)}, f32[4,8,128]{2,1,0:T(8,128)S(1)}, ...) custom-call(f32[136,128]{1,0:T(8,128)S(1)} %get-tuple-element.37.see, ...), custom_call_target="tpu_custom_call" | custom-call | flops 1650000000 | bytes 5400000 | tf_op jit(solution)/shard_map/prepare/pallas_call | solution.py:596
  7.2 0.0 collective-permute-done.refs_1_.piece_ref.refs_0_
  7.3 1.8 %collective-permute-start.3 = (f32[256,128]{1,0:T(8,128)S(1)}, f32[256,128]{1,0:T(8,128)S(1)}, u32[]{:S(2)}, u32[]{:S(2)}) collective-permute-start(f32[256,128]{1,0:T(8,128)S(1)} %get-tuple-element.53), channel_id=1, source_target_pairs={{1,4},{3,6},{5,8},{7,10},{9,12},{11,14},{2,0},{15,13},{4,1},{6,3},... | collective-permute-start | bytes 393224 | tf_op jit(solution)/shard_map/ppermute | solution.py:624
  9.1 0.0 collective-permute-done.1.refs_2_.refs_1_
  9.1 0.7 %collective-permute-done.2.refs_3_.refs_2_ = f32[136,128]{1,0:T(8,128)S(1)} collective-permute-done((f32[136,128]{1,0:T(8,128)S(1)}, f32[136,128]{1,0:T(8,128)S(1)}, u32[]{:S(2)}, u32[]{:S(2)}) %collective-permute-start.2) | collective-permute-done | bytes 69664 | tf_op jit(solution)/shard_map/ppermute | solution.py:536
  9.7 2.1 %forward.1 = (f32[2,256,256]{2,1,0:T(8,128)S(1)}, f32[2,256,256]{2,1,0:T(8,128)S(1)}, f32[2,256,1024]{2,1,0:T(8,128)S(1)}, f32[3,2,256,128]{3,2,1,0:T(8,128)S(1)}, f32[8,128]{1,0:T(8,128)S(1)}) custom-call(f32[136,128]{1,0:T(8,128)S(1)} %get-tuple-element.37.seed_ref.refs_0_, f32[392,128]{1,0:T(8,128)S(1)} %collective-permute-done.refs_1_.piece_ref.refs_0_, ...), custom_call_target="tpu_custom_call" | custom-call | flops 3080000000 | bytes 10080000 | tf_op jit(solution)/shard_map/forward/pallas_call | solution.py:626
  11.8 0.5 %collective-permute-done.3.refs_4_.refs_6_ = f32[256,128]{1,0:T(8,128)S(1)} collective-permute-done((f32[256,128]{1,0:T(8,128)S(1)}, f32[256,128]{1,0:T(8,128)S(1)}, u32[]{:S(2)}, u32[]{:S(2)}) %collective-permute-start.3) | collective-permute-done | bytes 131104 | tf_op jit(solution)/shard_map/ppermute | solution.py:624
  12.3 0.2 prior.1
  12.5 1.3 %collective-permute-start.5 = (f32[8,128]{1,0:T(8,128)S(1)}, f32[8,128]{1,0:T(8,128)S(1)}, u32[]{:S(2)}, u32[]{:S(2)}) collective-permute-start(f32[8,128]{1,0:T(8,128)S(1)} %get-tuple-element.61.refs_3_), channel_id=1, source_target_pairs={{0,4},{4,8},{8,12},{12,0},{1,5},{5,9},{9,13},{13,1},{2,6},{6,10},{... | collective-permute-start | bytes 12296 | tf_op jit(solution)/shard_map/ppermute | solution.py:646
  13.8 2.6 %collective-permute-start.6 = (f32[8,128]{1,0:T(8,128)S(1)}, f32[8,128]{1,0:T(8,128)S(1)}, u32[]{:S(2)}, u32[]{:S(2)}) collective-permute-start(f32[8,128]{1,0:T(8,128)S(1)} %get-tuple-element.61.refs_3_), channel_id=1, source_target_pairs={{0,8},{4,12},{8,0},{12,4},{1,9},{5,13},{9,1},{13,5},{2,10},{6,14},... | collective-permute-start | bytes 12296 | tf_op jit(solution)/shard_map/ppermute | solution.py:646
  16.4 1.3 %collective-permute-start.7 = (f32[8,128]{1,0:T(8,128)S(1)}, f32[8,128]{1,0:T(8,128)S(1)}, u32[]{:S(2)}, u32[]{:S(2)}) collective-permute-start(f32[8,128]{1,0:T(8,128)S(1)} %get-tuple-element.61.refs_3_), channel_id=1, source_target_pairs={{0,12},{4,0},{8,4},{12,8},{1,13},{5,1},{9,5},{13,9},{2,14},{6,2},{... | collective-permute-start | bytes 12296 | tf_op jit(solution)/shard_map/ppermute | solution.py:646
  17.8 0.8 %backward.1 = (f32[72,128]{1,0:T(8,128)S(1)}, f32[72,128]{1,0:T(8,128)S(1)}, f32[272,128]{1,0:T(8,128)S(1)}, f32[1,256,128]{2,1,0:T(8,128)S(1)}) custom-call(f32[2,256,256]{2,1,0:T(8,128)S(1)} %get-tuple-element.45.refs_0_, f32[2,256,256]{2,1,0:T(8,128)S(1)} %get-tuple-element.46.refs_1_, f32[2,256,1024]{2,1,0:T(8,128)S(1)} %get-tuple-element.47.refs_2_, ...), custom_call_target="tpu_custom_call" | custom-call | flops 880000000 | bytes 2880000 | tf_op jit(solution)/shard_map/backward/pallas_call | solution.py:650
  18.6 0.1 collective-permute-start.4
  18.7 0.0 collective-permute-done.5.refs_0_
  18.7 0.0 collective-permute-done.6.refs_1_
  18.7 1.3 %collective-permute-done.7.refs_2_ = f32[8,128]{1,0:T(8,128)S(1)} collective-permute-done((f32[8,128]{1,0:T(8,128)S(1)}, f32[8,128]{1,0:T(8,128)S(1)}, u32[]{:S(2)}, u32[]{:S(2)}) %collective-permute-start.7) | collective-permute-done | bytes 4128 | tf_op jit(solution)/shard_map/ppermute | solution.py:646
  20.0 0.0 collective-permute-done.4.refs_1_
  20.1 1.6 %collective-permute-start.8 = (f32[144,128]{1,0:T(8,128)S(1)}, f32[144,128]{1,0:T(8,128)S(1)}, u32[]{:S(2)}, u32[]{:S(2)}) collective-permute-start(f32[144,128]{1,0:T(8,128)S(1)} %seal.1), channel_id=1, source_target_pairs={{0,2},{1,3},{2,0},{3,1},{4,6},{5,7},{6,4},{7,5},{8,10},{9,11},{10,... | collective-permute-start | bytes 221192 | tf_op jit(solution)/shard_map/ppermute | solution.py:664
  21.6 0.0 collective-permute-start.10
  21.6 0.6 %collective-permute-start.9 = (f32[8,128]{1,0:T(8,128)S(1)}, f32[8,128]{1,0:T(8,128)S(1)}, u32[]{:S(2)}, u32[]{:S(2)}) collective-permute-start(f32[8,128]{1,0:T(8,128)S(1)} %sum.1.total_ref.refs_3_), channel_id=1, source_target_pairs={{0,3},{1,2},{2,1},{3,0},{4,7},{5,6},{6,5},{7,4},{8,11},{9,10},{10,... | collective-permute-start | bytes 12296 | tf_op jit(solution)/shard_map/ppermute | solution.py:664
  22.3 0.5 %collective-permute-done.10.refs_5_ = f32[8,128]{1,0:T(8,128)S(1)} collective-permute-done((f32[8,128]{1,0:T(8,128)S(1)}, f32[8,128]{1,0:T(8,128)S(1)}, u32[]{:S(2)}, u32[]{:S(2)}) %collective-permute-start.10) | collective-permute-done | bytes 4128 | tf_op jit(solution)/shard_map/ppermute | solution.py:664
  22.8 1.9 %collective-permute-done.9.refs_4_ = f32[8,128]{1,0:T(8,128)S(1)} collective-permute-done((f32[8,128]{1,0:T(8,128)S(1)}, f32[8,128]{1,0:T(8,128)S(1)}, u32[]{:S(2)}, u32[]{:S(2)}) %collective-permute-start.9) | collective-permute-done | bytes 4128 | tf_op jit(solution)/shard_map/ppermute | solution.py:664
  24.7 0.0 collective-permute-done.8.refs_2_
  24.7 0.8 %join.1 = (f32[2,128,128]{2,1,0:T(8,128)}, f32[1]{0:T(128)}) custom-call(f32[72,128]{1,0:T(8,128)S(1)} %get-tuple-element.59.refs_0_, f32[272,128]{1,0:T(8,128)S(1)} %collective-permute-done.4.refs_1_, f32[144,128]{1,0:T(8,128)S(1)} %collective-permute-done.8.refs_2_, f32[8,128]{1,0:T(8,128)S(1)} %sum.1.total_ref.refs_3_, ...), custom_call_target="tpu_custom_call" | custom-call | flops 880000000 | bytes 2880000 | tf_op jit(solution)/shard_map/join/pallas_call | solution.py:677
  (5 shorter events, 0.1 us)
Async XLA Ops:
  2.5 4.7 %collective-permute-start = (f32[392,128]{1,0:T(8,128)S(1)}, f32[392,128]{1,0:T(8,128)S(1)}, u32[]{:S(2)}, u32[]{:S(2)}) collective-permute-start(f32[392,128]{1,0:T(8,128)S(1)} %get-tuple-element.38), channel_id=1, source_target_pairs={{0,1},{1,0},{2,3},{3,2},{4,5},{5,4},{6,7},{7,6},{8,9},{9,8},{10,11... | collective-permute-start | bytes 602120 | tf_op jit(solution)/shard_map/ppermute | solution.py:536
  3.0 6.0 %collective-permute-start.1 = (f32[136,128]{1,0:T(8,128)S(1)}, f32[136,128]{1,0:T(8,128)S(1)}, u32[]{:S(2)}, u32[]{:S(2)}) collective-permute-start(f32[136,128]{1,0:T(8,128)S(1)} %get-tuple-element.39), channel_id=1, source_target_pairs={{0,2},{1,3},{2,0},{3,1},{4,6},{5,7},{6,4},{7,5},{8,10},{9,11},{10,... | collective-permute-start | bytes 208904 | tf_op jit(solution)/shard_map/ppermute | solution.py:536
  5.6 4.1 %collective-permute-start.2 = (f32[136,128]{1,0:T(8,128)S(1)}, f32[136,128]{1,0:T(8,128)S(1)}, u32[]{:S(2)}, u32[]{:S(2)}) collective-permute-start(f32[136,128]{1,0:T(8,128)S(1)} %get-tuple-element.40), channel_id=1, source_target_pairs={{0,3},{1,2},{2,1},{3,0},{4,7},{5,6},{6,5},{7,4},{8,11},{9,10},{10,... | collective-permute-start | bytes 208904 | tf_op jit(solution)/shard_map/ppermute | solution.py:536
  7.3 5.0 %collective-permute-start.3 = (f32[256,128]{1,0:T(8,128)S(1)}, f32[256,128]{1,0:T(8,128)S(1)}, u32[]{:S(2)}, u32[]{:S(2)}) collective-permute-start(f32[256,128]{1,0:T(8,128)S(1)} %get-tuple-element.53), channel_id=1, source_target_pairs={{1,4},{3,6},{5,8},{7,10},{9,12},{11,14},{2,0},{15,13},{4,1},{6,3},... | collective-permute-start | bytes 393224 | tf_op jit(solution)/shard_map/ppermute | solution.py:624
  12.5 6.2 %collective-permute-start.5 = (f32[8,128]{1,0:T(8,128)S(1)}, f32[8,128]{1,0:T(8,128)S(1)}, u32[]{:S(2)}, u32[]{:S(2)}) collective-permute-start(f32[8,128]{1,0:T(8,128)S(1)} %get-tuple-element.61.refs_3_), channel_id=1, source_target_pairs={{0,4},{4,8},{8,12},{12,0},{1,5},{5,9},{9,13},{13,1},{2,6},{6,10},{... | collective-permute-start | bytes 12296 | tf_op jit(solution)/shard_map/ppermute | solution.py:646
  13.8 4.9 %collective-permute-start.6 = (f32[8,128]{1,0:T(8,128)S(1)}, f32[8,128]{1,0:T(8,128)S(1)}, u32[]{:S(2)}, u32[]{:S(2)}) collective-permute-start(f32[8,128]{1,0:T(8,128)S(1)} %get-tuple-element.61.refs_3_), channel_id=1, source_target_pairs={{0,8},{4,12},{8,0},{12,4},{1,9},{5,13},{9,1},{13,5},{2,10},{6,14},... | collective-permute-start | bytes 12296 | tf_op jit(solution)/shard_map/ppermute | solution.py:646
  16.4 3.6 %collective-permute-start.7 = (f32[8,128]{1,0:T(8,128)S(1)}, f32[8,128]{1,0:T(8,128)S(1)}, u32[]{:S(2)}, u32[]{:S(2)}) collective-permute-start(f32[8,128]{1,0:T(8,128)S(1)} %get-tuple-element.61.refs_3_), channel_id=1, source_target_pairs={{0,12},{4,0},{8,4},{12,8},{1,13},{5,1},{9,5},{13,9},{2,14},{6,2},{... | collective-permute-start | bytes 12296 | tf_op jit(solution)/shard_map/ppermute | solution.py:646
  18.6 1.4 %collective-permute-start.4 = (f32[272,128]{1,0:T(8,128)S(1)}, f32[272,128]{1,0:T(8,128)S(1)}, u32[]{:S(2)}, u32[]{:S(2)}) collective-permute-start(f32[272,128]{1,0:T(8,128)S(1)} %get-tuple-element.60), channel_id=1, source_target_pairs={{0,1},{1,0},{2,3},{3,2},{4,5},{5,4},{6,7},{7,6},{8,9},{9,8},{10,11... | collective-permute-start | bytes 417800 | tf_op jit(solution)/shard_map/ppermute | solution.py:664
  20.1 4.6 %collective-permute-start.8 = (f32[144,128]{1,0:T(8,128)S(1)}, f32[144,128]{1,0:T(8,128)S(1)}, u32[]{:S(2)}, u32[]{:S(2)}) collective-permute-start(f32[144,128]{1,0:T(8,128)S(1)} %seal.1), channel_id=1, source_target_pairs={{0,2},{1,3},{2,0},{3,1},{4,6},{5,7},{6,4},{7,5},{8,10},{9,11},{10,... | collective-permute-start | bytes 221192 | tf_op jit(solution)/shard_map/ppermute | solution.py:664
  21.6 1.2 %collective-permute-start.10 = (f32[8,128]{1,0:T(8,128)S(1)}, f32[8,128]{1,0:T(8,128)S(1)}, u32[]{:S(2)}, u32[]{:S(2)}) collective-permute-start(f32[8,128]{1,0:T(8,128)S(1)} %sum.1.total_ref.refs_3_), channel_id=1, source_target_pairs={{0,1},{1,0},{2,3},{3,2},{4,5},{5,4},{6,7},{7,6},{8,9},{9,8},{10,11... | collective-permute-start | bytes 12296 | tf_op jit(solution)/shard_map/ppermute | solution.py:664
  21.6 3.0 %collective-permute-start.9 = (f32[8,128]{1,0:T(8,128)S(1)}, f32[8,128]{1,0:T(8,128)S(1)}, u32[]{:S(2)}, u32[]{:S(2)}) collective-permute-start(f32[8,128]{1,0:T(8,128)S(1)} %sum.1.total_ref.refs_3_), channel_id=1, source_target_pairs={{0,3},{1,2},{2,1},{3,0},{4,7},{5,6},{6,5},{7,4},{8,11},{9,10},{10,... | collective-permute-start | bytes 12296 | tf_op jit(solution)/shard_map/ppermute | solution.py:664

commit v7 on v6

--- a/solution.py
+++ b/solution.py
@@ -92,20 +92,15 @@
     return lax.axis_index(axis)
 
 
-def pack_kernel(plan, phase_hbm, direction_hbm, *refs):
-    outs = refs[: plan.mods]
-    direction_ref, phase_ref, sems = refs[plan.mods :]
-    loads = [
-        pltpu.make_async_copy(source, target, sems.at[i])
-        for i, (source, target) in enumerate(((direction_hbm, direction_ref), (phase_hbm, phase_ref)))
-    ]
-    for load in loads:
-        load.start()
+def tilt_kernel(tilt_ref, out_ref):
+    out_ref[...] = tilt_ref[...]
+
+
+def pack_kernel(plan, tilt_ref, phase_ref, direction_ref, *refs):
+    outs, near_ref = refs[: plan.mods], refs[plan.mods]
     me = place_on("mod")
     width, half, shard, frames = plan.width, plan.half, plan.shard, plan.frames
     lane = lax.broadcasted_iota(jnp.int32, (half, LANES), 1)
-    for load in loads:
-        load.wait()
     for k, out in enumerate(outs):
         dest = me ^ k
         frame, group = dest // plan.groups, dest % plan.groups
@@ -119,11 +114,13 @@
         rows = []
         for f in range(frames):
             rows += [direction_ref[f, 0:1, :], direction_ref[f, shard - 1 : shard, :]]
+        rows += [tilt_ref[p : p + 1, :] for p in range(plan.points)]
         rows += [jnp.zeros((1, LANES), jnp.float32)] * (plan.extra - len(rows))
         out[shard : shard + plan.extra, :] = jnp.concatenate(rows, axis=0)
     for f in range(frames):
         start = shard + plan.extra + f * shard
         outs[1][start : start + shard, :] = direction_ref[f]
+        near_ref[f] = direction_ref[f]
 
 
 def relay_kernel(plan, own_ref, piece_ref, after_ref, pair_ref, send_ref):
@@ -134,12 +131,6 @@
         pair_ref[f, pl.ds(pl.multiple_of(side * shard, SUB), shard), :] = own_ref[f]
         pair_ref[f, pl.ds(pl.multiple_of((1 - side) * shard, SUB), shard), :] = piece_ref[start : start + shard, :]
     send_ref[...] = pair_ref[side * (frames - 1)]
-
-
-def label_kernel(plan, tilt_ref, *refs):
-    at = plan.shard + 2 * plan.frames
-    for out in refs[plan.mods :]:
-        out[at : at + plan.points, :] = tilt_ref[...]
 
 
 def prep_kernel(plan, seed_ref, mask_hbm, noise_hbm, codes_hbm, *refs):
@@ -544,9 +535,9 @@
     total_frames = frames * steps
     cells, wide = plan.cells, plan.tiles * LANES
     tables = [jnp.asarray(t) for t in roof_tables(plan)]
-    phase, direction, pupil_mask, wind_codes, noise_weight, *tables = [
+    pupil_mask, wind_codes, noise_weight, *tables = [
         pltpu.with_memory_space_constraint(array, pltpu.HBM)
-        for array in (phase, direction, pupil_mask, wind_codes, noise_weight, *tables)
+        for array in (pupil_mask, wind_codes, noise_weight, *tables)
     ]
 
     def f32(*shape):
@@ -574,22 +565,15 @@
         )
 
     rows_in = shard + plan.extra
+    tilts = jnp.broadcast_to(mod_tilts.astype(jnp.float32)[:, None], (plan.points, LANES))
+    tilts = call(tilt_kernel, "tilts", [f32(plan.points, LANES)], [VMEM], work=0.8)(tilts)[0]
     *packed, direction_near = call(
         functools.partial(pack_kernel, plan),
         "pack",
         [f32(rows_in + (frames * shard if k == 1 else 0), LANES) for k in range(mods)] + [f32(*phase.shape)],
-        [HBM] * 2,
-        scratch_shapes=[scratch(phase), pltpu.SemaphoreType.DMA((2,))],
-        work=1.2,
-    )(phase, direction)
-    tilts = jnp.broadcast_to(mod_tilts.astype(jnp.float32)[:, None], (plan.points, LANES))
-    packed = call(
-        functools.partial(label_kernel, plan),
-        "label",
-        [f32(*p.shape) for p in packed],
-        [VMEM] * (mods + 1),
-        aliases={k + 1: k for k in range(mods)},
-    )(tilts, *packed)
+        [VMEM] * 3,
+        work=0.3,
+    )(tilts, phase, direction)
     pieces = exchange(packed, "mod")
 
     table = bf16(*tables[0].shape)

time: 25.7 us -> 25 us (0.973)
  Pallas kernels: 6.77 us -> 5.77 us
    pallas_call x1, Pallas kernels: 1.2 us -> 0.2 us  [per_device(): call(functools.partial(pack_kernel, plan), 'pack', [f32(rows_in + (frames...]
    unnamed x0 -> x4, local copies, waits for them, and re-layouts: none -> 0.26 us
where the time goes in v7:
time: 25 us; the launch traced here: 24.8 us
  starting transfers between devices  12.4 us (50%)
  Pallas kernels  5.77 us (23%)
  waiting for transfers between devices  4.89 us (20%)
  between operations  1.45 us (6%)
  local copies, waits for them, and re-layouts  0.26 us (1%)
    ppermute x3, starting transfers between devices, per_device(): lax.ppermute(total, 'tm', [(i, (i + k) % steps) for i in range(steps)])  5.23 us
    ppermute x3, starting transfers between devices, exchange(): lax.ppermute(arrays[k], axis, [(i, i ^ k) for i in range(count)])  3.15 us
    ppermute x4, waiting for transfers between devices, swap(): return lax.ppermute(array, 'mod', [(i, i ^ k) for i in range(mods)])  2.4 us
    ppermute x4, starting transfers between devices, swap(): return lax.ppermute(array, 'mod', [(i, i ^ k) for i in range(mods)])  2.28 us
    pallas_call x1, Pallas kernels, per_device(): call(functools.partial(forward_kernel, plan), 'forward', [f32(2, cells, w...  2.05 us
    ppermute x1, starting transfers between devices, per_device(): lax.ppermute(edge_frame, ('tm', 'mod'), ends + [(b, a) for a, b in ends])  1.79 us
    pallas_call x1, Pallas kernels, per_device(): call(functools.partial(prep_kernel, plan), 'prepare', [f32(2, cells, LANE...  1.55 us
    ppermute x3, waiting for transfers between devices, per_device(): lax.ppermute(total, 'tm', [(i, (i + k) % steps) for i in range(steps)])  1.31 us
  transfers between devices with their start and end apart: 11, of which 5 were waited for; matrix products, arithmetic and copies ran while one was open for 0% of the time, Pallas kernels for 18%

profile of v7, /device:TPU:0, one launch (start us, length us, event | category | flops | bytes accessed | tf_op | source)
XLA Modules:
  0.0 24.8 jit_solution(12718507553380933066)
XLA Ops:
  0.6 0.0 copy-start
  0.6 0.0 copy-start.1
  1.4 0.2 copy-done
  1.6 0.1 copy-done.1
  1.6 0.2 pack.1
  1.8 0.5 %collective-permute-start = (f32[392,128]{1,0:T(8,128)S(1)}, f32[392,128]{1,0:T(8,128)S(1)}, u32[]{:S(2)}, u32[]{:S(2)}) collective-permute-start(f32[392,128]{1,0:T(8,128)S(1)} %get-tuple-element.30), channel_id=1, source_target_pairs={{0,1},{1,0},{2,3},{3,2},{4,5},{5,4},{6,7},{7,6},{8,9},{9,8},{10,11... | collective-permute-start | bytes 602120 | tf_op jit(solution)/shard_map/ppermute | solution.py:527
  2.3 2.6 %collective-permute-start.1 = (f32[136,128]{1,0:T(8,128)S(1)}, f32[136,128]{1,0:T(8,128)S(1)}, u32[]{:S(2)}, u32[]{:S(2)}) collective-permute-start(f32[136,128]{1,0:T(8,128)S(1)} %get-tuple-element.31), channel_id=1, source_target_pairs={{0,2},{1,3},{2,0},{3,1},{4,6},{5,7},{6,4},{7,5},{8,10},{9,11},{10,... | collective-permute-start | bytes 208904 | tf_op jit(solution)/shard_map/ppermute | solution.py:527
  4.9 0.1 collective-permute-start.2
  5.0 1.5 %prepare.1 = (f32[2,256,128]{2,1,0:T(8,128)S(1)}, f32[2,2,256,128]{3,2,1,0:T(8,128)S(1)}, f32[4,256,128]{2,1,0:T(8,128)S(1)}, f32[4,8,128]{2,1,0:T(8,128)S(1)}, ...) custom-call(f32[136,128]{1,0:T(8,128)S(1)} %get-tuple-element.29.see, ...), custom_call_target="tpu_custom_call" | custom-call | flops 1650000000 | bytes 5400000 | tf_op jit(solution)/shard_map/prepare/pallas_call | solution.py:580
  6.5 0.0 collective-permute-done.refs_1_.piece_ref.refs_0_
  6.6 1.8 %collective-permute-start.3 = (f32[256,128]{1,0:T(8,128)S(1)}, f32[256,128]{1,0:T(8,128)S(1)}, u32[]{:S(2)}, u32[]{:S(2)}) collective-permute-start(f32[256,128]{1,0:T(8,128)S(1)} %get-tuple-element.45), channel_id=1, source_target_pairs={{1,4},{3,6},{5,8},{7,10},{9,12},{11,14},{2,0},{15,13},{4,1},{6,3},... | collective-permute-start | bytes 393224 | tf_op jit(solution)/shard_map/ppermute | solution.py:608
  8.4 0.0 collective-permute-done.1.refs_2_.refs_1_
  8.4 0.7 %collective-permute-done.2.refs_3_.refs_2_ = f32[136,128]{1,0:T(8,128)S(1)} collective-permute-done((f32[136,128]{1,0:T(8,128)S(1)}, f32[136,128]{1,0:T(8,128)S(1)}, u32[]{:S(2)}, u32[]{:S(2)}) %collective-permute-start.2) | collective-permute-done | bytes 69664 | tf_op jit(solution)/shard_map/ppermute | solution.py:527
  9.0 2.1 %forward.1 = (f32[2,256,256]{2,1,0:T(8,128)S(1)}, f32[2,256,256]{2,1,0:T(8,128)S(1)}, f32[2,256,1024]{2,1,0:T(8,128)S(1)}, f32[3,2,256,128]{3,2,1,0:T(8,128)S(1)}, f32[8,128]{1,0:T(8,128)S(1)}) custom-call(f32[136,128]{1,0:T(8,128)S(1)} %get-tuple-element.29.seed_ref.refs_0_, f32[392,128]{1,0:T(8,128)S(1)} %collective-permute-done.refs_1_.piece_ref.refs_0_, ...), custom_call_target="tpu_custom_call" | custom-call | flops 3080000000 | bytes 10080000 | tf_op jit(solution)/shard_map/forward/pallas_call | solution.py:610
  11.1 0.5 %collective-permute-done.3.refs_4_.refs_6_ = f32[256,128]{1,0:T(8,128)S(1)} collective-permute-done((f32[256,128]{1,0:T(8,128)S(1)}, f32[256,128]{1,0:T(8,128)S(1)}, u32[]{:S(2)}, u32[]{:S(2)}) %collective-permute-start.3) | collective-permute-done | bytes 131104 | tf_op jit(solution)/shard_map/ppermute | solution.py:608
  11.6 0.2 prior.1
  11.9 1.3 %collective-permute-start.5 = (f32[8,128]{1,0:T(8,128)S(1)}, f32[8,128]{1,0:T(8,128)S(1)}, u32[]{:S(2)}, u32[]{:S(2)}) collective-permute-start(f32[8,128]{1,0:T(8,128)S(1)} %get-tuple-element.53.refs_3_), channel_id=1, source_target_pairs={{0,4},{4,8},{8,12},{12,0},{1,5},{5,9},{9,13},{13,1},{2,6},{6,10},{... | collective-permute-start | bytes 12296 | tf_op jit(solution)/shard_map/ppermute | solution.py:630
  13.1 2.6 %collective-permute-start.6 = (f32[8,128]{1,0:T(8,128)S(1)}, f32[8,128]{1,0:T(8,128)S(1)}, u32[]{:S(2)}, u32[]{:S(2)}) collective-permute-start(f32[8,128]{1,0:T(8,128)S(1)} %get-tuple-element.53.refs_3_), channel_id=1, source_target_pairs={{0,8},{4,12},{8,0},{12,4},{1,9},{5,13},{9,1},{13,5},{2,10},{6,14},... | collective-permute-start | bytes 12296 | tf_op jit(solution)/shard_map/ppermute | solution.py:630
  15.7 1.3 %collective-permute-start.7 = (f32[8,128]{1,0:T(8,128)S(1)}, f32[8,128]{1,0:T(8,128)S(1)}, u32[]{:S(2)}, u32[]{:S(2)}) collective-permute-start(f32[8,128]{1,0:T(8,128)S(1)} %get-tuple-element.53.refs_3_), channel_id=1, source_target_pairs={{0,12},{4,0},{8,4},{12,8},{1,13},{5,1},{9,5},{13,9},{2,14},{6,2},{... | collective-permute-start | bytes 12296 | tf_op jit(solution)/shard_map/ppermute | solution.py:630
  17.1 0.8 %backward.1 = (f32[72,128]{1,0:T(8,128)S(1)}, f32[72,128]{1,0:T(8,128)S(1)}, f32[272,128]{1,0:T(8,128)S(1)}, f32[1,256,128]{2,1,0:T(8,128)S(1)}) custom-call(f32[2,256,256]{2,1,0:T(8,128)S(1)} %get-tuple-element.37.refs_0_, f32[2,256,256]{2,1,0:T(8,128)S(1)} %get-tuple-element.38.refs_1_, f32[2,256,1024]{2,1,0:T(8,128)S(1)} %get-tuple-element.39.refs_2_, ...), custom_call_target="tpu_custom_call" | custom-call | flops 880000000 | bytes 2880000 | tf_op jit(solution)/shard_map/backward/pallas_call | solution.py:634
  17.9 0.1 collective-permute-start.4
  18.0 0.0 collective-permute-done.5.refs_0_
  18.0 0.0 collective-permute-done.6.refs_1_
  18.0 1.3 %collective-permute-done.7.refs_2_ = f32[8,128]{1,0:T(8,128)S(1)} collective-permute-done((f32[8,128]{1,0:T(8,128)S(1)}, f32[8,128]{1,0:T(8,128)S(1)}, u32[]{:S(2)}, u32[]{:S(2)}) %collective-permute-start.7) | collective-permute-done | bytes 4128 | tf_op jit(solution)/shard_map/ppermute | solution.py:630
  19.4 0.0 collective-permute-done.4.refs_1_
  19.4 1.6 %collective-permute-start.8 = (f32[144,128]{1,0:T(8,128)S(1)}, f32[144,128]{1,0:T(8,128)S(1)}, u32[]{:S(2)}, u32[]{:S(2)}) collective-permute-start(f32[144,128]{1,0:T(8,128)S(1)} %seal.1), channel_id=1, source_target_pairs={{0,2},{1,3},{2,0},{3,1},{4,6},{5,7},{6,4},{7,5},{8,10},{9,11},{10,... | collective-permute-start | bytes 221192 | tf_op jit(solution)/shard_map/ppermute | solution.py:648
  20.9 0.0 collective-permute-start.10
  20.9 0.6 %collective-permute-start.9 = (f32[8,128]{1,0:T(8,128)S(1)}, f32[8,128]{1,0:T(8,128)S(1)}, u32[]{:S(2)}, u32[]{:S(2)}) collective-permute-start(f32[8,128]{1,0:T(8,128)S(1)} %sum.1.total_ref.refs_3_), channel_id=1, source_target_pairs={{0,3},{1,2},{2,1},{3,0},{4,7},{5,6},{6,5},{7,4},{8,11},{9,10},{10,... | collective-permute-start | bytes 12296 | tf_op jit(solution)/shard_map/ppermute | solution.py:648
  21.6 0.5 %collective-permute-done.10.refs_5_ = f32[8,128]{1,0:T(8,128)S(1)} collective-permute-done((f32[8,128]{1,0:T(8,128)S(1)}, f32[8,128]{1,0:T(8,128)S(1)}, u32[]{:S(2)}, u32[]{:S(2)}) %collective-permute-start.10) | collective-permute-done | bytes 4128 | tf_op jit(solution)/shard_map/ppermute | solution.py:648
  22.1 1.9 %collective-permute-done.9.refs_4_ = f32[8,128]{1,0:T(8,128)S(1)} collective-permute-done((f32[8,128]{1,0:T(8,128)S(1)}, f32[8,128]{1,0:T(8,128)S(1)}, u32[]{:S(2)}, u32[]{:S(2)}) %collective-permute-start.9) | collective-permute-done | bytes 4128 | tf_op jit(solution)/shard_map/ppermute | solution.py:648
  24.0 0.0 collective-permute-done.8.refs_2_
  24.0 0.8 %join.1 = (f32[2,128,128]{2,1,0:T(8,128)}, f32[1]{0:T(128)}) custom-call(f32[72,128]{1,0:T(8,128)S(1)} %get-tuple-element.51.refs_0_, f32[272,128]{1,0:T(8,128)S(1)} %collective-permute-done.4.refs_1_, f32[144,128]{1,0:T(8,128)S(1)} %collective-permute-done.8.refs_2_, f32[8,128]{1,0:T(8,128)S(1)} %sum.1.total_ref.refs_3_, ...), custom_call_target="tpu_custom_call" | custom-call | flops 880000000 | bytes 2880000 | tf_op jit(solution)/shard_map/join/pallas_call | solution.py:661
  (5 shorter events, 0.1 us)
Async XLA Ops:
  0.6 0.9 %copy-start = (f32[2,128,128]{2,1,0:T(8,128)S(1)}, f32[2,128,128]{2,1,0:T(8,128)}, u32[]{:S(2)}) copy-start(f32[2,128,128]{2,1,0:T(8,128)} %phase_ref.1) | copy-start | bytes 393220
  0.6 1.0 %copy-start.1 = (f32[2,128,128]{2,1,0:T(8,128)S(1)}, f32[2,128,128]{2,1,0:T(8,128)}, u32[]{:S(2)}) copy-start(f32[2,128,128]{2,1,0:T(8,128)} %direction_ref.1) | copy-start | bytes 393220
  1.8 4.7 %collective-permute-start = (f32[392,128]{1,0:T(8,128)S(1)}, f32[392,128]{1,0:T(8,128)S(1)}, u32[]{:S(2)}, u32[]{:S(2)}) collective-permute-start(f32[392,128]{1,0:T(8,128)S(1)} %get-tuple-element.30), channel_id=1, source_target_pairs={{0,1},{1,0},{2,3},{3,2},{4,5},{5,4},{6,7},{7,6},{8,9},{9,8},{10,11... | collective-permute-start | bytes 602120 | tf_op jit(solution)/shard_map/ppermute | solution.py:527
  2.3 6.0 %collective-permute-start.1 = (f32[136,128]{1,0:T(8,128)S(1)}, f32[136,128]{1,0:T(8,128)S(1)}, u32[]{:S(2)}, u32[]{:S(2)}) collective-permute-start(f32[136,128]{1,0:T(8,128)S(1)} %get-tuple-element.31), channel_id=1, source_target_pairs={{0,2},{1,3},{2,0},{3,1},{4,6},{5,7},{6,4},{7,5},{8,10},{9,11},{10,... | collective-permute-start | bytes 208904 | tf_op jit(solution)/shard_map/ppermute | solution.py:527
  4.9 4.1 %collective-permute-start.2 = (f32[136,128]{1,0:T(8,128)S(1)}, f32[136,128]{1,0:T(8,128)S(1)}, u32[]{:S(2)}, u32[]{:S(2)}) collective-permute-start(f32[136,128]{1,0:T(8,128)S(1)} %get-tuple-element.32), channel_id=1, source_target_pairs={{0,3},{1,2},{2,1},{3,0},{4,7},{5,6},{6,5},{7,4},{8,11},{9,10},{10,... | collective-permute-start | bytes 208904 | tf_op jit(solution)/shard_map/ppermute | solution.py:527
  6.6 5.0 %collective-permute-start.3 = (f32[256,128]{1,0:T(8,128)S(1)}, f32[256,128]{1,0:T(8,128)S(1)}, u32[]{:S(2)}, u32[]{:S(2)}) collective-permute-start(f32[256,128]{1,0:T(8,128)S(1)} %get-tuple-element.45), channel_id=1, source_target_pairs={{1,4},{3,6},{5,8},{7,10},{9,12},{11,14},{2,0},{15,13},{4,1},{6,3},... | collective-permute-start | bytes 393224 | tf_op jit(solution)/shard_map/ppermute | solution.py:608
  11.9 6.2 %collective-permute-start.5 = (f32[8,128]{1,0:T(8,128)S(1)}, f32[8,128]{1,0:T(8,128)S(1)}, u32[]{:S(2)}, u32[]{:S(2)}) collective-permute-start(f32[8,128]{1,0:T(8,128)S(1)} %get-tuple-element.53.refs_3_), channel_id=1, source_target_pairs={{0,4},{4,8},{8,12},{12,0},{1,5},{5,9},{9,13},{13,1},{2,6},{6,10},{... | collective-permute-start | bytes 12296 | tf_op jit(solution)/shard_map/ppermute | solution.py:630
  13.1 4.9 %collective-permute-start.6 = (f32[8,128]{1,0:T(8,128)S(1)}, f32[8,128]{1,0:T(8,128)S(1)}, u32[]{:S(2)}, u32[]{:S(2)}) collective-permute-start(f32[8,128]{1,0:T(8,128)S(1)} %get-tuple-element.53.refs_3_), channel_id=1, source_target_pairs={{0,8},{4,12},{8,0},{12,4},{1,9},{5,13},{9,1},{13,5},{2,10},{6,14},... | collective-permute-start | bytes 12296 | tf_op jit(solution)/shard_map/ppermute | solution.py:630
  15.7 3.6 %collective-permute-start.7 = (f32[8,128]{1,0:T(8,128)S(1)}, f32[8,128]{1,0:T(8,128)S(1)}, u32[]{:S(2)}, u32[]{:S(2)}) collective-permute-start(f32[8,128]{1,0:T(8,128)S(1)} %get-tuple-element.53.refs_3_), channel_id=1, source_target_pairs={{0,12},{4,0},{8,4},{12,8},{1,13},{5,1},{9,5},{13,9},{2,14},{6,2},{... | collective-permute-start | bytes 12296 | tf_op jit(solution)/shard_map/ppermute | solution.py:630
  17.9 1.4 %collective-permute-start.4 = (f32[272,128]{1,0:T(8,128)S(1)}, f32[272,128]{1,0:T(8,128)S(1)}, u32[]{:S(2)}, u32[]{:S(2)}) collective-permute-start(f32[272,128]{1,0:T(8,128)S(1)} %get-tuple-element.52), channel_id=1, source_target_pairs={{0,1},{1,0},{2,3},{3,2},{4,5},{5,4},{6,7},{7,6},{8,9},{9,8},{10,11... | collective-permute-start | bytes 417800 | tf_op jit(solution)/shard_map/ppermute | solution.py:648
  19.4 4.6 %collective-permute-start.8 = (f32[144,128]{1,0:T(8,128)S(1)}, f32[144,128]{1,0:T(8,128)S(1)}, u32[]{:S(2)}, u32[]{:S(2)}) collective-permute-start(f32[144,128]{1,0:T(8,128)S(1)} %seal.1), channel_id=1, source_target_pairs={{0,2},{1,3},{2,0},{3,1},{4,6},{5,7},{6,4},{7,5},{8,10},{9,11},{10,... | collective-permute-start | bytes 221192 | tf_op jit(solution)/shard_map/ppermute | solution.py:648
  20.9 1.2 %collective-permute-start.10 = (f32[8,128]{1,0:T(8,128)S(1)}, f32[8,128]{1,0:T(8,128)S(1)}, u32[]{:S(2)}, u32[]{:S(2)}) collective-permute-start(f32[8,128]{1,0:T(8,128)S(1)} %sum.1.total_ref.refs_3_), channel_id=1, source_target_pairs={{0,1},{1,0},{2,3},{3,2},{4,5},{5,4},{6,7},{7,6},{8,9},{9,8},{10,11... | collective-permute-start | bytes 12296 | tf_op jit(solution)/shard_map/ppermute | solution.py:648
  20.9 3.0 %collective-permute-start.9 = (f32[8,128]{1,0:T(8,128)S(1)}, f32[8,128]{1,0:T(8,128)S(1)}, u32[]{:S(2)}, u32[]{:S(2)}) collective-permute-start(f32[8,128]{1,0:T(8,128)S(1)} %sum.1.total_ref.refs_3_), channel_id=1, source_target_pairs={{0,3},{1,2},{2,1},{3,0},{4,7},{5,6},{6,5},{7,4},{8,11},{9,10},{10,... | collective-permute-start | bytes 12296 | tf_op jit(solution)/shard_map/ppermute | solution.py:648

commit v8 on v7

--- a/solution.py
+++ b/solution.py
@@ -480,38 +480,50 @@
     total_ref[...] = total
 
 
-def final_kernel(plan, entries, *refs):
-    mods, half, width, shard = plan.mods, plan.half, plan.width, plan.shard
-    size, pairs = half + SUB, plan.mods // 2
-    own_ref, near_ref, far = refs[0], refs[1], refs[2 : pairs + 1]
-    sums, refs = refs[pairs + 1 : 2 * pairs + 2], refs[2 * pairs + 2 :]
-    prior_ref, coef_ref, edge_ref, hess_ref, curvature_ref = refs
-    pieces = [(own_ref, 0), (near_ref, 0)]
-    for ref in far:
-        pieces += [(ref, 0), (ref, size)]
+def add_pieces(plan, me, pieces, hess_ref):
+    half, width = plan.half, plan.width
+    lane_group = lax.broadcasted_iota(jnp.int32, (half, LANES), 1) // width
+    for k, piece, at in pieces:
+        source = me ^ k
+        frame, group = source // plan.groups, source % plan.groups
+        for parity in range(2):
+            own = pl.ds(parity, half, stride=2)
+            cells = piece[at : at + half, :]
+            if plan.copies == 2:
+                moved = jnp.where(group == parity, cells, pltpu.roll(cells, width, 1))
+            else:
+                moved = pltpu.roll(cells, (group * width - parity * width + LANES) % LANES, 1)
+            hess_ref[frame, own, :] += jnp.where(lane_group == group, moved, 0.0)
+
+
+def begin_kernel(plan, own_ref, near_ref, prior_ref, hess_ref):
+    shard, start = plan.shard, plan.mods // 2 * (plan.half + SUB)
     me = place_on("mod")
     side, held = me % 2, plan.frames // 2
     mine = pl.ds(pl.multiple_of(side * shard, SUB), shard)
     for f in range(held):
-        start = pairs * size + f * shard
         hess_ref[side * held + f] = prior_ref[f, mine, :]
-        hess_ref[(1 - side) * held + f] = near_ref[start : start + shard, :]
-    lane = lax.broadcasted_iota(jnp.int32, (half, LANES), 1)
-    for parity in range(2):
-        own = pl.ds(parity, half, stride=2)
-        for k, (piece, at) in enumerate(pieces):
-            source = me ^ k
-            frame, group = source // plan.groups, source % plan.groups
-            turn = (group * width - parity * width + LANES) % LANES
-            moved = pltpu.roll(piece[at : at + half, :], turn, 1)
-            hess_ref[frame, own, :] += jnp.where(lane // width == group, moved, 0.0)
+        hess_ref[(1 - side) * held + f] = near_ref[start + f * shard : start + (f + 1) * shard, :]
+    add_pieces(plan, me, [(0, own_ref, 0), (1, near_ref, 0)], hess_ref)
+
+
+def final_kernel(plan, entries, *refs):
+    half, shard = plan.half, plan.shard
+    size, pairs = half + SUB, plan.mods // 2
+    begun_ref, far, sums = refs[0], refs[1:pairs], refs[pairs : 2 * pairs + 1]
+    coef_ref, edge_ref, hess_ref, curvature_ref = refs[2 * pairs + 1 :]
+    me = place_on("mod")
+    side = me % 2
+    pieces = [(2 * i + 2 + p, ref, p * size) for i, ref in enumerate(far) for p in range(2)]
+    hess_ref[...] = begun_ref[...]
+    add_pieces(plan, me, pieces, hess_ref)
     zero_row = jnp.zeros((1, LANES), jnp.float32)
     total, above, below = zero_row, zero_row, zero_row
     for ref in sums:
         total += ref[0:1, :]
     for ref in far:
         total += ref[half + 2 : half + 3, :]
-    for k, (piece, at) in enumerate(pieces):
+    for k, piece, at in pieces:
         source, at = me ^ k, at + half
         above = jnp.where((source == me + 1) & (side == 1), piece[at : at + 1, :], above)
         below = jnp.where((source == me - 1) & (side == 0), piece[at + 1 : at + 2, :], below)
@@ -656,16 +668,19 @@
         [VMEM] * (pairs + 1),
     )(total, *sent[1:], near)
     far = [swap(array, 2 * k + 2) for k, array in enumerate(joined)]
-    sums = [total] + [swap(total, k) for k in range(mods - 1, 0, -2)]
-
+    sums = [total] + [swap(total, k) for k in range(1, mods, 2)]
+
+    begun = call(functools.partial(begin_kernel, plan), "begin", [f32(*phase.shape)], [VMEM] * 3, work=0.2)(
+        sent[0], near, prior
+    )[0]
     hess_vec, curvature = call(
         functools.partial(final_kernel, plan, float(total_frames * plan.pupil * rows)),
         "join",
         [f32(*phase.shape), f32(1)],
-        [VMEM] * (2 * pairs + 5),
+        [VMEM] * (2 * pairs + 3),
         out_specs=[VMEM, SMEM],
         work=0.8,
-    )(sent[0], near, *far, *sums, prior, coef, edge)
+    )(begun, *far, *sums, coef, edge)
     return hess_vec, curvature
 
 

time: 25 us -> 24.9 us (level)
  transfers between devices with their start and end apart: 11 -> 11, of which waited for: 5 -> 4; matrix products, arithmetic and copies ran while one was open for 0% -> 0% of each run, Pallas kernels for 18% -> 19%
where the time goes in v8:
time: 24.9 us; the launch traced here: 24.8 us
  starting transfers between devices  12.4 us (50%)
  Pallas kernels  5.82 us (23%)
  waiting for transfers between devices  4.8 us (19%)
  between operations  1.45 us (6%)
  local copies, waits for them, and re-layouts  0.26 us (1%)
    ppermute x3, starting transfers between devices, per_device(): lax.ppermute(total, 'tm', [(i, (i + k) % steps) for i in range(steps)])  5.23 us
    ppermute x3, starting transfers between devices, exchange(): lax.ppermute(arrays[k], axis, [(i, i ^ k) for i in range(count)])  3.15 us
    ppermute x4, waiting for transfers between devices, swap(): return lax.ppermute(array, 'mod', [(i, i ^ k) for i in range(mods)])  2.31 us
    ppermute x4, starting transfers between devices, swap(): return lax.ppermute(array, 'mod', [(i, i ^ k) for i in range(mods)])  2.28 us
    pallas_call x1, Pallas kernels, per_device(): call(functools.partial(forward_kernel, plan), 'forward', [f32(2, cells, w...  2.05 us
    ppermute x1, starting transfers between devices, per_device(): lax.ppermute(edge_frame, ('tm', 'mod'), ends + [(b, a) for a, b in ends])  1.79 us
    pallas_call x1, Pallas kernels, per_device(): call(functools.partial(prep_kernel, plan), 'prepare', [f32(2, cells, LANE...  1.55 us
    ppermute x3, waiting for transfers between devices, per_device(): lax.ppermute(total, 'tm', [(i, (i + k) % steps) for i in range(steps)])  1.31 us
  transfers between devices with their start and end apart: 11, of which 4 were waited for; matrix products, arithmetic and copies ran while one was open for 0% of the time, Pallas kernels for 19%

profile of v8, /device:TPU:0, one launch (start us, length us, event | category | flops | bytes accessed | tf_op | source)
XLA Modules:
  0.0 24.8 jit_solution(5558984331833148027)
XLA Ops:
  0.6 0.0 copy-start
  0.6 0.0 copy-start.1
  1.4 0.2 copy-done
  1.6 0.1 copy-done.1
  1.6 0.2 pack.1
  1.8 0.5 %collective-permute-start = (f32[392,128]{1,0:T(8,128)S(1)}, f32[392,128]{1,0:T(8,128)S(1)}, u32[]{:S(2)}, u32[]{:S(2)}) collective-permute-start(f32[392,128]{1,0:T(8,128)S(1)} %get-tuple-element.30), channel_id=1, source_target_pairs={{0,1},{1,0},{2,3},{3,2},{4,5},{5,4},{6,7},{7,6},{8,9},{9,8},{10,11... | collective-permute-start | bytes 602120 | tf_op jit(solution)/shard_map/ppermute | solution.py:539
  2.3 2.6 %collective-permute-start.1 = (f32[136,128]{1,0:T(8,128)S(1)}, f32[136,128]{1,0:T(8,128)S(1)}, u32[]{:S(2)}, u32[]{:S(2)}) collective-permute-start(f32[136,128]{1,0:T(8,128)S(1)} %get-tuple-element.31), channel_id=1, source_target_pairs={{0,2},{1,3},{2,0},{3,1},{4,6},{5,7},{6,4},{7,5},{8,10},{9,11},{10,... | collective-permute-start | bytes 208904 | tf_op jit(solution)/shard_map/ppermute | solution.py:539
  4.9 0.1 collective-permute-start.2
  5.0 1.5 %prepare.1 = (f32[2,256,128]{2,1,0:T(8,128)S(1)}, f32[2,2,256,128]{3,2,1,0:T(8,128)S(1)}, f32[4,256,128]{2,1,0:T(8,128)S(1)}, f32[4,8,128]{2,1,0:T(8,128)S(1)}, ...) custom-call(f32[136,128]{1,0:T(8,128)S(1)} %get-tuple-element.29.see, ...), custom_call_target="tpu_custom_call" | custom-call | flops 1650000000 | bytes 5400000 | tf_op jit(solution)/shard_map/prepare/pallas_call | solution.py:592
  6.5 0.0 collective-permute-done.refs_1_.piece_ref.refs_0_
  6.6 1.8 %collective-permute-start.3 = (f32[256,128]{1,0:T(8,128)S(1)}, f32[256,128]{1,0:T(8,128)S(1)}, u32[]{:S(2)}, u32[]{:S(2)}) collective-permute-start(f32[256,128]{1,0:T(8,128)S(1)} %get-tuple-element.45), channel_id=1, source_target_pairs={{1,4},{3,6},{5,8},{7,10},{9,12},{11,14},{2,0},{15,13},{4,1},{6,3},... | collective-permute-start | bytes 393224 | tf_op jit(solution)/shard_map/ppermute | solution.py:620
  8.4 0.0 collective-permute-done.1.refs_2_.refs_1_
  8.4 0.7 %collective-permute-done.2.refs_3_.refs_2_ = f32[136,128]{1,0:T(8,128)S(1)} collective-permute-done((f32[136,128]{1,0:T(8,128)S(1)}, f32[136,128]{1,0:T(8,128)S(1)}, u32[]{:S(2)}, u32[]{:S(2)}) %collective-permute-start.2) | collective-permute-done | bytes 69664 | tf_op jit(solution)/shard_map/ppermute | solution.py:539
  9.0 2.1 %forward.1 = (f32[2,256,256]{2,1,0:T(8,128)S(1)}, f32[2,256,256]{2,1,0:T(8,128)S(1)}, f32[2,256,1024]{2,1,0:T(8,128)S(1)}, f32[3,2,256,128]{3,2,1,0:T(8,128)S(1)}, f32[8,128]{1,0:T(8,128)S(1)}) custom-call(f32[136,128]{1,0:T(8,128)S(1)} %get-tuple-element.29.seed_ref.refs_0_, f32[392,128]{1,0:T(8,128)S(1)} %collective-permute-done.refs_1_.piece_ref.refs_0_, ...), custom_call_target="tpu_custom_call" | custom-call | flops 3080000000 | bytes 10080000 | tf_op jit(solution)/shard_map/forward/pallas_call | solution.py:622
  11.1 0.5 %collective-permute-done.3.refs_4_.refs_6_ = f32[256,128]{1,0:T(8,128)S(1)} collective-permute-done((f32[256,128]{1,0:T(8,128)S(1)}, f32[256,128]{1,0:T(8,128)S(1)}, u32[]{:S(2)}, u32[]{:S(2)}) %collective-permute-start.3) | collective-permute-done | bytes 131104 | tf_op jit(solution)/shard_map/ppermute | solution.py:620
  11.6 0.2 prior.1
  11.9 1.3 %collective-permute-start.5 = (f32[8,128]{1,0:T(8,128)S(1)}, f32[8,128]{1,0:T(8,128)S(1)}, u32[]{:S(2)}, u32[]{:S(2)}) collective-permute-start(f32[8,128]{1,0:T(8,128)S(1)} %get-tuple-element.54.refs_3_), channel_id=1, source_target_pairs={{0,4},{4,8},{8,12},{12,0},{1,5},{5,9},{9,13},{13,1},{2,6},{6,10},{... | collective-permute-start | bytes 12296 | tf_op jit(solution)/shard_map/ppermute | solution.py:642
  13.1 2.6 %collective-permute-start.6 = (f32[8,128]{1,0:T(8,128)S(1)}, f32[8,128]{1,0:T(8,128)S(1)}, u32[]{:S(2)}, u32[]{:S(2)}) collective-permute-start(f32[8,128]{1,0:T(8,128)S(1)} %get-tuple-element.54.refs_3_), channel_id=1, source_target_pairs={{0,8},{4,12},{8,0},{12,4},{1,9},{5,13},{9,1},{13,5},{2,10},{6,14},... | collective-permute-start | bytes 12296 | tf_op jit(solution)/shard_map/ppermute | solution.py:642
  15.7 1.3 %collective-permute-start.7 = (f32[8,128]{1,0:T(8,128)S(1)}, f32[8,128]{1,0:T(8,128)S(1)}, u32[]{:S(2)}, u32[]{:S(2)}) collective-permute-start(f32[8,128]{1,0:T(8,128)S(1)} %get-tuple-element.54.refs_3_), channel_id=1, source_target_pairs={{0,12},{4,0},{8,4},{12,8},{1,13},{5,1},{9,5},{13,9},{2,14},{6,2},{... | collective-permute-start | bytes 12296 | tf_op jit(solution)/shard_map/ppermute | solution.py:642
  17.1 0.8 %backward.1 = (f32[72,128]{1,0:T(8,128)S(1)}, f32[72,128]{1,0:T(8,128)S(1)}, f32[272,128]{1,0:T(8,128)S(1)}, f32[1,256,128]{2,1,0:T(8,128)S(1)}) custom-call(f32[2,256,256]{2,1,0:T(8,128)S(1)} %get-tuple-element.37.refs_0_, f32[2,256,256]{2,1,0:T(8,128)S(1)} %get-tuple-element.38.refs_1_, f32[2,256,1024]{2,1,0:T(8,128)S(1)} %get-tuple-element.39.refs_2_, ...), custom_call_target="tpu_custom_call" | custom-call | flops 880000000 | bytes 2880000 | tf_op jit(solution)/shard_map/backward/pallas_call | solution.py:646
  17.9 0.1 collective-permute-start.4
  18.0 0.0 collective-permute-done.5.refs_0_
  18.0 0.0 collective-permute-done.6.refs_1_
  18.0 1.3 %collective-permute-done.7.refs_2_ = f32[8,128]{1,0:T(8,128)S(1)} collective-permute-done((f32[8,128]{1,0:T(8,128)S(1)}, f32[8,128]{1,0:T(8,128)S(1)}, u32[]{:S(2)}, u32[]{:S(2)}) %collective-permute-start.7) | collective-permute-done | bytes 4128 | tf_op jit(solution)/shard_map/ppermute | solution.py:642
  19.4 0.0 collective-permute-done.4.near_ref.refs_1_
  19.4 1.6 %collective-permute-start.8 = (f32[144,128]{1,0:T(8,128)S(1)}, f32[144,128]{1,0:T(8,128)S(1)}, u32[]{:S(2)}, u32[]{:S(2)}) collective-permute-start(f32[144,128]{1,0:T(8,128)S(1)} %seal.1), channel_id=1, source_target_pairs={{0,2},{1,3},{2,0},{3,1},{4,6},{5,7},{6,4},{7,5},{8,10},{9,11},{10,... | collective-permute-start | bytes 221192 | tf_op jit(solution)/shard_map/ppermute | solution.py:660
  20.9 0.0 collective-permute-start.10
  20.9 0.6 %collective-permute-start.9 = (f32[8,128]{1,0:T(8,128)S(1)}, f32[8,128]{1,0:T(8,128)S(1)}, u32[]{:S(2)}, u32[]{:S(2)}) collective-permute-start(f32[8,128]{1,0:T(8,128)S(1)} %sum.1.total_ref.refs_2_), channel_id=1, source_target_pairs={{0,1},{1,0},{2,3},{3,2},{4,5},{5,4},{6,7},{7,6},{8,9},{9,8},{10,11... | collective-permute-start | bytes 12296 | tf_op jit(solution)/shard_map/ppermute | solution.py:660
  21.6 0.1 begin.1.refs_0_
  21.7 2.3 %collective-permute-done.10.refs_4_ = f32[8,128]{1,0:T(8,128)S(1)} collective-permute-done((f32[8,128]{1,0:T(8,128)S(1)}, f32[8,128]{1,0:T(8,128)S(1)}, u32[]{:S(2)}, u32[]{:S(2)}) %collective-permute-start.10) | collective-permute-done | bytes 4128 | tf_op jit(solution)/shard_map/ppermute | solution.py:660
  24.0 0.0 collective-permute-done.9.refs_3_
  24.0 0.0 collective-permute-done.8.refs_1_
  24.0 0.8 %join.1 = (f32[2,128,128]{2,1,0:T(8,128)}, f32[1]{0:T(128)}) custom-call(f32[2,128,128]{2,1,0:T(8,128)S(1)} %begin.1.refs_0_, f32[144,128]{1,0:T(8,128)S(1)} %collective-permute-done.8.refs_1_, f32[8,128]{1,0:T(8,128)S(1)} %sum.1.total_ref.refs_2_, f32[8,128]{1,0:T(8,128)S(1)} %collective-permute-done.9.refs_3_, ...), custom_call_target="tpu_custom_call" | custom-call | flops 880000000 | bytes 2880000 | tf_op jit(solution)/shard_map/join/pallas_call | solution.py:676
  (5 shorter events, 0.1 us)
Async XLA Ops:
  0.6 0.9 %copy-start = (f32[2,128,128]{2,1,0:T(8,128)S(1)}, f32[2,128,128]{2,1,0:T(8,128)}, u32[]{:S(2)}) copy-start(f32[2,128,128]{2,1,0:T(8,128)} %phase_ref.1) | copy-start | bytes 393220
  0.6 1.0 %copy-start.1 = (f32[2,128,128]{2,1,0:T(8,128)S(1)}, f32[2,128,128]{2,1,0:T(8,128)}, u32[]{:S(2)}) copy-start(f32[2,128,128]{2,1,0:T(8,128)} %direction_ref.1) | copy-start | bytes 393220
  1.8 4.7 %collective-permute-start = (f32[392,128]{1,0:T(8,128)S(1)}, f32[392,128]{1,0:T(8,128)S(1)}, u32[]{:S(2)}, u32[]{:S(2)}) collective-permute-start(f32[392,128]{1,0:T(8,128)S(1)} %get-tuple-element.30), channel_id=1, source_target_pairs={{0,1},{1,0},{2,3},{3,2},{4,5},{5,4},{6,7},{7,6},{8,9},{9,8},{10,11... | collective-permute-start | bytes 602120 | tf_op jit(solution)/shard_map/ppermute | solution.py:539
  2.3 6.0 %collective-permute-start.1 = (f32[136,128]{1,0:T(8,128)S(1)}, f32[136,128]{1,0:T(8,128)S(1)}, u32[]{:S(2)}, u32[]{:S(2)}) collective-permute-start(f32[136,128]{1,0:T(8,128)S(1)} %get-tuple-element.31), channel_id=1, source_target_pairs={{0,2},{1,3},{2,0},{3,1},{4,6},{5,7},{6,4},{7,5},{8,10},{9,11},{10,... | collective-permute-start | bytes 208904 | tf_op jit(solution)/shard_map/ppermute | solution.py:539
  4.9 4.1 %collective-permute-start.2 = (f32[136,128]{1,0:T(8,128)S(1)}, f32[136,128]{1,0:T(8,128)S(1)}, u32[]{:S(2)}, u32[]{:S(2)}) collective-permute-start(f32[136,128]{1,0:T(8,128)S(1)} %get-tuple-element.32), channel_id=1, source_target_pairs={{0,3},{1,2},{2,1},{3,0},{4,7},{5,6},{6,5},{7,4},{8,11},{9,10},{10,... | collective-permute-start | bytes 208904 | tf_op jit(solution)/shard_map/ppermute | solution.py:539
  6.6 5.0 %collective-permute-start.3 = (f32[256,128]{1,0:T(8,128)S(1)}, f32[256,128]{1,0:T(8,128)S(1)}, u32[]{:S(2)}, u32[]{:S(2)}) collective-permute-start(f32[256,128]{1,0:T(8,128)S(1)} %get-tuple-element.45), channel_id=1, source_target_pairs={{1,4},{3,6},{5,8},{7,10},{9,12},{11,14},{2,0},{15,13},{4,1},{6,3},... | collective-permute-start | bytes 393224 | tf_op jit(solution)/shard_map/ppermute | solution.py:620
  11.9 6.2 %collective-permute-start.5 = (f32[8,128]{1,0:T(8,128)S(1)}, f32[8,128]{1,0:T(8,128)S(1)}, u32[]{:S(2)}, u32[]{:S(2)}) collective-permute-start(f32[8,128]{1,0:T(8,128)S(1)} %get-tuple-element.54.refs_3_), channel_id=1, source_target_pairs={{0,4},{4,8},{8,12},{12,0},{1,5},{5,9},{9,13},{13,1},{2,6},{6,10},{... | collective-permute-start | bytes 12296 | tf_op jit(solution)/shard_map/ppermute | solution.py:642
  13.1 4.9 %collective-permute-start.6 = (f32[8,128]{1,0:T(8,128)S(1)}, f32[8,128]{1,0:T(8,128)S(1)}, u32[]{:S(2)}, u32[]{:S(2)}) collective-permute-start(f32[8,128]{1,0:T(8,128)S(1)} %get-tuple-element.54.refs_3_), channel_id=1, source_target_pairs={{0,8},{4,12},{8,0},{12,4},{1,9},{5,13},{9,1},{13,5},{2,10},{6,14},... | collective-permute-start | bytes 12296 | tf_op jit(solution)/shard_map/ppermute | solution.py:642
  15.7 3.6 %collective-permute-start.7 = (f32[8,128]{1,0:T(8,128)S(1)}, f32[8,128]{1,0:T(8,128)S(1)}, u32[]{:S(2)}, u32[]{:S(2)}) collective-permute-start(f32[8,128]{1,0:T(8,128)S(1)} %get-tuple-element.54.refs_3_), channel_id=1, source_target_pairs={{0,12},{4,0},{8,4},{12,8},{1,13},{5,1},{9,5},{13,9},{2,14},{6,2},{... | collective-permute-start | bytes 12296 | tf_op jit(solution)/shard_map/ppermute | solution.py:642
  17.9 1.4 %collective-permute-start.4 = (f32[272,128]{1,0:T(8,128)S(1)}, f32[272,128]{1,0:T(8,128)S(1)}, u32[]{:S(2)}, u32[]{:S(2)}) collective-permute-start(f32[272,128]{1,0:T(8,128)S(1)} %get-tuple-element.52), channel_id=1, source_target_pairs={{0,1},{1,0},{2,3},{3,2},{4,5},{5,4},{6,7},{7,6},{8,9},{9,8},{10,11... | collective-permute-start | bytes 417800 | tf_op jit(solution)/shard_map/ppermute | solution.py:660
  19.4 4.6 %collective-permute-start.8 = (f32[144,128]{1,0:T(8,128)S(1)}, f32[144,128]{1,0:T(8,128)S(1)}, u32[]{:S(2)}, u32[]{:S(2)}) collective-permute-start(f32[144,128]{1,0:T(8,128)S(1)} %seal.1), channel_id=1, source_target_pairs={{0,2},{1,3},{2,0},{3,1},{4,6},{5,7},{6,4},{7,5},{8,10},{9,11},{10,... | collective-permute-start | bytes 221192 | tf_op jit(solution)/shard_map/ppermute | solution.py:660
  20.9 3.0 %collective-permute-start.10 = (f32[8,128]{1,0:T(8,128)S(1)}, f32[8,128]{1,0:T(8,128)S(1)}, u32[]{:S(2)}, u32[]{:S(2)}) collective-permute-start(f32[8,128]{1,0:T(8,128)S(1)} %sum.1.total_ref.refs_2_), channel_id=1, source_target_pairs={{0,3},{1,2},{2,1},{3,0},{4,7},{5,6},{6,5},{7,4},{8,11},{9,10},{10,... | collective-permute-start | bytes 12296 | tf_op jit(solution)/shard_map/ppermute | solution.py:660
  20.9 3.0 %collective-permute-start.9 = (f32[8,128]{1,0:T(8,128)S(1)}, f32[8,128]{1,0:T(8,128)S(1)}, u32[]{:S(2)}, u32[]{:S(2)}) collective-permute-start(f32[8,128]{1,0:T(8,128)S(1)} %sum.1.total_ref.refs_2_), channel_id=1, source_target_pairs={{0,1},{1,0},{2,3},{3,2},{4,5},{5,4},{6,7},{7,6},{8,9},{9,8},{10,11... | collective-permute-start | bytes 12296 | tf_op jit(solution)/shard_map/ppermute | solution.py:660

commit v9 on v8

--- a/solution.py
+++ b/solution.py
@@ -108,9 +108,15 @@
         ahead = (LANES + width - group * width) % LANES
         for parity in range(2):
             own = pl.ds(parity, half, stride=2)
-            one = pltpu.roll(phase_ref[frame, own, :], back, 1)
-            two = pltpu.roll(direction_ref[frame, own, :], ahead, 1)
-            out[parity * half : (parity + 1) * half, :] = jnp.where(lane < width, one, two)
+            one, two = phase_ref[frame, own, :], direction_ref[frame, own, :]
+            if plan.copies == 2:
+                kept = jnp.where(group == 0, one, two)
+                moved = pltpu.roll(jnp.where(group == 0, two, one), width, 1)
+                low = (lane < width) == (group == 0)
+                mixed = jnp.where(low, kept, moved)
+            else:
+                mixed = jnp.where(lane < width, pltpu.roll(one, back, 1), pltpu.roll(two, ahead, 1))
+            out[parity * half : (parity + 1) * half, :] = mixed
         rows = []
         for f in range(frames):
             rows += [direction_ref[f, 0:1, :], direction_ref[f, shard - 1 : shard, :]]

time: 24.9 us -> 24.9 us (level)
  no operation moved by 1% of the time
where the time goes in v9:
time: 24.9 us; the launch traced here: 24.7 us
  starting transfers between devices  12.4 us (50%)
  Pallas kernels  5.76 us (23%)
  waiting for transfers between devices  4.8 us (19%)
  between operations  1.45 us (6%)
  local copies, waits for them, and re-layouts  0.26 us (1%)
    ppermute x3, starting transfers between devices, per_device(): lax.ppermute(total, 'tm', [(i, (i + k) % steps) for i in range(steps)])  5.23 us
    ppermute x3, starting transfers between devices, exchange(): lax.ppermute(arrays[k], axis, [(i, i ^ k) for i in range(count)])  3.15 us
    ppermute x4, waiting for transfers between devices, swap(): return lax.ppermute(array, 'mod', [(i, i ^ k) for i in range(mods)])  2.3 us
    ppermute x4, starting transfers between devices, swap(): return lax.ppermute(array, 'mod', [(i, i ^ k) for i in range(mods)])  2.28 us
    pallas_call x1, Pallas kernels, per_device(): call(functools.partial(forward_kernel, plan), 'forward', [f32(2, cells, w...  2.05 us
    ppermute x1, starting transfers between devices, per_device(): lax.ppermute(edge_frame, ('tm', 'mod'), ends + [(b, a) for a, b in ends])  1.79 us
    pallas_call x1, Pallas kernels, per_device(): call(functools.partial(prep_kernel, plan), 'prepare', [f32(2, cells, LANE...  1.55 us
    ppermute x3, waiting for transfers between devices, per_device(): lax.ppermute(total, 'tm', [(i, (i + k) % steps) for i in range(steps)])  1.31 us
  transfers between devices with their start and end apart: 11, of which 4 were waited for; matrix products, arithmetic and copies ran while one was open for 0% of the time, Pallas kernels for 19%

profile of v9, /device:TPU:0, one launch (start us, length us, event | category | flops | bytes accessed | tf_op | source)
XLA Modules:
  0.0 24.7 jit_solution(9438283455055949889)
XLA Ops:
  0.6 0.0 copy-start
  0.6 0.0 copy-start.1
  1.4 0.2 copy-done
  1.6 0.1 copy-done.1
  1.6 0.1 pack.1
  1.8 0.5 %collective-permute-start = (f32[392,128]{1,0:T(8,128)S(1)}, f32[392,128]{1,0:T(8,128)S(1)}, u32[]{:S(2)}, u32[]{:S(2)}) collective-permute-start(f32[392,128]{1,0:T(8,128)S(1)} %get-tuple-element.30), channel_id=1, source_target_pairs={{0,1},{1,0},{2,3},{3,2},{4,5},{5,4},{6,7},{7,6},{8,9},{9,8},{10,11... | collective-permute-start | bytes 602120 | tf_op jit(solution)/shard_map/ppermute | solution.py:545
  2.3 2.6 %collective-permute-start.1 = (f32[136,128]{1,0:T(8,128)S(1)}, f32[136,128]{1,0:T(8,128)S(1)}, u32[]{:S(2)}, u32[]{:S(2)}) collective-permute-start(f32[136,128]{1,0:T(8,128)S(1)} %get-tuple-element.31), channel_id=1, source_target_pairs={{0,2},{1,3},{2,0},{3,1},{4,6},{5,7},{6,4},{7,5},{8,10},{9,11},{10,... | collective-permute-start | bytes 208904 | tf_op jit(solution)/shard_map/ppermute | solution.py:545
  4.9 0.1 collective-permute-start.2
  4.9 1.5 %prepare.1 = (f32[2,256,128]{2,1,0:T(8,128)S(1)}, f32[2,2,256,128]{3,2,1,0:T(8,128)S(1)}, f32[4,256,128]{2,1,0:T(8,128)S(1)}, f32[4,8,128]{2,1,0:T(8,128)S(1)}, ...) custom-call(f32[136,128]{1,0:T(8,128)S(1)} %get-tuple-element.29.see, ...), custom_call_target="tpu_custom_call" | custom-call | flops 1650000000 | bytes 5400000 | tf_op jit(solution)/shard_map/prepare/pallas_call | solution.py:598
  6.5 0.0 collective-permute-done.refs_1_.piece_ref.refs_0_
  6.5 1.8 %collective-permute-start.3 = (f32[256,128]{1,0:T(8,128)S(1)}, f32[256,128]{1,0:T(8,128)S(1)}, u32[]{:S(2)}, u32[]{:S(2)}) collective-permute-start(f32[256,128]{1,0:T(8,128)S(1)} %get-tuple-element.45), channel_id=1, source_target_pairs={{1,4},{3,6},{5,8},{7,10},{9,12},{11,14},{2,0},{15,13},{4,1},{6,3},... | collective-permute-start | bytes 393224 | tf_op jit(solution)/shard_map/ppermute | solution.py:626
  8.3 0.0 collective-permute-done.1.refs_2_.refs_1_
  8.3 0.7 %collective-permute-done.2.refs_3_.refs_2_ = f32[136,128]{1,0:T(8,128)S(1)} collective-permute-done((f32[136,128]{1,0:T(8,128)S(1)}, f32[136,128]{1,0:T(8,128)S(1)}, u32[]{:S(2)}, u32[]{:S(2)}) %collective-permute-start.2) | collective-permute-done | bytes 69664 | tf_op jit(solution)/shard_map/ppermute | solution.py:545
  9.0 2.1 %forward.1 = (f32[2,256,256]{2,1,0:T(8,128)S(1)}, f32[2,256,256]{2,1,0:T(8,128)S(1)}, f32[2,256,1024]{2,1,0:T(8,128)S(1)}, f32[3,2,256,128]{3,2,1,0:T(8,128)S(1)}, f32[8,128]{1,0:T(8,128)S(1)}) custom-call(f32[136,128]{1,0:T(8,128)S(1)} %get-tuple-element.29.seed_ref.refs_0_, f32[392,128]{1,0:T(8,128)S(1)} %collective-permute-done.refs_1_.piece_ref.refs_0_, ...), custom_call_target="tpu_custom_call" | custom-call | flops 3080000000 | bytes 10080000 | tf_op jit(solution)/shard_map/forward/pallas_call | solution.py:628
  11.0 0.5 %collective-permute-done.3.refs_4_.refs_6_ = f32[256,128]{1,0:T(8,128)S(1)} collective-permute-done((f32[256,128]{1,0:T(8,128)S(1)}, f32[256,128]{1,0:T(8,128)S(1)}, u32[]{:S(2)}, u32[]{:S(2)}) %collective-permute-start.3) | collective-permute-done | bytes 131104 | tf_op jit(solution)/shard_map/ppermute | solution.py:626
  11.6 0.2 prior.1
  11.8 1.3 %collective-permute-start.5 = (f32[8,128]{1,0:T(8,128)S(1)}, f32[8,128]{1,0:T(8,128)S(1)}, u32[]{:S(2)}, u32[]{:S(2)}) collective-permute-start(f32[8,128]{1,0:T(8,128)S(1)} %get-tuple-element.54.refs_3_), channel_id=1, source_target_pairs={{0,4},{4,8},{8,12},{12,0},{1,5},{5,9},{9,13},{13,1},{2,6},{6,10},{... | collective-permute-start | bytes 12296 | tf_op jit(solution)/shard_map/ppermute | solution.py:648
  13.1 2.6 %collective-permute-start.6 = (f32[8,128]{1,0:T(8,128)S(1)}, f32[8,128]{1,0:T(8,128)S(1)}, u32[]{:S(2)}, u32[]{:S(2)}) collective-permute-start(f32[8,128]{1,0:T(8,128)S(1)} %get-tuple-element.54.refs_3_), channel_id=1, source_target_pairs={{0,8},{4,12},{8,0},{12,4},{1,9},{5,13},{9,1},{13,5},{2,10},{6,14},... | collective-permute-start | bytes 12296 | tf_op jit(solution)/shard_map/ppermute | solution.py:648
  15.7 1.3 %collective-permute-start.7 = (f32[8,128]{1,0:T(8,128)S(1)}, f32[8,128]{1,0:T(8,128)S(1)}, u32[]{:S(2)}, u32[]{:S(2)}) collective-permute-start(f32[8,128]{1,0:T(8,128)S(1)} %get-tuple-element.54.refs_3_), channel_id=1, source_target_pairs={{0,12},{4,0},{8,4},{12,8},{1,13},{5,1},{9,5},{13,9},{2,14},{6,2},{... | collective-permute-start | bytes 12296 | tf_op jit(solution)/shard_map/ppermute | solution.py:648
  17.0 0.8 %backward.1 = (f32[72,128]{1,0:T(8,128)S(1)}, f32[72,128]{1,0:T(8,128)S(1)}, f32[272,128]{1,0:T(8,128)S(1)}, f32[1,256,128]{2,1,0:T(8,128)S(1)}) custom-call(f32[2,256,256]{2,1,0:T(8,128)S(1)} %get-tuple-element.37.refs_0_, f32[2,256,256]{2,1,0:T(8,128)S(1)} %get-tuple-element.38.refs_1_, f32[2,256,1024]{2,1,0:T(8,128)S(1)} %get-tuple-element.39.refs_2_, ...), custom_call_target="tpu_custom_call" | custom-call | flops 880000000 | bytes 2880000 | tf_op jit(solution)/shard_map/backward/pallas_call | solution.py:652
  17.9 0.1 collective-permute-start.4
  18.0 0.0 collective-permute-done.5.refs_0_
  18.0 0.0 collective-permute-done.6.refs_1_
  18.0 1.3 %collective-permute-done.7.refs_2_ = f32[8,128]{1,0:T(8,128)S(1)} collective-permute-done((f32[8,128]{1,0:T(8,128)S(1)}, f32[8,128]{1,0:T(8,128)S(1)}, u32[]{:S(2)}, u32[]{:S(2)}) %collective-permute-start.7) | collective-permute-done | bytes 4128 | tf_op jit(solution)/shard_map/ppermute | solution.py:648
  19.3 0.0 collective-permute-done.4.near_ref.refs_1_
  19.3 1.6 %collective-permute-start.8 = (f32[144,128]{1,0:T(8,128)S(1)}, f32[144,128]{1,0:T(8,128)S(1)}, u32[]{:S(2)}, u32[]{:S(2)}) collective-permute-start(f32[144,128]{1,0:T(8,128)S(1)} %seal.1), channel_id=1, source_target_pairs={{0,2},{1,3},{2,0},{3,1},{4,6},{5,7},{6,4},{7,5},{8,10},{9,11},{10,... | collective-permute-start | bytes 221192 | tf_op jit(solution)/shard_map/ppermute | solution.py:666
  20.9 0.0 collective-permute-start.10
  20.9 0.6 %collective-permute-start.9 = (f32[8,128]{1,0:T(8,128)S(1)}, f32[8,128]{1,0:T(8,128)S(1)}, u32[]{:S(2)}, u32[]{:S(2)}) collective-permute-start(f32[8,128]{1,0:T(8,128)S(1)} %sum.1.total_ref.refs_2_), channel_id=1, source_target_pairs={{0,1},{1,0},{2,3},{3,2},{4,5},{5,4},{6,7},{7,6},{8,9},{9,8},{10,11... | collective-permute-start | bytes 12296 | tf_op jit(solution)/shard_map/ppermute | solution.py:666
  21.5 0.1 begin.1.refs_0_
  21.6 2.3 %collective-permute-done.10.refs_4_ = f32[8,128]{1,0:T(8,128)S(1)} collective-permute-done((f32[8,128]{1,0:T(8,128)S(1)}, f32[8,128]{1,0:T(8,128)S(1)}, u32[]{:S(2)}, u32[]{:S(2)}) %collective-permute-start.10) | collective-permute-done | bytes 4128 | tf_op jit(solution)/shard_map/ppermute | solution.py:666
  23.9 0.0 collective-permute-done.9.refs_3_
  23.9 0.0 collective-permute-done.8.refs_1_
  23.9 0.8 %join.1 = (f32[2,128,128]{2,1,0:T(8,128)}, f32[1]{0:T(128)}) custom-call(f32[2,128,128]{2,1,0:T(8,128)S(1)} %begin.1.refs_0_, f32[144,128]{1,0:T(8,128)S(1)} %collective-permute-done.8.refs_1_, f32[8,128]{1,0:T(8,128)S(1)} %sum.1.total_ref.refs_2_, f32[8,128]{1,0:T(8,128)S(1)} %collective-permute-done.9.refs_3_, ...), custom_call_target="tpu_custom_call" | custom-call | flops 880000000 | bytes 2880000 | tf_op jit(solution)/shard_map/join/pallas_call | solution.py:682
  (5 shorter events, 0.1 us)
Async XLA Ops:
  0.6 0.9 %copy-start = (f32[2,128,128]{2,1,0:T(8,128)S(1)}, f32[2,128,128]{2,1,0:T(8,128)}, u32[]{:S(2)}) copy-start(f32[2,128,128]{2,1,0:T(8,128)} %phase_ref.1) | copy-start | bytes 393220
  0.6 1.0 %copy-start.1 = (f32[2,128,128]{2,1,0:T(8,128)S(1)}, f32[2,128,128]{2,1,0:T(8,128)}, u32[]{:S(2)}) copy-start(f32[2,128,128]{2,1,0:T(8,128)} %direction_ref.1) | copy-start | bytes 393220
  1.8 4.7 %collective-permute-start = (f32[392,128]{1,0:T(8,128)S(1)}, f32[392,128]{1,0:T(8,128)S(1)}, u32[]{:S(2)}, u32[]{:S(2)}) collective-permute-start(f32[392,128]{1,0:T(8,128)S(1)} %get-tuple-element.30), channel_id=1, source_target_pairs={{0,1},{1,0},{2,3},{3,2},{4,5},{5,4},{6,7},{7,6},{8,9},{9,8},{10,11... | collective-permute-start | bytes 602120 | tf_op jit(solution)/shard_map/ppermute | solution.py:545
  2.3 6.0 %collective-permute-start.1 = (f32[136,128]{1,0:T(8,128)S(1)}, f32[136,128]{1,0:T(8,128)S(1)}, u32[]{:S(2)}, u32[]{:S(2)}) collective-permute-start(f32[136,128]{1,0:T(8,128)S(1)} %get-tuple-element.31), channel_id=1, source_target_pairs={{0,2},{1,3},{2,0},{3,1},{4,6},{5,7},{6,4},{7,5},{8,10},{9,11},{10,... | collective-permute-start | bytes 208904 | tf_op jit(solution)/shard_map/ppermute | solution.py:545
  4.9 4.1 %collective-permute-start.2 = (f32[136,128]{1,0:T(8,128)S(1)}, f32[136,128]{1,0:T(8,128)S(1)}, u32[]{:S(2)}, u32[]{:S(2)}) collective-permute-start(f32[136,128]{1,0:T(8,128)S(1)} %get-tuple-element.32), channel_id=1, source_target_pairs={{0,3},{1,2},{2,1},{3,0},{4,7},{5,6},{6,5},{7,4},{8,11},{9,10},{10,... | collective-permute-start | bytes 208904 | tf_op jit(solution)/shard_map/ppermute | solution.py:545
  6.5 5.0 %collective-permute-start.3 = (f32[256,128]{1,0:T(8,128)S(1)}, f32[256,128]{1,0:T(8,128)S(1)}, u32[]{:S(2)}, u32[]{:S(2)}) collective-permute-start(f32[256,128]{1,0:T(8,128)S(1)} %get-tuple-element.45), channel_id=1, source_target_pairs={{1,4},{3,6},{5,8},{7,10},{9,12},{11,14},{2,0},{15,13},{4,1},{6,3},... | collective-permute-start | bytes 393224 | tf_op jit(solution)/shard_map/ppermute | solution.py:626
  11.8 6.2 %collective-permute-start.5 = (f32[8,128]{1,0:T(8,128)S(1)}, f32[8,128]{1,0:T(8,128)S(1)}, u32[]{:S(2)}, u32[]{:S(2)}) collective-permute-start(f32[8,128]{1,0:T(8,128)S(1)} %get-tuple-element.54.refs_3_), channel_id=1, source_target_pairs={{0,4},{4,8},{8,12},{12,0},{1,5},{5,9},{9,13},{13,1},{2,6},{6,10},{... | collective-permute-start | bytes 12296 | tf_op jit(solution)/shard_map/ppermute | solution.py:648
  13.1 4.9 %collective-permute-start.6 = (f32[8,128]{1,0:T(8,128)S(1)}, f32[8,128]{1,0:T(8,128)S(1)}, u32[]{:S(2)}, u32[]{:S(2)}) collective-permute-start(f32[8,128]{1,0:T(8,128)S(1)} %get-tuple-element.54.refs_3_), channel_id=1, source_target_pairs={{0,8},{4,12},{8,0},{12,4},{1,9},{5,13},{9,1},{13,5},{2,10},{6,14},... | collective-permute-start | bytes 12296 | tf_op jit(solution)/shard_map/ppermute | solution.py:648
  15.7 3.6 %collective-permute-start.7 = (f32[8,128]{1,0:T(8,128)S(1)}, f32[8,128]{1,0:T(8,128)S(1)}, u32[]{:S(2)}, u32[]{:S(2)}) collective-permute-start(f32[8,128]{1,0:T(8,128)S(1)} %get-tuple-element.54.refs_3_), channel_id=1, source_target_pairs={{0,12},{4,0},{8,4},{12,8},{1,13},{5,1},{9,5},{13,9},{2,14},{6,2},{... | collective-permute-start | bytes 12296 | tf_op jit(solution)/shard_map/ppermute | solution.py:648
  17.9 1.4 %collective-permute-start.4 = (f32[272,128]{1,0:T(8,128)S(1)}, f32[272,128]{1,0:T(8,128)S(1)}, u32[]{:S(2)}, u32[]{:S(2)}) collective-permute-start(f32[272,128]{1,0:T(8,128)S(1)} %get-tuple-element.52), channel_id=1, source_target_pairs={{0,1},{1,0},{2,3},{3,2},{4,5},{5,4},{6,7},{7,6},{8,9},{9,8},{10,11... | collective-permute-start | bytes 417800 | tf_op jit(solution)/shard_map/ppermute | solution.py:666
  19.3 4.6 %collective-permute-start.8 = (f32[144,128]{1,0:T(8,128)S(1)}, f32[144,128]{1,0:T(8,128)S(1)}, u32[]{:S(2)}, u32[]{:S(2)}) collective-permute-start(f32[144,128]{1,0:T(8,128)S(1)} %seal.1), channel_id=1, source_target_pairs={{0,2},{1,3},{2,0},{3,1},{4,6},{5,7},{6,4},{7,5},{8,10},{9,11},{10,... | collective-permute-start | bytes 221192 | tf_op jit(solution)/shard_map/ppermute | solution.py:666
  20.9 3.0 %collective-permute-start.10 = (f32[8,128]{1,0:T(8,128)S(1)}, f32[8,128]{1,0:T(8,128)S(1)}, u32[]{:S(2)}, u32[]{:S(2)}) collective-permute-start(f32[8,128]{1,0:T(8,128)S(1)} %sum.1.total_ref.refs_2_), channel_id=1, source_target_pairs={{0,3},{1,2},{2,1},{3,0},{4,7},{5,6},{6,5},{7,4},{8,11},{9,10},{10,... | collective-permute-start | bytes 12296 | tf_op jit(solution)/shard_map/ppermute | solution.py:666
  20.9 3.0 %collective-permute-start.9 = (f32[8,128]{1,0:T(8,128)S(1)}, f32[8,128]{1,0:T(8,128)S(1)}, u32[]{:S(2)}, u32[]{:S(2)}) collective-permute-start(f32[8,128]{1,0:T(8,128)S(1)} %sum.1.total_ref.refs_2_), channel_id=1, source_target_pairs={{0,1},{1,0},{2,3},{3,2},{4,5},{5,4},{6,7},{7,6},{8,9},{9,8},{10,11... | collective-permute-start | bytes 12296 | tf_op jit(solution)/shard_map/ppermute | solution.py:666
